TPU v7x, 256 devices: a whole 4x4x8 slice. The times are simulated.
256 devices in a mesh: role: 2 (over x_lo), grp: 16 (over x_hi, z), tp: 8 (over y, core).
Axes of the slice: x: 4 (x_hi: 2, x_lo: 2; x = x_hi * 2 + x_lo), y: 4, z: 8, core: 2. Of those that a mesh axis runs over, the one named last changes fastest.
Arguments:
- prompt_states: bfloat16 [2, 16, 512, 5120], P('role', 'grp', 'tp'), may hold values from -6 to 6
- new_states: bfloat16 [2, 256, 2, 5120], P('role', 'grp'), may hold values from -6 to 6
- answer_cache: bfloat16 [2, 256, 128, 2048], P('role', 'grp', None, 'tp'), may hold values from -6 to 6
- attn_gain: float32 [5120], replicated, may hold values from 0.1 to 1.9
- w_query: bfloat16 [5120, 3072], P(None, 'tp')
- key_weight: bfloat16 [5120, 1024], P(None, 'tp')
- value_weight: bfloat16 [5120, 1024], P(None, 'tp'), may hold values from -0.078125 to 0.078125
- w_out: bfloat16 [3072, 5120], P('tp'), may hold values from -0.15625 to 0.15625
- prompt_of: int32 [2, 256], P('role'), may hold values from 0 to 15, as said below
- suffix_len: int32 [2, 256], P('role', 'grp'), may hold values from 1 to 128, as said below
Outputs:
- prefill_out: bfloat16 [2, 16, 512, 5120], P('role', 'grp', 'tp')
- decode_out: float32 [2, 256, 2, 5120], P('role', 'grp')
Inputs may be any that keep to these rules, and one draw needn't show every extreme that they name: `prompt_of`: in each half every prompt index 0 to 15 appears exactly 16 times. `suffix_len`: each aligned block of 16 samples holds one sample of length 128.
All inputs are finite; a program needn't handle non-finite values.
Results may differ from a plain program's by a relative error of at most 0.017.
Values may be sent and summed in bfloat16 or wider, within the bound.
No kernel may reach another device: no remote copies, remote signals or barrier semaphores. Data moves between devices by JAX's collectives and lax.ppermute only.
A program may use at most 128 MiB of HBM per device.

v0:
```python
import jax
import jax.numpy as jnp
from jax import lax
from jax.sharding import PartitionSpec as P

HEAD_WIDTH = 128


EPSILON = 1e-06
ROPE_BASE = 1000000.0


def from_partner(value, axis, apart):
    mask = 2**apart
    pairs = [(source, source ^ mask) for source in range(lax.axis_size(axis))]
    return lax.ppermute(value, axis, pairs)


def normalize(entries, scales):
    wide = entries.astype(jnp.float32)
    factor = lax.rsqrt(jnp.mean(wide * wide, axis=-1, keepdims=True) + EPSILON)
    return (wide * factor * scales).astype(jnp.bfloat16)


def apply_rotation(values, token_positions):
    half_width = values.shape[-1] // 2
    frequency = ROPE_BASE ** (-2.0 * jnp.arange(half_width, dtype=jnp.float32) / values.shape[-1])
    angles = token_positions[..., None] * frequency
    cosine = jnp.concatenate([jnp.cos(angles), jnp.cos(angles)], axis=-1)
    sine_part = jnp.concatenate([jnp.sin(angles), jnp.sin(angles)], axis=-1)
    turned = jnp.concatenate([-values[..., half_width:], values[..., :half_width]], axis=-1)
    return values * cosine + turned * sine_part


def shards(
    prompt_states,
    new_states,
    answer_cache,
    attn_gain,
    w_query,
    key_weight,
    value_weight,
    w_out,
    prompt_of,
    suffix_len,
):
    head_size = HEAD_WIDTH
    local_query = w_query.shape[1] // head_size
    local_keys = key_weight.shape[1] // head_size
    group_count = local_query // local_keys
    score_scale = head_size ** (-0.5)
    token_rows = prompt_states[0, 0]
    model_width = token_rows.shape[1]
    segment = lax.all_gather(token_rows, "tp", axis=0, tiled=True)
    row_count = segment.shape[0]
    normed_states = normalize(segment, attn_gain)
    token_positions = jnp.arange(row_count, dtype=jnp.int32).astype(jnp.float32)[:, None]
    query_rows = apply_rotation(
        jnp.dot(normed_states, w_query, preferred_element_type=jnp.float32).reshape(
            row_count, local_query, head_size
        ),
        token_positions,
    )
    key_entries = apply_rotation(
        jnp.dot(normed_states, key_weight, preferred_element_type=jnp.float32).reshape(
            row_count, local_keys, head_size
        ),
        token_positions,
    )
    value_entries = jnp.dot(
        normed_states, value_weight, preferred_element_type=jnp.float32
    ).reshape(row_count, local_keys, head_size)
    key_value = jnp.stack([key_entries, value_entries], axis=2).reshape(
        row_count, local_keys * 2 * head_size
    )
    joined = jnp.concatenate(
        [query_rows.reshape(row_count, local_query * head_size), key_value], axis=1
    )
    projected = joined.astype(jnp.bfloat16)
    length = projected.shape[0]
    query_rows = projected[:, : local_query * head_size].reshape(
        length, local_keys, group_count, head_size
    )
    prefix_rows = projected[:, local_query * head_size :]
    prefix_split = prefix_rows.reshape(length, local_keys, 2, head_size)
    handed = from_partner(prefix_rows, "role", 0)
    scores = (
        jnp.einsum(
            "qkgd,skd->kgqs", query_rows, prefix_split[:, :, 0], preferred_element_type=jnp.float32
        )
        * score_scale
    )
    causal = jnp.arange(length)[:, None] >= jnp.arange(length)[None, :]
    scores = jnp.where(causal, scores, -jnp.inf)
    row_peak = jnp.max(scores, axis=-1, keepdims=True)
    expo = jnp.exp(scores - row_peak)
    totals = jnp.sum(expo, axis=-1)
    mixed_heads = jnp.einsum(
        "kgqs,skd->qkgd",
        expo.astype(jnp.bfloat16),
        prefix_split[:, :, 1],
        preferred_element_type=jnp.float32,
    )
    mixed_heads = mixed_heads / jnp.transpose(totals, (2, 0, 1))[..., None]
    head_rows = mixed_heads.astype(jnp.bfloat16).reshape(length, local_query * head_size)
    summed = lax.psum_scatter(
        jnp.dot(head_rows, w_out, preferred_element_type=jnp.float32).astype(jnp.bfloat16),
        "tp",
        scatter_dimension=0,
        tiled=True,
    ).astype(jnp.float32)
    prefill_out = (token_rows.astype(jnp.float32) + summed).astype(jnp.bfloat16)[None, None]
    tokens = new_states[0]
    samples = tokens.shape[0]
    lengths = suffix_len[0]
    normed_fresh = normalize(tokens.reshape(samples * 2, model_width), attn_gain)
    token_positions = (
        (length + lengths[:, None] + jnp.arange(2, dtype=jnp.int32))
        .astype(jnp.float32)
        .reshape(samples * 2, 1)
    )
    fresh_query = apply_rotation(
        jnp.dot(normed_fresh, w_query, preferred_element_type=jnp.float32).reshape(
            samples * 2, local_query, head_size
        ),
        token_positions,
    )
    fresh_query = fresh_query.astype(jnp.bfloat16).reshape(
        samples, 2, local_keys, group_count, head_size
    )
    fresh_keys = apply_rotation(
        jnp.dot(normed_fresh, key_weight, preferred_element_type=jnp.float32).reshape(
            samples * 2, local_keys, head_size
        ),
        token_positions,
    )
    fresh_keys = fresh_keys.astype(jnp.bfloat16).reshape(samples, 2, local_keys, head_size)
    fresh_values = (
        jnp.dot(normed_fresh, value_weight, preferred_element_type=jnp.float32)
        .astype(jnp.bfloat16)
        .reshape(samples, 2, local_keys, head_size)
    )
    cached_rows = answer_cache[0].reshape(samples, -1, local_keys, 2, head_size)
    cache_width = cached_rows.shape[1]
    score_cache = (
        jnp.einsum(
            "stkgd,sjkd->stkgj",
            fresh_query,
            cached_rows[:, :, :, 0],
            preferred_element_type=jnp.float32,
        )
        * score_scale
    )
    valid = (jnp.arange(cache_width)[None, :] < lengths[:, None])[:, None, None, None, :]
    score_cache = jnp.where(valid, score_cache, -jnp.inf)
    score_new = (
        jnp.einsum("stkgd,sukd->stkgu", fresh_query, fresh_keys, preferred_element_type=jnp.float32)
        * score_scale
    )
    later = (jnp.arange(2)[:, None] >= jnp.arange(2)[None, :])[None, :, None, None, :]
    score_new = jnp.where(later, score_new, -jnp.inf)
    peak_loc = jnp.maximum(jnp.max(score_cache, axis=-1), jnp.max(score_new, axis=-1))
    expo_cache = jnp.exp(score_cache - peak_loc[..., None])
    expo_new = jnp.exp(score_new - peak_loc[..., None])
    sum_loc = jnp.sum(expo_cache, axis=-1) + jnp.sum(expo_new, axis=-1)
    acc_loc = jnp.einsum(
        "stkgj,sjkd->stkgd",
        expo_cache.astype(jnp.bfloat16),
        cached_rows[:, :, :, 1],
        preferred_element_type=jnp.float32,
    )
    acc_loc = acc_loc + jnp.einsum(
        "stkgu,sukd->stkgd",
        expo_new.astype(jnp.bfloat16),
        fresh_values,
        preferred_element_type=jnp.float32,
    )
    all_prefixes = lax.all_gather(handed, "grp", axis=0, tiled=True).reshape(
        -1, length, local_keys, 2, head_size
    )
    my_prompts = lax.dynamic_slice_in_dim(prompt_of[0], lax.axis_index("grp") * samples, samples)
    own_prefix = jnp.take(all_prefixes, my_prompts, axis=0)
    score_pre = (
        jnp.einsum(
            "stkgd,slkd->stkgl",
            fresh_query,
            own_prefix[:, :, :, 0],
            preferred_element_type=jnp.float32,
        )
        * score_scale
    )
    peak_pre = jnp.max(score_pre, axis=-1)
    expo_pre = jnp.exp(score_pre - peak_pre[..., None])
    sum_pre = jnp.sum(expo_pre, axis=-1)
    acc_pre = jnp.einsum(
        "stkgl,slkd->stkgd",
        expo_pre.astype(jnp.bfloat16),
        own_prefix[:, :, :, 1],
        preferred_element_type=jnp.float32,
    )
    peak_both = jnp.maximum(peak_pre, peak_loc)
    factor_pre = jnp.exp(peak_pre - peak_both)
    factor_loc = jnp.exp(peak_loc - peak_both)
    total_both = sum_pre * factor_pre + sum_loc * factor_loc
    acc_both = acc_pre * factor_pre[..., None] + acc_loc * factor_loc[..., None]
    decoded = (
        (acc_both / total_both[..., None])
        .astype(jnp.bfloat16)
        .reshape(samples * 2, local_query * head_size)
    )
    partial_out = jnp.dot(decoded, w_out, preferred_element_type=jnp.float32)
    summed_heads = lax.psum(partial_out.astype(jnp.bfloat16), "tp").astype(jnp.float32)
    decode_out = tokens.reshape(samples * 2, model_width).astype(jnp.float32) + summed_heads
    return (prefill_out, decode_out.reshape(1, samples, 2, model_width))


def solution(mesh):
    placed = (
        P("role", "grp", "tp", None),
        P("role", "grp", None, None),
        P("role", "grp", None, "tp"),
        P(),
        P(None, "tp"),
        P(None, "tp"),
        P(None, "tp"),
        P("tp", None),
        P("role", None),
        P("role", "grp"),
    )
    return jax.shard_map(
        shards,
        mesh=mesh,
        in_specs=placed,
        out_specs=(P("role", "grp", "tp", None), P("role", "grp", None, None)),
        check_vma=False,
    )
```

profile of v0, /device:TPU:1, one launch (start us, length us, event | category | flops | bytes accessed | tf_op | source)
XLA Modules:
  0.0 314.1 jit_solution(15202161657541779097)
XLA Ops:
  8.5 44.7 %all-gather.6.cloned.1.call-done = bf16[1,1,512,5120]{3,2,1,0:T(8,128)(2,1)} async-done(((bf16[1,1,64,5120]{3,2,1,0:T(8,128)(2,1)}), bf16[1,1,512,5120]{3,2,1,0:T(8,128)(2,1)}) %all-gather.6.cloned.1.call-update) | async-done | bytes 5242896 | tf_op jit(solution)/shard_map/all_gather | solution.py:54
  53.2 3.7 %fusion = f32[512]{0:T(512)S(1)} fusion(bf16[1,1,512,5120]{3,2,1,0:T(8,128)(2,1)} %all-gather.6.cloned.1.call-done), kind=kLoop, calls=%fused_computation.3 | loop fusion | flops 7863808 | bytes 5244928 | tf_op jit(solution)/shard_map/reduce_sum | solution.py:21
  57.2 2.0 fusion.80
  59.4 2.0 convolution_convert_fusion.2
  62.1 1.2 collective-permute-start
  63.8 2.3 copy.37
  66.2 3.6 %collective-permute-done = bf16[512,256]{0,1:T(8,128)(2,1)S(1)} collective-permute-done((bf16[512,256]{0,1:T(8,128)(2,1)S(1)}, bf16[512,256]{0,1:T(8,128)(2,1)S(1)}, u32[]{:S(2)}, u32[]{:S(2)}) %collective-permute-start) | collective-permute-done | bytes 262176 | tf_op jit(solution)/shard_map/ppermute | solution.py:16
  69.7 0.7 copy-done.8
  71.2 6.2 %copy.35 = bf16[5120,384]{0,1:T(8,128)(2,1)} copy(bf16[5120,384]{1,0:T(8,128)(2,1)} %param.14) | data formatting | bytes 7864320 | tf_op args[4]
  78.7 3.4 %fusion.88 = f32[32,3,128]{2,0,1:T(8,128)S(1)} fusion(bf16[32,5120,1]{1,0,2:T(8,128)(2,1)S(1)} %reshape.638, bf16[3,128,5120]{2,1,0:T(8,128)(2,1)} %bitcast.245), kind=kOutput, calls=%fused_computation.143 | convolution fusion | flops 125829120 | bytes 4308992 | tf_op jit(solution)/shard_map/dot_general | solution.py:123
  82.2 1.0 fusion.86
  83.3 1.4 fusion.85
  85.4 1.2 fusion.64
  87.5 2.1 convolution_bitcast_fusion
  89.6 1.0 convolution_convert_fusion.3
  90.6 4.9 %fusion.78 = f32[512,384]{0,1:T(8,128)S(1)} fusion(bf16[5120,384]{1,0:T(8,128)(2,1)S(1)} %copy-done.3, bf16[1,1,512,5120]{3,2,1,0:T(8,128)(2,1)} %all-gather.6.cloned.1.call-done, f32[5120]{0:T(1024)S(1)} %copy-done.9, f32[512]{0:T(512)} %copy-done.16), kind=kOutput, calls=%fused_computation.138 | convolution fusion | flops 2023751680 | bytes 9984000 | tf_op jit(solution)/shard_map/dot_general | solution.py:59
  96.0 0.8 fusion.5
  96.8 0.7 fusion.3
  97.5 1.1 fusion.36
  98.5 74.4 %all-gather.4.cloned.1.call-done = bf16[8192,256]{0,1:T(8,128)(2,1)} async-done(((bf16[512,256]{0,1:T(8,128)(2,1)}), bf16[8192,256]{0,1:T(8,128)(2,1)}) %all-gather.4.cloned.1.call-update) | async-done | bytes 4194320 | tf_op jit(solution)/shard_map/all_gather | solution.py:178
  172.9 6.0 %copy.54 = bf16[32,8,16,512]{3,2,1,0:T(8,128)(2,1)} copy(bf16[32,8,16,512]{3,1,2,0:T(8,128)(2,1)} %bitcast.246) | data formatting | bytes 8388608
  178.9 7.9 %copy.33 = bf16[16,512,2,128]{3,1,2,0:T(8,128)(2,1)} copy(bf16[16,512,2,128]{1,0,3,2:T(8,128)(2,1)} %bitcast.244) | data formatting | bytes 8388608 | tf_op jit(solution)/shard_map/reshape | solution.py:178
  186.8 5.2 %gather_fusion = bf16[16,512,2,128]{3,1,2,0:T(8,128)(2,1)} fusion(bf16[16,512,2,128]{3,1,2,0:T(8,128)(2,1)} %copy.33, s32[1024]{0:T(1024)S(1)} %pad_clamp_fusion), kind=kCustom, calls=%fused_computation | custom fusion | bytes 8388672 | tf_op jit(solution)/shard_map/jit(_take)/gather | solution.py:182
  192.0 2.7 bitcast_select_fusion
  194.7 0.8 fusion.87
  196.8 1.5 convolution_convert_fusion.1
  198.4 6.8 %convolution_convert_fusion = bf16[512,5120]{1,0:T(8,128)(2,1)} fusion(bf16[512,384]{0,1:T(8,128)(2,1)S(1)} %bitcast.253, bf16[384,5120]{1,0:T(8,128)(2,1)} %param.17), kind=kOutput, calls=%fused_computation.6 | convolution fusion | flops 2015887360 | bytes 9568256 | tf_op jit(solution)/shard_map/dot_general | solution.py:107
  205.2 56.5 %all-reduce.2.cloned.1.call-done = bf16[32,5120]{1,0:T(8,128)(2,1)} async-done(((bf16[32,5120]{1,0:T(8,128)(2,1)}), bf16[32,5120]{1,0:T(8,128)(2,1)}) %all-reduce.2.cloned.1.call-update) | async-done | bytes 327696 | tf_op jit(solution)/shard_map/psum | solution.py:212
  261.8 1.0 convert_add_fusion.1
  262.8 1.2 reshape.620
  264.0 41.5 %reduce-scatter.2.cloned.1.call-done = bf16[64,5120]{1,0:T(8,128)(2,1)} async-done(((bf16[512,5120]{1,0:T(8,128)(2,1)}), bf16[64,5120]{1,0:T(8,128)(2,1)}) %reduce-scatter.2.cloned.1.call-update) | async-done | bytes 655376 | tf_op jit(solution)/shard_map/reduce_scatter | solution.py:106
  305.5 2.1 fusion.40
  (90 shorter events, 8.5 us)
Async XLA Ops:
  7.2 49.8 %copy-start = (bf16[5120,128]{1,0:T(8,128)(2,1)S(1)}, bf16[5120,128]{1,0:T(8,128)(2,1)}, u32[]{:S(2)}) copy-start(bf16[5120,128]{1,0:T(8,128)(2,1)} %param.15) | copy-start | bytes 3932164
  7.2 49.8 %copy-start.9 = (f32[5120]{0:T(1024)S(1)}, f32[5120]{0:T(1024)}, u32[]{:S(2)}) copy-start(f32[5120]{0:T(1024)} %param.13) | copy-start | bytes 61444
  7.2 46.0 %all-gather.6.cloned.1.call-start = ((), (), s32[]{:S(2)}) async-start(), calls=%async_computation.4 | async-start | bytes 5898240 | tf_op jit(solution)/shard_map/all_gather | solution.py:54
  7.9 165.0 %all-gather.4.cloned.1.call-start = ((), (), s32[]{:S(2)}) async-start(), calls=%async_computation.2 | async-start | bytes 4456448 | tf_op jit(solution)/shard_map/all_gather | solution.py:178
  53.2 4.0 %copy-start.2 = (bf16[1,1,512,5120]{3,2,1,0:T(8,128)(2,1)S(1)}, bf16[1,1,512,5120]{3,2,1,0:T(8,128)(2,1)}, u32[]{:S(2)}) copy-start(bf16[1,1,512,5120]{3,2,1,0:T(8,128)(2,1)} %all-gather.6.cloned.1.call-done) | copy-start | bytes 15728644
  57.2 2.1 copy-start.16
  57.2 2.1 copy-start.6
  59.4 3.9 %copy-start.4 = (bf16[1,16,2,5120]{3,2,1,0:T(2,128)(2,1)S(1)}, bf16[1,16,2,5120]{3,2,1,0:T(2,128)(2,1)}, u32[]{:S(2)}) copy-start(bf16[1,16,2,5120]{3,2,1,0:T(2,128)(2,1)} %param.11) | copy-start | bytes 983044
  61.4 0.7 copy-start.10
  62.1 7.7 %collective-permute-start = (bf16[512,256]{0,1:T(8,128)(2,1)S(1)}, bf16[512,256]{0,1:T(8,128)(2,1)S(1)}, u32[]{:S(2)}, u32[]{:S(2)}) collective-permute-start(bf16[512,256]{0,1:T(8,128)(2,1)S(1)} %bitcast.255), channel_id=1, source_target_pairs={{0,128},{128,0},{1,129},{129,1},{2,130},{130,2},{3,131},{131,3},{4... | collective-permute-start | bytes 786440 | tf_op jit(solution)/shard_map/ppermute | solution.py:16
  66.2 11.9 %copy-start.15 = (f32[32]{0:T(128)}, f32[32]{0:T(128)S(1)}, u32[]{:S(2)}) copy-start(f32[32]{0:T(128)S(1)} %rsqrt.22) | copy-start | bytes 388
  69.7 0.7 copy-start.8
  70.5 191.3 %all-reduce.2.cloned.1.call-start = ((), (), s32[]{:S(2)}) async-start(), calls=%async_computation.3 | async-start | bytes 655360 | tf_op jit(solution)/shard_map/psum | solution.py:212
  71.2 6.2 %copy-start.18 = (s32[1,16]{1,0:T(1,128)S(1)}, s32[1,16]{1,0:T(1,128)}, u32[]{:S(2)}) copy-start(s32[1,16]{1,0:T(1,128)} %param.19) | copy-start | bytes 196
  78.1 6.6 %copy-start.19 = (s32[1,256]{1,0:T(1,128)S(1)}, s32[1,256]{1,0:T(1,128)}, u32[]{:S(2)}) copy-start(s32[1,256]{1,0:T(1,128)} %param.18) | copy-start | bytes 3076
  82.0 7.6 %copy-start.7 = (bf16[5120,128]{1,0:T(8,128)(2,1)S(1)}, bf16[5120,128]{1,0:T(8,128)(2,1)}, u32[]{:S(2)}) copy-start(bf16[5120,128]{1,0:T(8,128)(2,1)} %param.16) | copy-start | bytes 3932164
  82.2 2.5 copy-start.13
  84.7 5.9 %copy-start.3 = (bf16[5120,384]{1,0:T(8,128)(2,1)S(1)}, bf16[5120,384]{1,0:T(8,128)(2,1)}, u32[]{:S(2)}) copy-start(bf16[5120,384]{1,0:T(8,128)(2,1)} %param.14) | copy-start | bytes 11796484
  96.0 1.5 copy-start.11
  186.8 5.2 %copy-start.17 = (pred[16]{0:T(512)(128)(4,1)S(1)}, pred[16]{0:T(512)(128)(4,1)}, u32[]{:S(2)}) copy-start(pred[16]{0:T(512)(128)(4,1)} %compare_and_fusion) | copy-start | bytes 52
  192.0 2.7 copy-start.14
  192.0 3.8 %copy-start.12 = (f32[16,2,1,3,2]{3,4,1,0,2:T(2,128)S(1)}, f32[16,2,1,3,2]{3,4,1,0,2:T(2,128)}, u32[]{:S(2)}) copy-start(f32[16,2,1,3,2]{3,4,1,0,2:T(2,128)} %get-tuple-element.26) | copy-start | bytes 2308
  192.0 3.8 %copy-start.20 = (f32[16,128,2,3]{1,3,2,0:T(4,128)S(1)}, f32[16,128,2,3]{1,3,2,0:T(4,128)}, u32[]{:S(2)}) copy-start(f32[16,128,2,3]{1,3,2,0:T(4,128)} %convolution_bitcast_fusion) | copy-start | bytes 147460
  194.7 2.1 copy-start.1
  198.4 107.1 %reduce-scatter.2.cloned.1.call-start = ((), (), s32[]{:S(2)}) async-start(), calls=%async_computation.1 | async-start | bytes 5898240 | tf_op jit(solution)/shard_map/reduce_scatter | solution.py:106
  205.2 100.3 %copy-start.5 = (bf16[1,1,64,5120]{3,2,1,0:T(8,128)(2,1)S(1)}, bf16[1,1,64,5120]{3,2,1,0:T(8,128)(2,1)}, u32[]{:S(2)}) copy-start(bf16[1,1,64,5120]{3,2,1,0:T(8,128)(2,1)} %param.10) | copy-start | bytes 1966084
Sparse Core Ops, SparseCore 0:
  9.9 43.2 all-gather.5
  70.6 102.2 all-gather.3
  198.5 63.2 all-reduce.1
  264.3 41.1 reduce-scatter.1
where the time goes:
time: 317 us; the launch traced here: 314 us
  waiting for transfers between devices  221 us (70%)
  local copies, waits for them, and re-layouts  31.2 us (10%)
  matrix products  29.8 us (9%)
  other arithmetic  16 us (5%)
  between operations  14.2 us (4%)
    all_gather x1, waiting for transfers between devices, shards(): lax.all_gather(handed, 'grp', axis=0, tiled=True)  74.4 us
    psum x1, waiting for transfers between devices, shards(): lax.psum(partial_out.astype(jnp.bfloat16), 'tp').astype(jnp.float32)  56.5 us
    all_gather x1, waiting for transfers between devices, shards(): segment = lax.all_gather(token_rows, 'tp', axis=0, tiled=True)  44.7 us
    reduce_scatter x1, waiting for transfers between devices, shards(): lax.psum_scatter(jnp.dot(head_rows, w_out, preferred_element_type=jnp.flo...  41.5 us
    unnamed x45, local copies, waits for them, and re-layouts  16.5 us
    reshape x1, local copies, waits for them, and re-layouts, shards(): lax.all_gather(handed, 'grp', axis=0, tiled=True)  7.88 us
    dot_general x1, matrix products, shards(): jnp.dot(head_rows, w_out, preferred_element_type=jnp.float32)  6.77 us
  transfers between devices with their start and end apart: 5, of which 5 were waited for; matrix products, arithmetic and copies ran while one was open for 13% of the time, Pallas kernels for 0%

commit v1 on v0

v1 whole, which is shorter than its diff:
```python
import functools

import jax
import jax.numpy as jnp
from jax import lax
from jax.experimental import pallas as pl
from jax.experimental.pallas import tpu as pltpu
from jax.sharding import PartitionSpec as P

HEAD_WIDTH = 128
EPSILON = 1e-06
ROPE_BASE = 1000000.0
GROUP_STEPS = (4, 2, 1, 8)
VMEM_LIMIT = 40 * 1024 * 1024


def normalize(entries, scales):
    wide = entries.astype(jnp.float32)
    factor = lax.rsqrt(jnp.mean(wide * wide, axis=-1, keepdims=True) + EPSILON)
    return (wide * factor * scales).astype(jnp.bfloat16)


def rope_tables(positions):
    half = HEAD_WIDTH // 2
    frequency = ROPE_BASE ** (-2.0 * jnp.arange(half, dtype=jnp.float32) / HEAD_WIDTH)
    angles = positions.astype(jnp.float32)[:, None] * frequency
    cosine, sine = jnp.cos(angles), jnp.sin(angles)
    return jnp.concatenate([cosine, cosine], 1), jnp.concatenate([-sine, sine], 1)


def qkv_body(counts, steps, *refs):
    n = len(counts)
    xs, (wq, wk, wv, cos, sin, q_out, kv_out, acc) = refs[:n], refs[n:]
    step = pl.program_id(0)
    x = jnp.concatenate([r[...] for r in xs], axis=0) if n > 1 else xs[0][...]
    w = jnp.concatenate([wq[...], wk[...], wv[...]], axis=1)
    part = jnp.dot(x, w, preferred_element_type=jnp.float32)

    @pl.when(step == 0)
    def _():
        acc[...] = part

    @pl.when(step > 0)
    def _():
        acc[...] += part

    @pl.when(step == steps - 1)
    def _():
        c, s = cos[...], sin[...]
        wide = wq.shape[1]
        for h in range(wide // HEAD_WIDTH + 1):
            v = acc[:, h * HEAD_WIDTH : (h + 1) * HEAD_WIDTH]
            v = (v * c + pltpu.roll(v, HEAD_WIDTH // 2, 1) * s).astype(jnp.bfloat16)
            if h * HEAD_WIDTH < wide:
                q_out[:, h * HEAD_WIDTH : (h + 1) * HEAD_WIDTH] = v
            else:
                kv_out[:, :HEAD_WIDTH] = v
        kv_out[:, HEAD_WIDTH:] = acc[:, wide + HEAD_WIDTH :].astype(jnp.bfloat16)


def qkv(blocks, wq, wk, wv, tables):
    counts = [b.shape[0] for b in blocks]
    rows, depth = sum(counts), wq.shape[0]
    steps = 5 if depth % 640 == 0 else 1
    tile = depth // steps
    wide = wq.shape[1]
    whole = lambda shape: pl.BlockSpec(shape, lambda k: (0, 0))
    return pl.pallas_call(
        functools.partial(qkv_body, counts, steps),
        grid=(steps,),
        in_specs=[pl.BlockSpec((c, tile), lambda k: (0, k)) for c in counts]
        + [pl.BlockSpec((tile, w.shape[1]), lambda k: (k, 0)) for w in (wq, wk, wv)]
        + [whole((rows, HEAD_WIDTH))] * 2,
        out_specs=[whole((rows, wide)), whole((rows, 2 * HEAD_WIDTH))],
        out_shape=[
            jax.ShapeDtypeStruct((rows, wide), jnp.bfloat16),
            jax.ShapeDtypeStruct((rows, 2 * HEAD_WIDTH), jnp.bfloat16),
        ],
        scratch_shapes=[pltpu.VMEM((rows, wide + 2 * HEAD_WIDTH), jnp.float32)],
        compiler_params=pltpu.CompilerParams(vmem_limit_bytes=VMEM_LIMIT),
        cost_estimate=pl.CostEstimate(
            flops=2 * rows * depth * (wide + 256),
            bytes_accessed=2 * depth * (wide + 256 + rows),
            transcendentals=0,
        ),
    )(*blocks, wq, wk, wv, *tables)


def dot_t(a, b):
    return lax.dot_general(a, b, (((1,), (1,)), ((), ())), preferred_element_type=jnp.float32)


def simple_call(body, out_shape, flops, *args):
    nbytes = sum(a.size * a.dtype.itemsize for a in args)
    return pl.pallas_call(
        body,
        in_specs=[pl.BlockSpec(memory_space=pltpu.VMEM)] * len(args),
        out_specs=jax.tree.map(lambda _: pl.BlockSpec(memory_space=pltpu.VMEM), out_shape),
        out_shape=out_shape,
        compiler_params=pltpu.CompilerParams(vmem_limit_bytes=VMEM_LIMIT),
        cost_estimate=pl.CostEstimate(flops=flops, bytes_accessed=nbytes, transcendentals=0),
    )(*args)


def local_body(scale, q, kv, cache, lengths, out, stats):
    width, rows = HEAD_WIDTH, q.shape[0]
    groups, samples = q.shape[1] // width, cache.shape[0]
    slots = cache.shape[1]
    query = jnp.concatenate([q[:, g * width : (g + 1) * width] for g in range(groups)], axis=0)
    old = cache[...].reshape(samples * slots, 2 * width)
    total = groups * rows
    row = lax.broadcasted_iota(jnp.int32, (total, 1), 0) % rows
    column = lax.broadcasted_iota(jnp.int32, (1, samples * slots), 1)
    score_old = dot_t(query, old[:, :width]) * scale
    limit = row // 2 * slots + lengths[...]
    allowed = (column >= row // 2 * slots) & (column < limit)
    score_old = jnp.where(allowed, score_old, -jnp.inf)
    fresh = lax.broadcasted_iota(jnp.int32, (1, rows), 1)
    score_new = dot_t(query, kv[:, :width]) * scale
    score_new = jnp.where((fresh // 2 == row // 2) & (fresh <= row), score_new, -jnp.inf)
    peak = jnp.maximum(
        jnp.max(score_old, axis=1, keepdims=True), jnp.max(score_new, axis=1, keepdims=True)
    )
    expo_old, expo_new = jnp.exp(score_old - peak), jnp.exp(score_new - peak)
    both = jnp.sum(expo_old, axis=1, keepdims=True) + jnp.sum(expo_new, axis=1, keepdims=True)
    mixed = jnp.dot(
        expo_old.astype(jnp.bfloat16), old[:, width:], preferred_element_type=jnp.float32
    ) + jnp.dot(
        expo_new.astype(jnp.bfloat16), kv[:, width:], preferred_element_type=jnp.float32
    )
    out[...] = mixed
    lane = lax.broadcasted_iota(jnp.int32, stats.shape, 1)
    stats[...] = jnp.where(lane == 0, peak, both)


def local_attention(q, kv, cache, lengths, scale):
    total = q.shape[1] // HEAD_WIDTH * q.shape[0]
    shape = jax.ShapeDtypeStruct((total, HEAD_WIDTH), jnp.float32)
    flops = 4 * total * cache.shape[0] * cache.shape[1] * HEAD_WIDTH
    return simple_call(
        functools.partial(local_body, scale), (shape, shape), flops, q, kv, cache, lengths
    )


def prefix_body(scale, q, wanted, names, kv_a, kv_b, out):
    width, rows = HEAD_WIDTH, wanted.shape[0]
    groups = q.shape[1] // width
    chosen = (names[...] == wanted[...]).astype(jnp.bfloat16)
    picked = jnp.dot(chosen, q[...], preferred_element_type=jnp.float32).astype(jnp.bfloat16)
    query = jnp.concatenate([picked[:, g * width : (g + 1) * width] for g in range(groups)], axis=0)
    pairs = jnp.concatenate([kv_a[...], kv_b[...]], axis=0)
    score = dot_t(query, pairs[:, :width]) * scale
    peak = jnp.max(score, axis=1, keepdims=True)
    expo = jnp.exp(score - peak)
    both = jnp.sum(expo, axis=1, keepdims=True)
    mixed = jnp.dot(expo.astype(jnp.bfloat16), pairs[:, width:], preferred_element_type=jnp.float32)
    mixed = (mixed / both).astype(jnp.bfloat16)
    level = peak + jnp.log(both)
    lane = lax.broadcasted_iota(jnp.int32, (rows, width), 1)
    tail = jnp.zeros((rows, width), jnp.bfloat16)
    for g in range(groups):
        out[:, g * width : (g + 1) * width] = mixed[g * rows : (g + 1) * rows]
        rest = level[g * rows : (g + 1) * rows]
        for part in range(3):
            high = rest.astype(jnp.bfloat16)
            rest = rest - high.astype(jnp.float32)
            tail = jnp.where(lane == g * 3 + part, high, tail)
    out[:, groups * width :] = tail


def prefix_attention(q, wanted, names, kv_a, kv_b, scale):
    rows = wanted.shape[0]
    shape = jax.ShapeDtypeStruct((rows, q.shape[1] + HEAD_WIDTH), jnp.bfloat16)
    return simple_call(
        functools.partial(prefix_body, scale), shape, 100_000_000, q, wanted, names, kv_a, kv_b
    )


def merge_body(back, wanted, names, local, stats, out):
    width, rows = HEAD_WIDTH, wanted.shape[0]
    groups = local.shape[0] // rows
    chosen = (names[...] == wanted[...]).astype(jnp.bfloat16)
    picked = jnp.dot(chosen, back[...], preferred_element_type=jnp.float32)
    tail = picked[:, groups * width :]
    for g in range(groups):
        level = tail[:, g * 3 : g * 3 + 1] + tail[:, g * 3 + 1 : g * 3 + 2]
        level = level + tail[:, g * 3 + 2 : g * 3 + 3]
        peak = stats[g * rows : (g + 1) * rows, 0:1]
        both = stats[g * rows : (g + 1) * rows, 1:2]
        top = jnp.maximum(level, peak)
        factor_pre, factor_loc = jnp.exp(level - top), jnp.exp(peak - top)
        total = factor_pre + both * factor_loc
        mixed = picked[:, g * width : (g + 1) * width] * factor_pre
        mixed = mixed + local[g * rows : (g + 1) * rows] * factor_loc
        out[:, g * width : (g + 1) * width] = (mixed / total).astype(jnp.bfloat16)


def merge(back, wanted, names, local, stats):
    rows = wanted.shape[0]
    shape = jax.ShapeDtypeStruct((rows, back.shape[1] - HEAD_WIDTH), jnp.bfloat16)
    return simple_call(merge_body, shape, 10_000_000, back, wanted, names, local, stats)


def prefill_body(scale, mine_a, mine_b, q_a, q_b, kv_a, kv_b, place_row, place_column, own, other):
    width = HEAD_WIDTH
    groups = q_a.shape[1] // width
    pairs = jnp.concatenate([kv_a[...], kv_b[...]], axis=0)
    allowed = place_row[...] >= place_column[...]
    count_a, count_b = q_a.shape[0], q_b.shape[0]
    for g in range(groups):
        cols = slice(g * width, (g + 1) * width)
        query = jnp.concatenate([q_a[:, cols], q_b[:, cols]], axis=0)
        score = jnp.where(allowed, dot_t(query, pairs[:, :width]) * scale, -jnp.inf)
        expo = jnp.exp(score - jnp.max(score, axis=1, keepdims=True))
        both = jnp.sum(expo, axis=1, keepdims=True)
        mixed = jnp.dot(
            expo.astype(jnp.bfloat16), pairs[:, width:], preferred_element_type=jnp.float32
        )
        mixed = (mixed / both).astype(jnp.bfloat16)
        own[:mine_a, cols] = mixed[:mine_a]
        other[:mine_a, cols] = mixed[mine_a:count_a]
        own[mine_a:, cols] = mixed[count_a : count_a + mine_b]
        other[mine_a:, cols] = mixed[count_a + mine_b :]


def prefill_attention(q_a, q_b, kv_a, kv_b, places, scale):
    mine_a, mine_b = q_a.shape[0] // 2, q_b.shape[0] // 2
    shape = jax.ShapeDtypeStruct((mine_a + mine_b, q_a.shape[1]), jnp.bfloat16)
    length = q_a.shape[0] + q_b.shape[0]
    return simple_call(
        functools.partial(prefill_body, scale, mine_a, mine_b),
        (shape, shape),
        4 * length * length * q_a.shape[1],
        q_a, q_b, kv_a, kv_b, places[:, None], places[None, :],
    )


def out_body(own, other, w_own, w_other, *outs):
    part = jnp.dot(own[...], w_own[...], preferred_element_type=jnp.float32)
    part = part + jnp.dot(other[...], w_other[...], preferred_element_type=jnp.float32)
    rows = outs[0].shape[0]
    for i, out in enumerate(outs):
        out[...] = part[i * rows : (i + 1) * rows].astype(out.dtype)


def out_projection(own, other, w_own, w_other, block, dtype):
    rows, depth = own.shape
    wide = w_own.shape[1]
    tile = 512 if wide % 512 == 0 else wide
    count = rows // block
    return pl.pallas_call(
        out_body,
        grid=(wide // tile,),
        in_specs=[pl.BlockSpec((rows, depth), lambda n: (0, 0))] * 2
        + [pl.BlockSpec((depth, tile), lambda n: (0, n))] * 2,
        out_specs=[pl.BlockSpec((block, tile), lambda n: (0, n))] * count,
        out_shape=[jax.ShapeDtypeStruct((block, wide), dtype)] * count,
        compiler_params=pltpu.CompilerParams(vmem_limit_bytes=VMEM_LIMIT),
        cost_estimate=pl.CostEstimate(
            flops=4 * rows * depth * wide,
            bytes_accessed=4 * depth * wide + 2 * rows * wide,
            transcendentals=0,
        ),
    )(own, other, w_own, w_other)


def partial_body(heads, w, out):
    out[...] = jnp.dot(heads[...], w[...], preferred_element_type=jnp.float32).astype(out.dtype)


def partial_projection(heads, w):
    rows, depth = heads.shape
    wide = w.shape[1]
    tile = 1024 if wide % 1024 == 0 else wide
    return pl.pallas_call(
        partial_body,
        grid=(wide // tile,),
        in_specs=[
            pl.BlockSpec((rows, depth), lambda n: (0, 0)),
            pl.BlockSpec((depth, tile), lambda n: (0, n)),
        ],
        out_specs=pl.BlockSpec((rows, tile), lambda n: (0, n)),
        out_shape=jax.ShapeDtypeStruct((rows, wide), jnp.bfloat16),
        compiler_params=pltpu.CompilerParams(vmem_limit_bytes=VMEM_LIMIT),
        cost_estimate=pl.CostEstimate(
            flops=2 * rows * depth * wide, bytes_accessed=2 * depth * wide, transcendentals=0
        ),
    )(heads, w)


def shards(
    prompt_states,
    new_states,
    answer_cache,
    attn_gain,
    w_query,
    key_weight,
    value_weight,
    w_out,
    prompt_of,
    suffix_len,
):
    scale = HEAD_WIDTH ** (-0.5)
    rows = prompt_states[0, 0]
    block, width = rows.shape
    tp, grp = lax.axis_index("tp"), lax.axis_index("grp")
    y, core = tp // 2, tp % 2
    tp_size, grp_size = lax.axis_size("tp"), lax.axis_size("grp")
    chips = tp_size // 2

    def around(value, by):
        return lax.ppermute(value, "tp", [(i, (i + 2 * by) % tp_size) for i in range(tp_size)])

    def swap(value, axis, mask):
        return lax.ppermute(value, axis, [(i, i ^ mask) for i in range(lax.axis_size(axis))])

    normed = normalize(rows, attn_gain)
    from_down = around(normed, 1)
    from_up = around(normed, -1)
    mate_own = swap(normed, "tp", 1)

    samples = new_states.shape[1]
    lengths = suffix_len[0]
    tokens = new_states[0].reshape(samples * 2, width)
    fresh_places = (
        block * tp_size + lengths[:, None] + jnp.arange(2, dtype=jnp.int32)
    ).reshape(samples * 2)
    fresh_q, fresh_kv = qkv(
        [normalize(tokens, attn_gain)], w_query, key_weight, value_weight, rope_tables(fresh_places)
    )
    gathered = fresh_q
    order = [0]
    for mask in GROUP_STEPS:
        gathered = jnp.concatenate([gathered, swap(gathered, "grp", mask)], axis=0)
        order = order + [k ^ mask for k in order]
    owners = jnp.bitwise_xor(jnp.array(order, dtype=jnp.int32), grp)
    names = (owners[:, None] * (samples * 2) + jnp.arange(samples * 2, dtype=jnp.int32)).reshape(
        1, -1
    )
    w_mate = swap(w_out, "tp", 1)

    half = block // 2
    ahead = around(from_down[:half], 1)
    behind = around(from_up[half:], -1)
    mate_down = swap(from_down, "tp", 1)
    mate_up = swap(from_up, "tp", 1)
    far = jnp.concatenate([ahead, behind], axis=0)
    mate_far = swap(far, "tp", 1)

    prompts = prompt_of[0]
    index = jnp.arange(prompts.shape[0], dtype=jnp.int32)
    same = prompts[:, None] == prompts[None, :]
    rank = jnp.sum((same & (index[None, :] < index[:, None])).astype(jnp.int32), axis=1)
    slot = jnp.arange(samples, dtype=jnp.int32)
    hit = (prompts == grp)[None, :] & (rank[None, :] == slot[:, None])
    sought = jnp.sum(jnp.where(hit, index[None, :], 0), axis=1)
    pair = jnp.arange(2, dtype=jnp.int32)
    wanted = (sought[:, None] * 2 + pair).reshape(samples * 2, 1)
    home = lax.dynamic_slice_in_dim(prompts * samples + rank, grp * samples, samples)
    returned = (home[:, None] * 2 + pair).reshape(samples * 2, 1)
    groups = w_query.shape[1] // HEAD_WIDTH
    limits = jnp.tile(jnp.repeat(lengths, 2), groups)[:, None]

    turns = jnp.array([0, -1, 1, 2], dtype=jnp.int32)
    chip = (y + turns) % chips
    inside = jnp.arange(block, dtype=jnp.int32)
    mine = ((2 * chip + core) * block)[:, None] + inside
    theirs = ((2 * chip + 1 - core) * block)[:, None] + inside
    places_a = jnp.concatenate([mine[:3].reshape(-1), theirs[:3].reshape(-1)])
    places_b = jnp.concatenate([mine[3], theirs[3]])
    places = jnp.concatenate([places_a, places_b])

    weights = (w_query, key_weight, value_weight)
    q_a, kv_a = qkv(
        [normed, from_down, from_up, mate_own, mate_down, mate_up], *weights, rope_tables(places_a)
    )
    handed_a = swap(kv_a, "role", 1)
    q_b, kv_b = qkv([far, mate_far], *weights, rope_tables(places_b))
    handed_b = swap(kv_b, "role", 1)

    local, stats = local_attention(fresh_q, fresh_kv, answer_cache[0], limits, scale)

    heads_own, heads_other = prefill_attention(q_a, q_b, kv_a, kv_b, places, scale)
    heads_mate = swap(heads_other, "tp", 1)
    near = 3 * block
    to_own, to_down, to_up, to_far = out_projection(
        heads_own, heads_mate, w_out, w_mate, block, jnp.bfloat16
    )
    sum_far = around(to_far, 2)
    sum_up = around(to_up, 1)
    sum_down = around(to_down, -1)

    answered = prefix_attention(gathered, wanted, names, handed_a, handed_b, scale)
    spread = jnp.broadcast_to(answered[None], (grp_size,) + answered.shape)
    back = lax.all_to_all(spread, "grp", 0, 0, tiled=False)
    back = back.reshape(grp_size * samples * 2, -1)
    decoded = merge(
        back, returned, jnp.arange(back.shape[0], dtype=jnp.int32)[None, :], local, stats
    )
    partial = partial_projection(decoded, w_out)
    kept = lax.dynamic_slice_in_dim(partial, core * samples, samples)
    given = lax.dynamic_slice_in_dim(partial, (1 - core) * samples, samples)
    taken = swap(given, "tp", 1)
    level = lax.optimization_barrier(
        (kept.astype(jnp.float32) + taken.astype(jnp.float32)).astype(jnp.bfloat16)
    )
    taken = swap(level, "tp", 2)
    level = lax.optimization_barrier(
        (level.astype(jnp.float32) + taken.astype(jnp.float32)).astype(jnp.bfloat16)
    )
    taken = swap(level, "tp", 4)
    summed = level.astype(jnp.float32) + taken.astype(jnp.float32)
    theirs_sum = swap(summed, "tp", 1)
    low = jnp.where(core == 0, summed, theirs_sum)
    high = jnp.where(core == 0, theirs_sum, summed)
    total = jnp.concatenate([low, high], axis=0)
    decode_out = tokens.astype(jnp.float32) + total

    prefill_out = (
        rows.astype(jnp.float32)
        + to_own.astype(jnp.float32)
        + sum_far.astype(jnp.float32)
        + sum_up.astype(jnp.float32)
        + sum_down.astype(jnp.float32)
    ).astype(jnp.bfloat16)
    return prefill_out[None, None], decode_out.reshape(1, samples, 2, width)


def solution(mesh):
    placed = (
        P("role", "grp", "tp", None),
        P("role", "grp", None, None),
        P("role", "grp", None, "tp"),
        P(),
        P(None, "tp"),
        P(None, "tp"),
        P(None, "tp"),
        P("tp", None),
        P("role", None),
        P("role", "grp"),
    )
    return jax.shard_map(
        shards,
        mesh=mesh,
        in_specs=placed,
        out_specs=(P("role", "grp", "tp", None), P("role", "grp", None, None)),
        check_vma=False,
    )
```

time: 317 us -> 168 us (0.53)
  waiting for transfers between devices: 221 us -> 60 us
  starting transfers between devices: 1.52 us -> 44.2 us
  matrix products: 29.8 us -> 0 us
  Pallas kernels: 0 us -> 23.9 us
  between operations: 14.2 us -> 1.2 us
  local copies, waits for them, and re-layouts: 31.2 us -> 18.5 us
  other arithmetic: 16 us -> 19.2 us
    all_gather x2 -> x0, waiting for transfers between devices: 119 us -> none  [the longest x1 74.4 us: shards(): lax.all_gather(handed, 'grp', axis=0, tiled=True)]
    psum x1 -> x0, waiting for transfers between devices: 56.5 us -> none  [shards(): lax.psum(partial_out.astype(jnp.bfloat16), 'tp').astype(jnp.float32)]
    ppermute x1 -> x23, waiting for transfers between devices: 3.57 us -> 47.6 us  [the longest x7 31.7 us: around(): lax.ppermute(value, 'tp', [(i, (i + 2 * by) % tp_size) for i in range(tp_...]
    reduce_scatter x1 -> x0, waiting for transfers between devices: 41.5 us -> none  [shards(): lax.psum_scatter(jnp.dot(head_rows, w_out, preferred_element_type=jnp.flo...]
    ppermute x1 -> x23, starting transfers between devices: 1.18 us -> 40.6 us  [the longest x16 29.6 us: swap(): lax.ppermute(value, axis, [(i, i ^ mask) for i in range(lax.axis_size(axi...]
    dot_general x16 -> x0, matrix products: 29.8 us -> none  [the longest x1 6.77 us: shards(): jnp.dot(head_rows, w_out, preferred_element_type=jnp.float32)]
    pallas_call x0 -> x9, Pallas kernels: none -> 23.9 us  [the longest x3 10.6 us: qkv(): pl.pallas_call(functools.partial(qkv_body, counts, steps), grid=(steps,),...]
    all_to_all x0 -> x1, waiting for transfers between devices: none -> 12.3 us  [shards(): back = lax.all_to_all(spread, 'grp', 0, 0, tiled=False)]
  transfers between devices with their start and end apart: 5 -> 24, of which waited for: 5 -> 12; matrix products, arithmetic and copies ran while one was open for 13% -> 15% of each run, Pallas kernels for 0% -> 8%
where the time goes in v1:
time: 168 us; the launch traced here: 167 us
  waiting for transfers between devices  60 us (36%)
  starting transfers between devices  44.2 us (26%)
  Pallas kernels  23.9 us (14%)
  other arithmetic  19.2 us (11%)
  local copies, waits for them, and re-layouts  18.5 us (11%)
    ppermute x7, waiting for transfers between devices, around(): lax.ppermute(value, 'tp', [(i, (i + 2 * by) % tp_size) for i in range(tp_...  31.7 us
    ppermute x16, starting transfers between devices, swap(): lax.ppermute(value, axis, [(i, i ^ mask) for i in range(lax.axis_size(axi...  29.6 us
    ppermute x16, waiting for transfers between devices, swap(): lax.ppermute(value, axis, [(i, i ^ mask) for i in range(lax.axis_size(axi...  16 us
    all_to_all x1, waiting for transfers between devices, shards(): back = lax.all_to_all(spread, 'grp', 0, 0, tiled=False)  12.3 us
    unnamed x69, local copies, waits for them, and re-layouts  11.5 us
    ppermute x7, starting transfers between devices, around(): lax.ppermute(value, 'tp', [(i, (i + 2 * by) % tp_size) for i in range(tp_...  11 us
    pallas_call x3, Pallas kernels, qkv(): pl.pallas_call(functools.partial(qkv_body, counts, steps), grid=(steps,),...  10.6 us
    pallas_call x1, Pallas kernels, out_projection(): pl.pallas_call(out_body, grid=(wide // tile,), in_specs=[pl.BlockSpec((ro...  8.05 us
  transfers between devices with their start and end apart: 24, of which 12 were waited for; matrix products, arithmetic and copies ran while one was open for 15% of the time, Pallas kernels for 8%

profile of v1, /device:TPU:1, one launch (start us, length us, event | category | flops | bytes accessed | tf_op | source)
XLA Modules:
  0.0 167.0 jit_solution(17942447188948395436)
XLA Ops:
  3.4 2.2 %collective-permute-start = (bf16[64,5120]{1,0:T(8,128)(2,1)S(1)}, bf16[64,5120]{1,0:T(8,128)(2,1)}, u32[]{:S(2)}, u32[]{:S(2)}) collective-permute-start(bf16[64,5120]{1,0:T(8,128)(2,1)S(1)} %fusion.2.refs_0_), channel_id=1, source_target_pairs={{0,2},{1,3},{2,4},{3,5},{4,6},{5,7},{6,0},{7,1},{8,10},{9,11},{10,... | collective-permute-start | bytes 1966088 | tf_op jit(solution)/shard_map/ppermute | solution.py:312
  7.2 2.8 %collective-permute-start.2 = (bf16[64,5120]{1,0:T(8,128)(2,1)S(1)}, bf16[64,5120]{1,0:T(8,128)(2,1)}, u32[]{:S(2)}, u32[]{:S(2)}) collective-permute-start(bf16[64,5120]{1,0:T(8,128)(2,1)S(1)} %fusion.2.refs_0_), channel_id=1, source_target_pairs={{0,1},{1,0},{2,3},{3,2},{4,5},{5,4},{6,7},{7,6},{8,9},{9,8},{10,11... | collective-permute-start | bytes 1966088 | tf_op jit(solution)/shard_map/ppermute | solution.py:315
  10.0 1.9 %reshape.187 = f32[32,5120]{1,0:T(8,128)} reshape(bf16[1,16,2,5120]{3,2,1,0:T(2,128)(2,1)} %param.13) | data formatting | bytes 983040 | tf_op jit(solution)/shard_map/convert_element_type | solution.py:417
  15.1 2.1 %copy-done = bf16[5120,384]{1,0:T(8,128)(2,1)S(1)} copy-done((bf16[5120,384]{1,0:T(8,128)(2,1)S(1)}, bf16[5120,384]{1,0:T(8,128)(2,1)}, u32[]{:S(2)}) %copy-start) | copy-done | bytes 3932184
  17.2 1.9 %shard_map.135 = (bf16[32,384]{1,0:T(8,128)(2,1)S(1)}, bf16[32,256]{1,0:T(8,128)(2,1)S(1)}) custom-call(bf16[32,5120]{1,0:T(8,128)(2,1)S(1)} %multiply_convert_fusion.refs_0_, bf16[5120,384]{1,0:T(8,128)(2,1)S(1)} %copy-done, bf16[5120,128]{1,0:T(8,128)(2,1)S(1)} %copy-done.5, bf16[5120,128]{1,0:T(8,128)(2,1)S(1)} %copy-done.6, ...), custom_call_target="tpu_custom_call" | custom-call | flops 209715200 | bytes 6881280 | tf_op jit(solution)/shard_map/pallas_call | solution.py:68
  19.1 5.3 %collective-permute-start.13 = (bf16[32,384]{1,0:T(8,128)(2,1)S(1)}, bf16[32,384]{1,0:T(8,128)(2,1)}, u32[]{:S(2)}, u32[]{:S(2)}) collective-permute-start(bf16[32,384]{1,0:T(8,128)(2,1)S(1)} %get-tuple-element.26.q), channel_id=1, source_target_pairs={{0,32},{8,40},{16,48},{24,56},{32,0},{40,8},{48,16},{56,24},{64,96... | collective-permute-start | bytes 73736 | tf_op jit(solution)/shard_map/ppermute | solution.py:315
  27.9 2.0 %pad_maximum_fusion.1 = (f32[384,128]{1,0:T(8,128)S(1)}, f32[384,128]{1,0:T(8,128)}) fusion(f32[384,64]{1,0:T(8,128)} %get-tuple-element.36, f32[384,64]{1,0:T(8,128)} %get-tuple-element.35, f32[384,64]{1,0:T(8,128)} %get-tuple-element.34), kind=kLoop, calls=%fused_computation.23 | loop fusion | flops 98304 | bytes 688128 | tf_op jit(solution)/shard_map/concatenate | solution.py:28
  29.9 1.6 pad_maximum_fusion.5.refs_5_
  31.6 1.6 pad_maximum_fusion.6.refs_6_
  33.3 1.7 %slice.24 = bf16[32,5120]{1,0:T(8,128)(2,1)} slice(bf16[64,5120]{1,0:T(8,128)(2,1)} %collective-permute-done.refs_1_), slice={[0:32], [0:5120]} | slice | bytes 655360 | tf_op jit(solution)/shard_map/slice | solution.py:343
  40.2 2.7 %collective-permute-start.6 = (bf16[32,5120]{1,0:T(8,128)(2,1)S(1)}, bf16[32,5120]{1,0:T(8,128)(2,1)S(1)}, u32[]{:S(2)}, u32[]{:S(2)}) collective-permute-start(bf16[32,5120]{1,0:T(8,128)(2,1)S(1)} %slice.25), channel_id=1, source_target_pairs={{0,6},{1,7},{2,0},{3,1},{4,2},{5,3},{6,4},{7,5},{8,14},{9,15},{10,... | collective-permute-start | bytes 983048 | tf_op jit(solution)/shard_map/ppermute | solution.py:312
  49.1 1.8 %collective-permute-start.7 = (bf16[64,5120]{1,0:T(8,128)(2,1)S(1)}, bf16[64,5120]{1,0:T(8,128)(2,1)S(1)}, u32[]{:S(2)}, u32[]{:S(2)}) collective-permute-start(bf16[64,5120]{1,0:T(8,128)(2,1)S(1)} %constant_dynamic-update-slice_fusion.refs_0_), channel_id=1, source_target_pairs={{0,1},{1,0},{2,3},{3,2},{4,5},{5,4},{6,7},{7,6},{8,9},{9,8},{10,11... | collective-permute-start | bytes 1966088 | tf_op jit(solution)/shard_map/ppermute | solution.py:315
  52.5 3.7 %collective-permute-done.15 = bf16[128,384]{1,0:T(8,128)(2,1)S(1)} collective-permute-done((bf16[128,384]{1,0:T(8,128)(2,1)S(1)}, bf16[128,384]{1,0:T(8,128)(2,1)S(1)}, u32[]{:S(2)}, u32[]{:S(2)}) %collective-permute-start.15) | collective-permute-done | bytes 98336 | tf_op jit(solution)/shard_map/ppermute | solution.py:315
  56.9 2.8 %collective-permute-start.16 = (bf16[256,384]{1,0:T(8,128)(2,1)S(1)}, bf16[256,384]{1,0:T(8,128)(2,1)S(1)}, u32[]{:S(2)}, u32[]{:S(2)}) collective-permute-start(bf16[256,384]{1,0:T(8,128)(2,1)S(1)} %pad_maximum_fusion.3), channel_id=1, source_target_pairs={{0,64},{8,72},{16,80},{24,88},{32,96},{40,104},{48,112},{56,120},{... | collective-permute-start | bytes 589832 | tf_op jit(solution)/shard_map/ppermute | solution.py:315
  59.8 2.1 %copy-done.1 = bf16[5120,384]{1,0:T(8,128)(2,1)S(1)} copy-done((bf16[5120,384]{1,0:T(8,128)(2,1)S(1)}, bf16[5120,384]{1,0:T(8,128)(2,1)}, u32[]{:S(2)}) %copy-start.1) | copy-done | bytes 3932184
  61.9 6.3 %shard_map.131 = (bf16[384,384]{1,0:T(8,128)(2,1)S(1)}, bf16[384,256]{1,0:T(8,128)(2,1)S(1)}) custom-call(bf16[64,5120]{1,0:T(8,128)(2,1)S(1)} %fusion.2.refs_0_, bf16[64,5120]{1,0:T(8,128)(2,1)} %collective-permute-done.refs_1_, bf16[64,5120]{1,0:T(8,128)(2,1)} %collective-permute-done.1.refs_2_, bf16[64,5120]{1,0:T(8,128)(2,1)} %collective-permute-done.2.refs_3_, ...), custom_call_target="tpu_custom_call" | custom-call | flops 2516582400 | bytes 10485760 | tf_op jit(solution)/shard_map/pallas_call | solution.py:68
  68.8 2.4 %shard_map.132 = (bf16[128,384]{1,0:T(8,128)(2,1)S(1)}, bf16[128,256]{1,0:T(8,128)(2,1)S(1)}) custom-call(bf16[64,5120]{1,0:T(8,128)(2,1)S(1)} %constant_dynamic-update-slice_fusion.refs_0_, bf16[64,5120]{1,0:T(8,128)(2,1)S(1)} %collective-permute-done.7.refs_1_, bf16[5120,384]{1,0:T(8,128)(2,1)S(1)} %copy-done.2, bf16[5120,128]{1,0:T(8,128)(2,1)S(1)} %copy-done.5, ...), custom_call_target="tpu_custom_call" | custom-call | flops 838860800 | bytes 7864320 | tf_op jit(solution)/shard_map/pallas_call | solution.py:68
  73.8 1.7 %collective-permute-done.18.kv_b = bf16[128,256]{1,0:T(8,128)(2,1)S(1)} collective-permute-done((bf16[128,256]{1,0:T(8,128)(2,1)S(1)}, bf16[128,256]{1,0:T(8,128)(2,1)S(1)}, u32[]{:S(2)}, u32[]{:S(2)}) %collective-permute-start.18) | collective-permute-done | bytes 65568 | tf_op jit(solution)/shard_map/ppermute | solution.py:315
  77.0 3.6 %all-to-all-start = ((bf16[16,32,512]{2,1,0:T(8,128)(2,1)}), bf16[16,32,512]{2,1,0:T(8,128)(2,1)S(1)}, u32[]{:S(2)}, u32[]{:S(2)}) async-start(bf16[16,32,512]{2,1,0:T(8,128)(2,1)} %broadcast_in_dim.27), calls=%async_computation | async-start | bytes 1048576 | tf_op jit(solution)/shard_map/all_to_all | solution.py:395
  82.0 12.3 %all-to-all-done = bf16[16,32,512]{2,1,0:T(8,128)(2,1)S(1)} async-done(((bf16[16,32,512]{2,1,0:T(8,128)(2,1)}), bf16[16,32,512]{2,1,0:T(8,128)(2,1)S(1)}, u32[]{:S(2)}, u32[]{:S(2)}) %all-to-all-start) | async-done | bytes 524320 | tf_op jit(solution)/shard_map/all_to_all | solution.py:395
  95.0 2.1 %copy-done.3 = bf16[384,5120]{1,0:T(8,128)(2,1)S(1)} copy-done((bf16[384,5120]{1,0:T(8,128)(2,1)S(1)}, bf16[384,5120]{1,0:T(8,128)(2,1)}, u32[]{:S(2)}) %copy-start.3) | copy-done | bytes 3932184
  98.7 3.9 %collective-permute-start.19 = (bf16[16,5120]{1,0:T(8,128)(2,1)S(1)}, bf16[16,5120]{1,0:T(8,128)(2,1)S(1)}, u32[]{:S(2)}, u32[]{:S(2)}) collective-permute-start(bf16[16,5120]{1,0:T(8,128)(2,1)S(1)} %constant_dynamic-slice_fusion), channel_id=1, source_target_pairs={{0,1},{1,0},{2,3},{3,2},{4,5},{5,4},{6,7},{7,6},{8,9},{9,8},{10,11... | collective-permute-start | bytes 491528 | tf_op jit(solution)/shard_map/ppermute | solution.py:315
  105.3 3.9 %collective-permute-done.20 = bf16[16,5120]{1,0:T(8,128)(2,1)S(1)} collective-permute-done((bf16[16,5120]{1,0:T(8,128)(2,1)S(1)}, bf16[16,5120]{1,0:T(8,128)(2,1)S(1)}, u32[]{:S(2)}, u32[]{:S(2)}) %collective-permute-start.20) | collective-permute-done | bytes 163872 | tf_op jit(solution)/shard_map/ppermute | solution.py:315
  109.2 3.5 %collective-permute-start.21 = (bf16[16,5120]{1,0:T(8,128)(2,1)S(1)}, bf16[16,5120]{1,0:T(8,128)(2,1)S(1)}, u32[]{:S(2)}, u32[]{:S(2)}) collective-permute-start(bf16[16,5120]{1,0:T(8,128)(2,1)S(1)} %add_convert_fusion), channel_id=1, source_target_pairs={{0,4},{1,5},{2,6},{3,7},{4,0},{5,1},{6,2},{7,3},{8,12},{9,13},{10,... | collective-permute-start | bytes 491528 | tf_op jit(solution)/shard_map/ppermute | solution.py:315
  112.8 3.6 %collective-permute-done.21 = bf16[16,5120]{1,0:T(8,128)(2,1)S(1)} collective-permute-done((bf16[16,5120]{1,0:T(8,128)(2,1)S(1)}, bf16[16,5120]{1,0:T(8,128)(2,1)S(1)}, u32[]{:S(2)}, u32[]{:S(2)}) %collective-permute-start.21) | collective-permute-done | bytes 163872 | tf_op jit(solution)/shard_map/ppermute | solution.py:315
  116.4 1.7 %collective-permute-start.22 = (f32[16,5120]{1,0:T(8,128)S(1)}, f32[16,5120]{1,0:T(8,128)S(1)}, u32[]{:S(2)}, u32[]{:S(2)}) collective-permute-start(f32[16,5120]{1,0:T(8,128)S(1)} %convert_add_fusion.1), channel_id=1, source_target_pairs={{0,1},{1,0},{2,3},{3,2},{4,5},{5,4},{6,7},{7,6},{8,9},{9,8},{10,11... | collective-permute-start | bytes 983048 | tf_op jit(solution)/shard_map/ppermute | solution.py:315
  118.3 1.6 shard_map.133
  121.5 2.1 %copy-done.4 = bf16[384,5120]{1,0:T(8,128)(2,1)S(1)} copy-done((bf16[384,5120]{1,0:T(8,128)(2,1)S(1)}, bf16[384,5120]{1,0:T(8,128)(2,1)}, u32[]{:S(2)}) %copy-start.4) | copy-done | bytes 3932184
  123.6 8.0 %shard_map.134 = (bf16[64,5120]{1,0:T(8,128)(2,1)S(1)}, bf16[64,5120]{1,0:T(8,128)(2,1)S(1)}, bf16[64,5120]{1,0:T(8,128)(2,1)S(1)}, bf16[64,5120]{1,0:T(8,128)(2,1)S(1)}) custom-call(bf16[256,384]{1,0:T(8,128)(2,1)S(1)} %get-tuple-element.20.own, bf16[256,384]{1,0:T(8,128)(2,1)S(1)} %collective-permute-done.8.other, bf16[384,5120]{1,0:T(8,128)(2,1)S(1)} %copy-done.4, ...), custom_call_target="tpu_custom_call" | custom-call | flops 2013265920 | bytes 10485760 | tf_op jit(solution)/shard_map/pallas_call | solution.py:251
  131.6 3.0 %collective-permute-start.12 = (bf16[64,5120]{1,0:T(8,128)(2,1)S(1)}, bf16[64,5120]{1,0:T(8,128)(2,1)S(1)}, u32[]{:S(2)}, u32[]{:S(2)}) collective-permute-start(bf16[64,5120]{1,0:T(8,128)(2,1)S(1)} %get-tuple-element.25), channel_id=1, source_target_pairs={{0,6},{1,7},{2,0},{3,1},{4,2},{5,3},{6,4},{7,5},{8,14},{9,15},{10,... | collective-permute-start | bytes 1966088 | tf_op jit(solution)/shard_map/ppermute | solution.py:312
  137.1 25.5 %collective-permute-done.12 = bf16[64,5120]{1,0:T(8,128)(2,1)S(1)} collective-permute-done((bf16[64,5120]{1,0:T(8,128)(2,1)S(1)}, bf16[64,5120]{1,0:T(8,128)(2,1)S(1)}, u32[]{:S(2)}, u32[]{:S(2)}) %collective-permute-start.12) | collective-permute-done | bytes 655392 | tf_op jit(solution)/shard_map/ppermute | solution.py:312
  162.5 3.2 %collective-permute-done.11 = bf16[64,5120]{1,0:T(8,128)(2,1)S(1)} collective-permute-done((bf16[64,5120]{1,0:T(8,128)(2,1)S(1)}, bf16[64,5120]{1,0:T(8,128)(2,1)S(1)}, u32[]{:S(2)}, u32[]{:S(2)}) %collective-permute-start.11) | collective-permute-done | bytes 655392 | tf_op jit(solution)/shard_map/ppermute | solution.py:312
  (159 shorter events, 41.2 us)
Async XLA Ops:
  3.4 29.9 %collective-permute-start = (bf16[64,5120]{1,0:T(8,128)(2,1)S(1)}, bf16[64,5120]{1,0:T(8,128)(2,1)}, u32[]{:S(2)}, u32[]{:S(2)}) collective-permute-start(bf16[64,5120]{1,0:T(8,128)(2,1)S(1)} %fusion.2.refs_0_), channel_id=1, source_target_pairs={{0,2},{1,3},{2,4},{3,5},{4,6},{5,7},{6,0},{7,1},{8,10},{9,11},{10,... | collective-permute-start | bytes 1966088 | tf_op jit(solution)/shard_map/ppermute | solution.py:312
  5.6 33.5 %collective-permute-start.1 = (bf16[64,5120]{1,0:T(8,128)(2,1)S(1)}, bf16[64,5120]{1,0:T(8,128)(2,1)}, u32[]{:S(2)}, u32[]{:S(2)}) collective-permute-start(bf16[64,5120]{1,0:T(8,128)(2,1)S(1)} %fusion.2.refs_0_), channel_id=1, source_target_pairs={{0,6},{1,7},{2,0},{3,1},{4,2},{5,3},{6,4},{7,5},{8,14},{9,15},{10,... | collective-permute-start | bytes 1966088 | tf_op jit(solution)/shard_map/ppermute | solution.py:312
  7.2 52.6 %collective-permute-start.2 = (bf16[64,5120]{1,0:T(8,128)(2,1)S(1)}, bf16[64,5120]{1,0:T(8,128)(2,1)}, u32[]{:S(2)}, u32[]{:S(2)}) collective-permute-start(bf16[64,5120]{1,0:T(8,128)(2,1)S(1)} %fusion.2.refs_0_), channel_id=1, source_target_pairs={{0,1},{1,0},{2,3},{3,2},{4,5},{5,4},{6,7},{7,6},{8,9},{9,8},{10,11... | collective-permute-start | bytes 1966088 | tf_op jit(solution)/shard_map/ppermute | solution.py:315
  19.1 16.7 %collective-permute-start.13 = (bf16[32,384]{1,0:T(8,128)(2,1)S(1)}, bf16[32,384]{1,0:T(8,128)(2,1)}, u32[]{:S(2)}, u32[]{:S(2)}) collective-permute-start(bf16[32,384]{1,0:T(8,128)(2,1)S(1)} %get-tuple-element.26.q), channel_id=1, source_target_pairs={{0,32},{8,40},{16,48},{24,56},{32,0},{40,8},{48,16},{56,24},{64,96... | collective-permute-start | bytes 73736 | tf_op jit(solution)/shard_map/ppermute | solution.py:315
  35.0 10.5 %collective-permute-start.5 = (bf16[32,5120]{1,0:T(8,128)(2,1)}, bf16[32,5120]{1,0:T(8,128)(2,1)}, u32[]{:S(2)}, u32[]{:S(2)}) collective-permute-start(bf16[32,5120]{1,0:T(8,128)(2,1)} %slice.24), channel_id=1, source_target_pairs={{0,2},{1,3},{2,4},{3,5},{4,6},{5,7},{6,0},{7,1},{8,10},{9,11},{10,... | collective-permute-start | bytes 983048 | tf_op jit(solution)/shard_map/ppermute | solution.py:312
  36.6 14.3 %collective-permute-start.14 = (bf16[64,384]{1,0:T(8,128)(2,1)S(1)}, bf16[64,384]{1,0:T(8,128)(2,1)S(1)}, u32[]{:S(2)}, u32[]{:S(2)}) collective-permute-start(bf16[64,384]{1,0:T(8,128)(2,1)S(1)} %pad_maximum_fusion.7), channel_id=1, source_target_pairs={{0,16},{8,24},{16,0},{24,8},{32,48},{40,56},{48,32},{56,40},{64,80... | collective-permute-start | bytes 147464 | tf_op jit(solution)/shard_map/ppermute | solution.py:315
  39.1 20.6 %copy-start.8 = (f32[384,128]{1,0:T(8,128)S(1)}, f32[384,128]{1,0:T(8,128)}, u32[]{:S(2)}) copy-start(f32[384,128]{1,0:T(8,128)} %get-tuple-element.44.refs_10_) | copy-start | bytes 589828
  40.2 8.9 %collective-permute-start.6 = (bf16[32,5120]{1,0:T(8,128)(2,1)S(1)}, bf16[32,5120]{1,0:T(8,128)(2,1)S(1)}, u32[]{:S(2)}, u32[]{:S(2)}) collective-permute-start(bf16[32,5120]{1,0:T(8,128)(2,1)S(1)} %slice.25), channel_id=1, source_target_pairs={{0,6},{1,7},{2,0},{3,1},{4,2},{5,3},{6,4},{7,5},{8,14},{9,15},{10,... | collective-permute-start | bytes 983048 | tf_op jit(solution)/shard_map/ppermute | solution.py:312
  42.9 16.9 %collective-permute-start.3 = (bf16[64,5120]{1,0:T(8,128)(2,1)}, bf16[64,5120]{1,0:T(8,128)(2,1)S(1)}, u32[]{:S(2)}, u32[]{:S(2)}) collective-permute-start(bf16[64,5120]{1,0:T(8,128)(2,1)} %collective-permute-done.refs_1_), channel_id=1, source_target_pairs={{0,1},{1,0},{2,3},{3,2},{4,5},{5,4},{6,7},{7,6},{8,9},{9,8},{10,11... | collective-permute-start | bytes 1966088 | tf_op jit(solution)/shard_map/ppermute | solution.py:315
  45.5 14.2 %collective-permute-start.4 = (bf16[64,5120]{1,0:T(8,128)(2,1)}, bf16[64,5120]{1,0:T(8,128)(2,1)S(1)}, u32[]{:S(2)}, u32[]{:S(2)}) collective-permute-start(bf16[64,5120]{1,0:T(8,128)(2,1)} %collective-permute-done.1.refs_2_), channel_id=1, source_target_pairs={{0,1},{1,0},{2,3},{3,2},{4,5},{5,4},{6,7},{7,6},{8,9},{9,8},{10,11... | collective-permute-start | bytes 1966088 | tf_op jit(solution)/shard_map/ppermute | solution.py:315
  49.1 19.7 %collective-permute-start.7 = (bf16[64,5120]{1,0:T(8,128)(2,1)S(1)}, bf16[64,5120]{1,0:T(8,128)(2,1)S(1)}, u32[]{:S(2)}, u32[]{:S(2)}) collective-permute-start(bf16[64,5120]{1,0:T(8,128)(2,1)S(1)} %constant_dynamic-update-slice_fusion.refs_0_), channel_id=1, source_target_pairs={{0,1},{1,0},{2,3},{3,2},{4,5},{5,4},{6,7},{7,6},{8,9},{9,8},{10,11... | collective-permute-start | bytes 1966088 | tf_op jit(solution)/shard_map/ppermute | solution.py:315
  51.7 4.5 %collective-permute-start.15 = (bf16[128,384]{1,0:T(8,128)(2,1)S(1)}, bf16[128,384]{1,0:T(8,128)(2,1)S(1)}, u32[]{:S(2)}, u32[]{:S(2)}) collective-permute-start(bf16[128,384]{1,0:T(8,128)(2,1)S(1)} %pad_maximum_fusion.4), channel_id=1, source_target_pairs={{0,8},{8,0},{16,24},{24,16},{32,40},{40,32},{48,56},{56,48},{64,72... | collective-permute-start | bytes 294920 | tf_op jit(solution)/shard_map/ppermute | solution.py:315
  56.9 15.6 %collective-permute-start.16 = (bf16[256,384]{1,0:T(8,128)(2,1)S(1)}, bf16[256,384]{1,0:T(8,128)(2,1)S(1)}, u32[]{:S(2)}, u32[]{:S(2)}) collective-permute-start(bf16[256,384]{1,0:T(8,128)(2,1)S(1)} %pad_maximum_fusion.3), channel_id=1, source_target_pairs={{0,64},{8,72},{16,80},{24,88},{32,96},{40,104},{48,112},{56,120},{... | collective-permute-start | bytes 589832 | tf_op jit(solution)/shard_map/ppermute | solution.py:315
  68.2 5.6 %collective-permute-start.17 = (bf16[384,256]{1,0:T(8,128)(2,1)S(1)}, bf16[384,256]{1,0:T(8,128)(2,1)S(1)}, u32[]{:S(2)}, u32[]{:S(2)}) collective-permute-start(bf16[384,256]{1,0:T(8,128)(2,1)S(1)} %get-tuple-element.18.kv_a), channel_id=1, source_target_pairs={{0,128},{128,0},{1,129},{129,1},{2,130},{130,2},{3,131},{131,3},{4... | collective-permute-start | bytes 589832 | tf_op jit(solution)/shard_map/ppermute | solution.py:315
  71.2 4.2 %collective-permute-start.18 = (bf16[128,256]{1,0:T(8,128)(2,1)S(1)}, bf16[128,256]{1,0:T(8,128)(2,1)S(1)}, u32[]{:S(2)}, u32[]{:S(2)}) collective-permute-start(bf16[128,256]{1,0:T(8,128)(2,1)S(1)} %get-tuple-element.19.kv_b), channel_id=1, source_target_pairs={{0,128},{128,0},{1,129},{129,1},{2,130},{130,2},{3,131},{131,3},{4... | collective-permute-start | bytes 196616 | tf_op jit(solution)/shard_map/ppermute | solution.py:315
  77.0 17.4 %all-to-all-start = ((bf16[16,32,512]{2,1,0:T(8,128)(2,1)}), bf16[16,32,512]{2,1,0:T(8,128)(2,1)S(1)}, u32[]{:S(2)}, u32[]{:S(2)}) async-start(bf16[16,32,512]{2,1,0:T(8,128)(2,1)} %broadcast_in_dim.27), calls=%async_computation | async-start | bytes 1048576 | tf_op jit(solution)/shard_map/all_to_all | solution.py:395
  98.6 19.4 %copy-start.21 = (s32[192]{0:T(256)S(1)}, s32[192]{0:T(256)}, u32[]{:S(2)}) copy-start(s32[192]{0:T(256)} %copy-done.20) | copy-start | bytes 2308
  98.6 19.4 %copy-start.23 = (s32[192]{0:T(256)S(1)}, s32[192]{0:T(256)}, u32[]{:S(2)}) copy-start(s32[192]{0:T(256)} %copy-done.22) | copy-start | bytes 2308
  98.7 19.4 %copy-start.25 = (s32[64]{0:T(128)S(1)}, s32[64]{0:T(128)}, u32[]{:S(2)}) copy-start(s32[64]{0:T(128)} %copy-done.24) | copy-start | bytes 772
  98.7 19.4 %copy-start.27 = (s32[64]{0:T(128)S(1)}, s32[64]{0:T(128)}, u32[]{:S(2)}) copy-start(s32[64]{0:T(128)} %copy-done.26) | copy-start | bytes 772
  98.7 19.6 %copy-start.13 = (bf16[384,384]{1,0:T(8,128)(2,1)S(1)}, bf16[384,384]{1,0:T(8,128)(2,1)}, u32[]{:S(2)}) copy-start(bf16[384,384]{1,0:T(8,128)(2,1)} %copy-done.12) | copy-start | bytes 884740
  98.7 19.6 %copy-start.15 = (bf16[384,256]{1,0:T(8,128)(2,1)S(1)}, bf16[384,256]{1,0:T(8,128)(2,1)}, u32[]{:S(2)}) copy-start(bf16[384,256]{1,0:T(8,128)(2,1)} %copy-done.14) | copy-start | bytes 589828
  98.7 4.9 %collective-permute-start.19 = (bf16[16,5120]{1,0:T(8,128)(2,1)S(1)}, bf16[16,5120]{1,0:T(8,128)(2,1)S(1)}, u32[]{:S(2)}, u32[]{:S(2)}) collective-permute-start(bf16[16,5120]{1,0:T(8,128)(2,1)S(1)} %constant_dynamic-slice_fusion), channel_id=1, source_target_pairs={{0,1},{1,0},{2,3},{3,2},{4,5},{5,4},{6,7},{7,6},{8,9},{9,8},{10,11... | collective-permute-start | bytes 491528 | tf_op jit(solution)/shard_map/ppermute | solution.py:315
  103.7 5.5 %collective-permute-start.20 = (bf16[16,5120]{1,0:T(8,128)(2,1)S(1)}, bf16[16,5120]{1,0:T(8,128)(2,1)S(1)}, u32[]{:S(2)}, u32[]{:S(2)}) collective-permute-start(bf16[16,5120]{1,0:T(8,128)(2,1)S(1)} %add_convert_fusion.1), channel_id=1, source_target_pairs={{0,2},{1,3},{2,0},{3,1},{4,6},{5,7},{6,4},{7,5},{8,10},{9,11},{10,... | collective-permute-start | bytes 491528 | tf_op jit(solution)/shard_map/ppermute | solution.py:315
  104.7 16.8 %collective-permute-start.9 = (bf16[384,5120]{1,0:T(8,128)(2,1)}, bf16[384,5120]{1,0:T(8,128)(2,1)}, u32[]{:S(2)}, u32[]{:S(2)}) collective-permute-start(bf16[384,5120]{1,0:T(8,128)(2,1)} %w.1), channel_id=1, source_target_pairs={{0,1},{1,0},{2,3},{3,2},{4,5},{5,4},{6,7},{7,6},{8,9},{9,8},{10,11... | collective-permute-start | bytes 11796488 | tf_op jit(solution)/shard_map/ppermute | solution.py:315
  109.2 7.1 %collective-permute-start.21 = (bf16[16,5120]{1,0:T(8,128)(2,1)S(1)}, bf16[16,5120]{1,0:T(8,128)(2,1)S(1)}, u32[]{:S(2)}, u32[]{:S(2)}) collective-permute-start(bf16[16,5120]{1,0:T(8,128)(2,1)S(1)} %add_convert_fusion), channel_id=1, source_target_pairs={{0,4},{1,5},{2,6},{3,7},{4,0},{5,1},{6,2},{7,3},{8,12},{9,13},{10,... | collective-permute-start | bytes 491528 | tf_op jit(solution)/shard_map/ppermute | solution.py:315
  116.4 3.7 %collective-permute-start.22 = (f32[16,5120]{1,0:T(8,128)S(1)}, f32[16,5120]{1,0:T(8,128)S(1)}, u32[]{:S(2)}, u32[]{:S(2)}) collective-permute-start(f32[16,5120]{1,0:T(8,128)S(1)} %convert_add_fusion.1), channel_id=1, source_target_pairs={{0,1},{1,0},{2,3},{3,2},{4,5},{5,4},{6,7},{7,6},{8,9},{9,8},{10,11... | collective-permute-start | bytes 983048 | tf_op jit(solution)/shard_map/ppermute | solution.py:315
  119.9 1.5 collective-permute-start.8
  131.6 34.1 %copy-start.16 = (bf16[1,1,64,5120]{3,2,1,0:T(8,128)(2,1)S(1)}, bf16[1,1,64,5120]{3,2,1,0:T(8,128)(2,1)}, u32[]{:S(2)}) copy-start(bf16[1,1,64,5120]{3,2,1,0:T(8,128)(2,1)} %param.12) | copy-start | bytes 1966084
  131.6 30.9 %collective-permute-start.12 = (bf16[64,5120]{1,0:T(8,128)(2,1)S(1)}, bf16[64,5120]{1,0:T(8,128)(2,1)S(1)}, u32[]{:S(2)}, u32[]{:S(2)}) collective-permute-start(bf16[64,5120]{1,0:T(8,128)(2,1)S(1)} %get-tuple-element.25), channel_id=1, source_target_pairs={{0,6},{1,7},{2,0},{3,1},{4,2},{5,3},{6,4},{7,5},{8,14},{9,15},{10,... | collective-permute-start | bytes 1966088 | tf_op jit(solution)/shard_map/ppermute | solution.py:312
  134.6 31.1 %collective-permute-start.11 = (bf16[64,5120]{1,0:T(8,128)(2,1)S(1)}, bf16[64,5120]{1,0:T(8,128)(2,1)S(1)}, u32[]{:S(2)}, u32[]{:S(2)}) collective-permute-start(bf16[64,5120]{1,0:T(8,128)(2,1)S(1)} %get-tuple-element.24), channel_id=1, source_target_pairs={{0,2},{1,3},{2,4},{3,5},{4,6},{5,7},{6,0},{7,1},{8,10},{9,11},{10,... | collective-permute-start | bytes 1966088 | tf_op jit(solution)/shard_map/ppermute | solution.py:312
  134.6 31.1 %collective-permute-start.10 = (bf16[64,5120]{1,0:T(8,128)(2,1)S(1)}, bf16[64,5120]{1,0:T(8,128)(2,1)S(1)}, u32[]{:S(2)}, u32[]{:S(2)}) collective-permute-start(bf16[64,5120]{1,0:T(8,128)(2,1)S(1)} %get-tuple-element.23), channel_id=1, source_target_pairs={{0,4},{1,5},{2,6},{3,7},{4,0},{5,1},{6,2},{7,3},{8,12},{9,13},{10,... | collective-permute-start | bytes 1966088 | tf_op jit(solution)/shard_map/ppermute | solution.py:312
  (24 other events, 168.0 us)

commit v2 on v1

v2 whole, which is shorter than its diff:
```python
import functools

import jax
import jax.numpy as jnp
import numpy as np
from jax import lax
from jax.experimental import pallas as pl
from jax.experimental.pallas import tpu as pltpu
from jax.sharding import PartitionSpec as P

HEAD_WIDTH = 128
EPSILON = 1e-06
ROPE_BASE = 1000000.0
VMEM_LIMIT = 14 * 1024 * 1024
FIRST, SECOND, THIRD, FOURTH = 4, 1, 2, 8
HELD = (0, FIRST, SECOND, FIRST ^ SECOND)
SERVED = (0, THIRD, FOURTH, THIRD ^ FOURTH)


def fixed_tables(start, length):
    spans = np.concatenate([np.arange(HEAD_WIDTH // 2)] * 2)
    angles = np.arange(start, start + length)[:, None] * ROPE_BASE ** (-2.0 * spans / HEAD_WIDTH)
    sign = np.where(np.arange(HEAD_WIDTH) < HEAD_WIDTH // 2, -1.0, 1.0)
    return np.concatenate([np.cos(angles), np.sin(angles) * sign], axis=1).astype(np.float32)


VMEM = pl.BlockSpec(memory_space=pltpu.VMEM)
SMEM = pl.BlockSpec(memory_space=pltpu.SMEM)
ANY = pl.BlockSpec(memory_space=pl.ANY)
HBM = pl.BlockSpec(memory_space=pltpu.HBM)


def simple_call(body, out_shape, flops, *args, specs=None, scratch=()):
    nbytes = sum(a.size * a.dtype.itemsize for a in args)
    return pl.pallas_call(
        body,
        in_specs=specs or [VMEM] * len(args),
        out_specs=jax.tree.map(lambda _: VMEM, out_shape),
        out_shape=out_shape,
        scratch_shapes=list(scratch),
        compiler_params=pltpu.CompilerParams(vmem_limit_bytes=VMEM_LIMIT),
        cost_estimate=pl.CostEstimate(flops=flops, bytes_accessed=nbytes if flops else 0, transcendentals=0),
    )(*args)


def normalized(wide, gain):
    factor = lax.rsqrt(jnp.mean(wide * wide, axis=-1, keepdims=True) + EPSILON)
    return (wide * factor * gain).astype(jnp.bfloat16)


def fetch(sources, targets, sems):
    copies = [
        pltpu.make_async_copy(source, target, sems.at[i])
        for i, (source, target) in enumerate(zip(sources, targets))
    ]
    for copy in copies:
        copy.start()
    return copies


def like(*arrays):
    held = [pltpu.VMEM(a.shape, a.dtype) for a in arrays]
    return held + [pltpu.SemaphoreType.DMA((len(arrays),))]


def norm_body(tp, grp, x_far, gain_far, out, x, gain, sems):
    for copy in fetch((x_far, gain_far), (x, gain), sems):
        copy.wait()
    for i in range(x.shape[0] // 16):
        part = slice(i * 16, (i + 1) * 16)
        out[part] = normalized(x[part].astype(jnp.float32), gain[...])


def row_lengths(lengths, rows):
    samples = lengths.shape[1]
    row = lax.broadcasted_iota(jnp.int32, (rows, samples), 0)
    own = lax.broadcasted_iota(jnp.int32, (rows, samples), 1) == row // 2
    wide = jnp.where(own, lengths[...].astype(jnp.float32), 0.0)
    return jnp.sum(wide, axis=1, keepdims=True).astype(jnp.int32)


def fresh_body(samples, where, *refs):
    count = 5
    far, (out, c_out, s_out, forth, back) = refs[:count], refs[count : 2 * count]
    near, (wide, spots, sems) = refs[2 * count : 3 * count], refs[3 * count :]
    copies = fetch(far, near, sems)
    x, gain, lengths, table, prompts = near
    copies[4].wait()
    route(samples, where[0], prompts, forth, back, spots)
    for copy in copies[:4]:
        copy.wait()
    rows = out.shape[0]
    for i in range(x.shape[0]):
        wide[2 * i : 2 * i + 2] = x[i].astype(jnp.float32)
    for i in range(rows // 16):
        part = slice(i * 16, (i + 1) * 16)
        out[part] = normalized(wide[part], gain[...])
    shape = (rows, table.shape[0])
    row = lax.broadcasted_iota(jnp.int32, shape, 0)
    column = lax.broadcasted_iota(jnp.int32, shape, 1)
    at = (column == row_lengths(lengths, rows) + row % 2).astype(jnp.float32)
    both = jnp.dot(at, table[...], precision=lax.Precision.HIGHEST)
    c_out[...] = both[:, :HEAD_WIDTH]
    s_out[...] = both[:, HEAD_WIDTH:]


def prepare_fresh(grp, x, gain, lengths, table, prompts):
    samples, width = x.shape[0], x.shape[2]
    rows, wide = 2 * samples, 8 * samples
    flat = jax.ShapeDtypeStruct((rows, HEAD_WIDTH), jnp.float32)
    choice = jax.ShapeDtypeStruct((wide, wide), jnp.bfloat16)
    far = (x, gain.reshape(1, -1), lengths, jnp.asarray(table), prompts)
    *held, sems = like(*far)
    return simple_call(
        functools.partial(fresh_body, samples),
        (jax.ShapeDtypeStruct((rows, width), jnp.bfloat16), flat, flat, choice, choice),
        1_000_000, grp, *far,
        specs=[SMEM] + [HBM] * 5,
        scratch=held
        + [
            pltpu.VMEM((rows, width), jnp.float32),
            pltpu.VMEM((2 * prompts.shape[1], wide), jnp.float32),
            sems,
        ],
    )


def norm_prompt(x, gain, tp, grp):
    shape = jax.ShapeDtypeStruct(x.shape, jnp.bfloat16)
    far = (x, gain.reshape(1, -1))
    return simple_call(
        norm_body, shape, 1_000_000, tp, grp, *far,
        specs=[SMEM] * 2 + [HBM] * 2, scratch=like(*far),
    )


def route(samples, grp, prompts, forth, back, spots):
    rows, count = 2 * samples, prompts.shape[1]
    wide = 2 * count
    wide_prompts = prompts[...].astype(jnp.float32)

    def grid(shape, axis):
        return lax.broadcasted_iota(jnp.int32, shape, axis)

    spread = (grid((count, wide), 1) // 2 == grid((count, wide), 0)).astype(jnp.bfloat16)
    across = jnp.dot(
        jnp.broadcast_to(wide_prompts, (8, count)).astype(jnp.bfloat16),
        spread,
        preferred_element_type=jnp.float32,
    )[:1]
    own = grid((wide, count), 1) == grid((wide, count), 0) // 2
    down = jnp.sum(jnp.where(own, wide_prompts, 0.0), axis=1, keepdims=True)
    earlier = (across == down) & (grid((wide, wide), 1) < grid((wide, wide), 0))
    rank = jnp.sum(earlier.astype(jnp.float32), axis=1, keepdims=True)
    spots[...] = jnp.broadcast_to(down * rows + rank, spots.shape)

    def cells(masks):
        parts = [spots[pl.ds(pl.multiple_of((grp ^ m) * rows, rows), rows)] for m in masks]
        return jnp.concatenate(parts, axis=0)

    def names(masks):
        column = grid((1, 4 * rows), 1)
        start = jnp.zeros((1, 4 * rows), jnp.int32)
        for i, m in enumerate(masks):
            start = jnp.where(column // rows == i, (grp ^ m) * rows, start)
        return (start + column % rows).astype(jnp.float32)

    picked = (cells(HELD) == names(SERVED)).astype(jnp.float32)
    forth[...] = picked.T.astype(jnp.bfloat16)
    back[...] = (cells(SERVED) == names(HELD)).astype(jnp.bfloat16)


def hold(values, after):
    count = len(values)
    return pl.pallas_call(
        lambda *refs: None,
        in_specs=[ANY] * (count + len(after)),
        out_specs=[ANY] * count,
        out_shape=[jax.ShapeDtypeStruct(v.shape, v.dtype) for v in values],
        input_output_aliases={i: i for i in range(count)},
        compiler_params=pltpu.CompilerParams(vmem_limit_bytes=VMEM_LIMIT),
        cost_estimate=pl.CostEstimate(flops=0, bytes_accessed=0, transcendentals=0),
    )(*values, *after)


def join_body(a, b, *rest):
    out = rest[-1]
    out[: a.shape[0]] = a[...]
    out[a.shape[0] :] = b[...]


def pick_body(choice, near, far, *rest):
    kept, third, fourth = rest[-3:]
    rows = kept.shape[0]
    held = jnp.concatenate([near[...], far[...]], axis=0)
    picked = jnp.dot(choice[...], held, preferred_element_type=jnp.float32).astype(jnp.bfloat16)
    kept[...] = picked[:rows]
    third[:rows] = picked[rows : 2 * rows]
    third[rows:] = picked[3 * rows :]
    fourth[...] = picked[2 * rows : 3 * rows]


def pass_body(part, came, *rest):
    out = rest[-1]
    rows = part.shape[0]
    out[...] = part[...] + came[rows:]


def exchange_near(value, swap, after):
    shape = jax.ShapeDtypeStruct((2 * value.shape[0], value.shape[1]), value.dtype)
    args = (value, swap(value, "grp", FIRST))
    specs = [VMEM] * 2 + [ANY] * len(after)
    return simple_call(join_body, shape, 0, *args, *after, specs=specs)


def exchange_pick(near, choice, swap, after):
    rows, wide = near.shape[0] // 2, near.shape[1]
    shape = lambda n: jax.ShapeDtypeStruct((n * rows, wide), near.dtype)
    args = (choice, near, swap(near, "grp", SECOND))
    return simple_call(
        pick_body, (shape(1), shape(2), shape(1)), 0, *args, *after,
        specs=[VMEM] * 3 + [ANY] * len(after),
    )


def exchange_pass(third, fourth, swap, after):
    came = swap(third, "grp", THIRD)
    shape = jax.ShapeDtypeStruct(fourth.shape, fourth.dtype)
    specs = [VMEM] * 2 + [ANY] * len(after)
    return came, simple_call(pass_body, shape, 0, fourth, came, *after, specs=specs)


def arrived(kept, came, last):
    return kept[...] + came[: kept.shape[0]] + last[...]


def cut_body(a, b, top, low):
    half = top.shape[0]
    top[...] = a[:half]
    low[...] = b[half:]


def cut(a, b):
    shape = jax.ShapeDtypeStruct((a.shape[0] // 2, a.shape[1]), a.dtype)
    return simple_call(cut_body, (shape, shape), 0, a, b)


TURNS = (0, 0, -1, 1, -1, 1, 2, 2)
FLIPS = (0, 1, 0, 0, 1, 1, 0, 1)


def start_of(tp, chips, block, i):
    chip = lax.rem(tp // 2 + TURNS[i] + chips, chips)
    return (2 * chip + ((tp % 2) ^ FLIPS[i])) * block


def rotate(acc, c, s, q_out, kv_out, base):
    wide = q_out.shape[1]
    for h in range(wide // HEAD_WIDTH + 1):
        v = acc[:, h * HEAD_WIDTH : (h + 1) * HEAD_WIDTH]
        v = (v * c + pltpu.roll(v, HEAD_WIDTH // 2, 1) * s).astype(jnp.bfloat16)
        if h * HEAD_WIDTH == wide:
            kv_out[base:, :HEAD_WIDTH] = v
        else:
            q_out[base:, h * HEAD_WIDTH : (h + 1) * HEAD_WIDTH] = v
    kv_out[base:, HEAD_WIDTH:] = acc[:, wide + HEAD_WIDTH :].astype(jnp.bfloat16)


def chunks(depth):
    count = 5 if depth % 640 == 0 else 1
    return [slice(i * depth // count, (i + 1) * depth // count) for i in range(count)]


def fresh_qkv_body(x, wq, wk, wv, cos, sin, q_out, kv_out, joined, acc, sems):
    copies = []
    for i, part in enumerate(chunks(x.shape[1])):
        at = 0
        for j, w in enumerate((wq, wk, wv)):
            target = joined.at[part, at : at + w.shape[1]]
            at += w.shape[1]
            copies.append(pltpu.make_async_copy(w.at[part], target, sems.at[i, j]))
            copies[-1].start()
    for i, part in enumerate(chunks(x.shape[1])):
        for j in range(3):
            copies[3 * i + j].wait()
        piece = jnp.dot(x[:, part], joined[part], preferred_element_type=jnp.float32)
        acc[...] = piece if i == 0 else acc[...] + piece
    rotate(acc, cos[...], sin[...], q_out, kv_out, 0)


def fresh_qkv(x, weights, tables):
    rows, depth = x.shape
    total = sum(w.shape[1] for w in weights)
    shape = lambda *dims: jax.ShapeDtypeStruct(dims, jnp.bfloat16)
    return simple_call(
        fresh_qkv_body,
        (shape(rows, total - 2 * HEAD_WIDTH), shape(rows, 2 * HEAD_WIDTH), shape(depth, total)),
        2 * rows * depth * total, x, *weights, *tables,
        specs=[VMEM] + [HBM] * 3 + [VMEM] * 2,
        scratch=[
            pltpu.VMEM((rows, total), jnp.float32),
            pltpu.SemaphoreType.DMA((len(chunks(depth)), 3)),
        ],
    )


def qkv_body(n, first, block, early, skip, *refs):
    xs, (w, table, where, *rest) = refs[:n], refs[n:]
    q_out, kv_out, acc = rest[-3:]
    for i, part in enumerate(chunks(w.shape[0])):
        x = jnp.concatenate([r[:, part] for r in xs], axis=0)
        piece = jnp.dot(x, w[part], preferred_element_type=jnp.float32)
        acc[...] = piece if i == 0 else acc[...] + piece
    base = 0
    if early:
        q_early, kv_early = rest[:2]
        base = q_early.shape[0]
        q_out[:base] = q_early[...]
        kv_out[:base] = kv_early[...]
    chips = table.shape[0] // block // 2
    spots = [start_of(where[0], chips, block, first + i) for i in range(acc.shape[0] // block)]
    spots = [pl.ds(pl.multiple_of(spot, block), block) for spot in spots]
    both = jnp.concatenate([table[spot] for spot in spots], axis=0)
    rotate(acc, both[:, :HEAD_WIDTH], both[:, HEAD_WIDTH:], q_out, kv_out, base)


def qkv(blocks, joined, table, where, first, block, early=(), after=()):
    rows, (depth, total) = sum(b.shape[0] for b in blocks), joined.shape
    base = early[0].shape[0] if early else 0
    shape = lambda wide: jax.ShapeDtypeStruct((base + rows, wide), jnp.bfloat16)
    return simple_call(
        functools.partial(qkv_body, len(blocks), first, block, bool(early), len(after)),
        (shape(total - 2 * HEAD_WIDTH), shape(2 * HEAD_WIDTH)),
        2 * rows * depth * total, *blocks, joined, jnp.asarray(table), where, *early, *after,
        specs=[VMEM] * (len(blocks) + 2) + [SMEM] + [VMEM] * len(early) + [ANY] * len(after),
        scratch=[pltpu.VMEM((rows, total), jnp.float32)],
    )


def dot_t(a, b):
    return lax.dot_general(a, b, (((1,), (1,)), ((), ())), preferred_element_type=jnp.float32)


def local_body(scale, q, kv, cache_far, lengths_far, after, out, stats, cache, lengths, sems):
    copies = fetch((cache_far, lengths_far), (cache, lengths), sems)
    for copy in copies:
        copy.wait()
    width, rows = HEAD_WIDTH, q.shape[0]
    groups, samples = q.shape[1] // width, cache.shape[0]
    slots = cache.shape[1]
    query = jnp.concatenate(
        [q[:, g * width : (g + 1) * width] for g in range(groups)], axis=0
    )
    old = cache[...].reshape(samples * slots, 2 * width)
    total = groups * rows
    row = lax.broadcasted_iota(jnp.int32, (total, 1), 0) % rows
    column = lax.broadcasted_iota(jnp.int32, (1, samples * slots), 1)
    score_old = dot_t(query, old[:, :width]) * scale
    limit = row // 2 * slots + jnp.concatenate([row_lengths(lengths, rows)] * groups, axis=0)
    allowed = (column >= row // 2 * slots) & (column < limit)
    score_old = jnp.where(allowed, score_old, -jnp.inf)
    fresh = lax.broadcasted_iota(jnp.int32, (1, rows), 1)
    score_new = dot_t(query, kv[:, :width]) * scale
    score_new = jnp.where((fresh // 2 == row // 2) & (fresh <= row), score_new, -jnp.inf)
    peak = jnp.maximum(
        jnp.max(score_old, axis=1, keepdims=True), jnp.max(score_new, axis=1, keepdims=True)
    )
    expo_old, expo_new = jnp.exp(score_old - peak), jnp.exp(score_new - peak)
    both = jnp.sum(expo_old, axis=1, keepdims=True) + jnp.sum(expo_new, axis=1, keepdims=True)
    mixed = jnp.dot(
        expo_old.astype(jnp.bfloat16), old[:, width:], preferred_element_type=jnp.float32
    ) + jnp.dot(
        expo_new.astype(jnp.bfloat16), kv[:, width:], preferred_element_type=jnp.float32
    )
    out[...] = mixed
    lane = lax.broadcasted_iota(jnp.int32, stats.shape, 1)
    stats[...] = jnp.where(lane == 0, peak, both)


def local_attention(q, kv, cache, lengths, scale, after):
    total = q.shape[1] // HEAD_WIDTH * q.shape[0]
    shape = jax.ShapeDtypeStruct((total, HEAD_WIDTH), jnp.float32)
    flops = 4 * total * cache.shape[0] * cache.shape[1] * HEAD_WIDTH
    return simple_call(
        functools.partial(local_body, scale), (shape, shape), flops,
        q, kv, cache, lengths, after,
        specs=[VMEM] * 2 + [HBM] * 2 + [ANY], scratch=like(cache, lengths),
    )


def prefix_body(scale, kept, came, last, kv_a, kv_b, after, out):
    width, rows = HEAD_WIDTH, kept.shape[0]
    groups = kept.shape[1] // width
    picked = arrived(kept, came, last)
    query = jnp.concatenate([picked[:, g * width : (g + 1) * width] for g in range(groups)], axis=0)
    pairs = jnp.concatenate([kv_a[...], kv_b[...]], axis=0)
    score = dot_t(query, pairs[:, :width]) * scale
    peak = jnp.max(score, axis=1, keepdims=True)
    expo = jnp.exp(score - peak)
    both = jnp.sum(expo, axis=1, keepdims=True)
    mixed = jnp.dot(expo.astype(jnp.bfloat16), pairs[:, width:], preferred_element_type=jnp.float32)
    mixed = (mixed / both).astype(jnp.bfloat16)
    level = peak + jnp.log(both)
    lane = lax.broadcasted_iota(jnp.int32, (rows, width), 1)
    tail = jnp.zeros((rows, width), jnp.bfloat16)
    for g in range(groups):
        out[:, g * width : (g + 1) * width] = mixed[g * rows : (g + 1) * rows]
        rest = level[g * rows : (g + 1) * rows]
        for part in range(3):
            high = rest.astype(jnp.bfloat16)
            rest = rest - high.astype(jnp.float32)
            tail = jnp.where(lane == g * 3 + part, high, tail)
    out[:, groups * width :] = tail


def prefix_attention(asked, kv_a, kv_b, scale, after):
    rows, wide = asked[0].shape
    shape = jax.ShapeDtypeStruct((rows, wide + HEAD_WIDTH), jnp.bfloat16)
    return simple_call(
        functools.partial(prefix_body, scale), shape, 100_000_000, *asked, kv_a, kv_b, after,
        specs=[VMEM] * 5 + [ANY],
    )


def merge_body(kept, came, last, local, stats, *rest):
    out = rest[-1]
    width, rows = HEAD_WIDTH, kept.shape[0]
    groups = local.shape[0] // rows
    picked = arrived(kept, came, last).astype(jnp.float32)
    tail = picked[:, groups * width :]
    for g in range(groups):
        level = tail[:, g * 3 : g * 3 + 1] + tail[:, g * 3 + 1 : g * 3 + 2]
        level = level + tail[:, g * 3 + 2 : g * 3 + 3]
        peak = stats[g * rows : (g + 1) * rows, 0:1]
        both = stats[g * rows : (g + 1) * rows, 1:2]
        top = jnp.maximum(level, peak)
        factor_pre, factor_loc = jnp.exp(level - top), jnp.exp(peak - top)
        total = factor_pre + both * factor_loc
        mixed = picked[:, g * width : (g + 1) * width] * factor_pre
        mixed = mixed + local[g * rows : (g + 1) * rows] * factor_loc
        out[:, g * width : (g + 1) * width] = (mixed / total).astype(jnp.bfloat16)


def merge(back, local, stats, after):
    rows, wide = back[0].shape
    shape = jax.ShapeDtypeStruct((rows, wide - HEAD_WIDTH), jnp.bfloat16)
    return simple_call(
        merge_body, shape, 0, *back, local, stats, *after,
        specs=[VMEM] * 5 + [ANY] * len(after),
    )


def prefill_body(scale, q_a, q_b, kv_a, kv_b, where, *rest):
    own, other = rest[-2:]
    width = HEAD_WIDTH
    groups = q_a.shape[1] // width
    block = own.shape[0] // 4
    pairs = jnp.concatenate([kv_a[...], kv_b[...]], axis=0)
    length = pairs.shape[0]

    def places(shape, axis):
        spot = lax.broadcasted_iota(jnp.int32, shape, axis)
        shift = jnp.zeros(shape, jnp.int32)
        count = length // block
        for i in range(count):
            start = start_of(where[0], count // 2, block, i)
            shift = jnp.where(spot // block == i, start - i * block, shift)
        return spot + shift

    allowed = places((length, 1), 0) >= places((1, length), 1)
    for g in range(groups):
        cols = slice(g * width, (g + 1) * width)
        query = jnp.concatenate([q_a[:, cols], q_b[:, cols]], axis=0)
        score = jnp.where(allowed, dot_t(query, pairs[:, :width]) * scale, -jnp.inf)
        expo = jnp.exp(score - jnp.max(score, axis=1, keepdims=True))
        both = jnp.sum(expo, axis=1, keepdims=True)
        mixed = jnp.dot(
            expo.astype(jnp.bfloat16), pairs[:, width:], preferred_element_type=jnp.float32
        )
        mixed = (mixed / both).astype(jnp.bfloat16)
        part = lambda i, n: mixed[i * block : (i + n) * block]
        for out, at in ((own, (0, 2, 6)), (other, (1, 4, 7))):
            out[:block, cols] = part(at[0], 1)
            out[block : 3 * block, cols] = part(at[1], 2)
            out[3 * block :, cols] = part(at[2], 1)


def prefill_attention(q_a, q_b, kv_a, kv_b, where, scale, after):
    length = q_a.shape[0] + q_b.shape[0]
    shape = jax.ShapeDtypeStruct((length // 2, q_a.shape[1]), jnp.bfloat16)
    return simple_call(
        functools.partial(prefill_body, scale),
        (shape, shape),
        4 * length * length * q_a.shape[1],
        q_a, q_b, kv_a, kv_b, where, *after,
        specs=[VMEM] * 4 + [SMEM] + [ANY] * len(after),
    )


def strips(wide):
    tile = 1024 if wide % 1024 == 0 else wide
    return [slice(i * tile, (i + 1) * tile) for i in range(wide // tile)]


def out_body(own, other, w_own, w_other, after, *outs):
    heads = jnp.concatenate([own[...], other[...]], axis=1)
    for part in strips(w_own.shape[1]):
        w = jnp.concatenate([w_own[:, part], w_other[:, part]], axis=0)
        rows = jnp.dot(heads, w, preferred_element_type=jnp.float32)
        base = 0
        for out in outs:
            out[:, part] = rows[base : base + out.shape[0]].astype(out.dtype)
            base += out.shape[0]


def out_projection(own, other, w_own, w_other, blocks, dtype, after):
    shapes = tuple(jax.ShapeDtypeStruct((b, w_own.shape[1]), dtype) for b in blocks)
    return simple_call(
        out_body, shapes, 0, own, other, w_own, w_other, after, specs=[VMEM] * 4 + [ANY]
    )


def partial_body(tp, heads, w, kept, given):
    core = tp[0] % 2
    rows = kept.shape[0]
    for columns in strips(w.shape[1]):
        part = jnp.dot(heads[...], w[:, columns], preferred_element_type=jnp.float32)
        low, high = part[:rows], part[rows:]
        kept[:, columns] = jnp.where(core == 0, low, high).astype(kept.dtype)
        given[:, columns] = jnp.where(core == 0, high, low).astype(given.dtype)


def partial_projection(tp, heads, w):
    shape = jax.ShapeDtypeStruct((heads.shape[0] // 2, w.shape[1]), jnp.bfloat16)
    return simple_call(
        partial_body, (shape, shape), 0, tp, heads, w, specs=[SMEM, VMEM, VMEM]
    )


def add_body(a, b, *rest):
    out = rest[-1]
    out[...] = (a[...].astype(jnp.float32) + b[...].astype(jnp.float32)).astype(out.dtype)


def add(a, b, dtype, after=()):
    shape = jax.ShapeDtypeStruct(a.shape, dtype)
    specs = [VMEM] * 2 + [ANY] * len(after)
    return simple_call(add_body, shape, 0, a, b, *after, specs=specs)


def add_half_body(first, whole, part, *rest):
    out = rest[-1]
    half = part.shape[0]
    for i in range(2):
        rows = slice(i * half, (i + 1) * half)
        if i == first:
            wide = whole[rows].astype(jnp.float32) + part[...].astype(jnp.float32)
            out[rows] = wide.astype(out.dtype)
        else:
            out[rows] = whole[rows]


def add_half(first, whole, part, after):
    shape = jax.ShapeDtypeStruct(whole.shape, whole.dtype)
    specs = [VMEM] * 2 + [ANY] * len(after)
    body = functools.partial(add_half_body, first)
    return simple_call(body, shape, 0, whole, part, *after, specs=specs)


def total_body(a, b, c, d, out, token):
    token[...] = jnp.zeros(token.shape, token.dtype)
    wide = a[...].astype(jnp.float32) + b[...].astype(jnp.float32)
    wide = wide + (c[...].astype(jnp.float32) + d[...].astype(jnp.float32))
    out[...] = wide.astype(out.dtype)


def finish_body(tp, kept, taken, tokens, out):
    core = tp[0] % 2
    for i in range(out.shape[0]):
        row = 2 * i % kept.shape[0]
        first = i < out.shape[0] // 2
        held, sent = kept[row : row + 2], taken[row : row + 2]
        total = jnp.where(core == 0, held if first else sent, sent if first else held)
        out[i] = tokens[i].astype(jnp.float32) + total


def finish(tp, kept, taken, tokens):
    shape = jax.ShapeDtypeStruct(tokens.shape, jnp.float32)
    return simple_call(
        finish_body, shape, 0, tp, kept, taken, tokens,
        specs=[SMEM] + [VMEM] * 3,
    )


def shards(
    prompt_states,
    new_states,
    answer_cache,
    attn_gain,
    w_query,
    key_weight,
    value_weight,
    w_out,
    prompt_of,
    suffix_len,
):
    scale = HEAD_WIDTH ** (-0.5)
    rows = prompt_states[0, 0]
    block, width = rows.shape
    tp, grp = lax.axis_index("tp").reshape(1), lax.axis_index("grp").reshape(1)
    tp_size = lax.axis_size("tp")

    def around(value, by):
        return lax.ppermute(value, "tp", [(i, (i + 2 * by) % tp_size) for i in range(tp_size)])

    def swap(value, axis, mask):
        return lax.ppermute(value, axis, [(i, i ^ mask) for i in range(lax.axis_size(axis))])

    weights = (w_query, key_weight, value_weight)
    half = block // 2

    normed = norm_prompt(rows, attn_gain, tp, grp)
    from_down = around(normed, 1)
    from_up = around(normed, -1)
    mate_own = swap(normed, "tp", 1)

    samples, slots = new_states.shape[1], answer_cache.shape[2]
    length = block * tp_size
    fresh_normed, *fresh_tables, forth, home = prepare_fresh(
        grp, new_states[0], attn_gain, suffix_len, fixed_tables(length, slots + 8), prompt_of
    )
    fresh_q, fresh_kv, weights = fresh_qkv(fresh_normed, weights, fresh_tables)
    w_mate = swap(w_out, "tp", 1)

    where = tp
    tables = fixed_tables(0, length)
    asked = exchange_near(fresh_q, swap, ())
    from_down, from_up = hold((from_down, from_up), (asked,))
    down_top, up_low = cut(from_down, from_up)
    ahead = around(down_top, 1)
    behind = around(up_low, -1)
    near = [from_down, from_up, swap(from_down, "tp", 1), swap(from_up, "tp", 1)]
    early = qkv([normed, mate_own], weights, tables, where, 0, block)
    kept, third, fourth = exchange_pick(asked, forth, swap, (ahead, behind))
    q_a, kv_a = qkv(near, weights, tables, where, 2, block, early)
    handed_a = swap(kv_a, "role", 1)
    far = [ahead, behind, swap(ahead, "tp", 1), swap(behind, "tp", 1)]
    q_b, kv_b = qkv(far, weights, tables, where, 6, block, after=(kept,))
    handed_b = swap(kv_b, "role", 1)
    came, fourth = exchange_pass(third, fourth, swap, (kv_a,))

    heads_own, heads_other = prefill_attention(q_a, q_b, kv_a, kv_b, where, scale, (fourth,))
    heads_mate = swap(heads_other, "tp", 1)

    asked = (kept, came, swap(fourth, "grp", FOURTH))
    answered = prefix_attention(asked, handed_a, handed_b, scale, heads_own)

    sizes = (block, block, block, half, half)
    to_own, to_down, to_up, far_top, far_low = out_projection(
        heads_own, heads_mate, w_out, w_mate, sizes, jnp.bfloat16, answered
    )
    via_up = around(far_top, 1)
    via_down = around(far_low, -1)

    back = exchange_near(answered, swap, ())
    local, stats = local_attention(fresh_q, fresh_kv, answer_cache[0], suffix_len, scale, back)
    kept, third, fourth = exchange_pick(back, home, swap, (local,))
    came, fourth = exchange_pass(third, fourth, swap, ())
    up = add_half(0, to_up, via_up, (fourth,))
    down = add_half(1, to_down, via_down, (fourth,))
    back = (kept, came, swap(fourth, "grp", FOURTH))
    sum_up = around(up, 1)
    sum_down = around(down, -1)
    prefill_out, token = simple_call(
        total_body,
        (jax.ShapeDtypeStruct(rows.shape, rows.dtype), jax.ShapeDtypeStruct((8, 128), jnp.float32)),
        0, rows, to_own, sum_up, sum_down,
    )

    decoded = merge(back, local, stats, (up, down))
    kept, given = partial_projection(tp, decoded, w_out)
    level = add(kept, swap(given, "tp", 1), jnp.bfloat16)
    level = add(level, swap(level, "tp", 2), jnp.bfloat16)
    summed = add(level, swap(level, "tp", 4), jnp.float32, (token,))
    decode_out = finish(tp, summed, swap(summed, "tp", 1), new_states[0])
    return prefill_out[None, None], decode_out[None]


def solution(mesh):
    placed = (
        P("role", "grp", "tp", None),
        P("role", "grp", None, None),
        P("role", "grp", None, "tp"),
        P(),
        P(None, "tp"),
        P(None, "tp"),
        P(None, "tp"),
        P("tp", None),
        P("role", None),
        P("role", "grp"),
    )
    return jax.shard_map(
        shards,
        mesh=mesh,
        in_specs=placed,
        out_specs=(P("role", "grp", "tp", None), P("role", "grp", None, None)),
        check_vma=False,
    )
```

time: 168 us -> 116 us (0.69)
  waiting for transfers between devices: 60 us -> 31.7 us
  other arithmetic: 19.2 us -> 0 us
  local copies, waits for them, and re-layouts: 18.5 us -> 9.8 us
  starting transfers between devices: 44.2 us -> 52.2 us
  Pallas kernels: 23.9 us -> 20.8 us
    ppermute x7 -> x8, waiting for transfers between devices: 31.7 us -> 6.19 us  [around(): lax.ppermute(value, 'tp', [(i, (i + 2 * by) % tp_size) for i in range(tp_...]
    all_to_all x1 -> x0, waiting for transfers between devices: 12.3 us -> none  [shards(): back = lax.all_to_all(spread, 'grp', 0, 0, tiled=False)]
    ppermute x16 -> x21, starting transfers between devices: 29.6 us -> 41 us  [swap(): lax.ppermute(value, axis, [(i, i ^ mask) for i in range(lax.axis_size(axi...]
    ppermute x16 -> x21, waiting for transfers between devices: 16 us -> 25.5 us  [swap(): lax.ppermute(value, axis, [(i, i ^ mask) for i in range(lax.axis_size(axi...]
    concatenate x9 -> x0, other arithmetic: 7.72 us -> none  [the longest x3 3.76 us: rope_tables(): jnp.concatenate([cosine, cosine], 1)]
    all_to_all x1 -> x0, starting transfers between devices: 3.59 us -> none  [shards(): back = lax.all_to_all(spread, 'grp', 0, 0, tiled=False)]
    pallas_call x9 -> x27, Pallas kernels: 23.9 us -> 20.8 us  [the longest x26 20.7 us: simple_call(): pl.pallas_call(body, in_specs=specs or [VMEM] * len(args), out_specs=jax....]
    reduce_sum x4 -> x0, other arithmetic: 3.01 us -> none  [the longest x2 2.72 us: normalize(): factor = lax.rsqrt(jnp.mean(wide * wide, axis=-1, keepdims=True) + EPSILON)]
  transfers between devices with their start and end apart: 24 -> 29, of which waited for: 12 -> 12; matrix products, arithmetic and copies ran while one was open for 15% -> 0% of each run, Pallas kernels for 8% -> 13%
where the time goes in v2:
time: 116 us; the launch traced here: 115 us
  starting transfers between devices  52.2 us (45%)
  waiting for transfers between devices  31.7 us (27%)
  Pallas kernels  20.8 us (18%)
  local copies, waits for them, and re-layouts  9.8 us (8%)
    ppermute x21, starting transfers between devices, swap(): lax.ppermute(value, axis, [(i, i ^ mask) for i in range(lax.axis_size(axi...  41 us
    ppermute x21, waiting for transfers between devices, swap(): lax.ppermute(value, axis, [(i, i ^ mask) for i in range(lax.axis_size(axi...  25.5 us
    pallas_call x26, Pallas kernels, simple_call(): pl.pallas_call(body, in_specs=specs or [VMEM] * len(args), out_specs=jax....  20.7 us
    ppermute x8, starting transfers between devices, around(): lax.ppermute(value, 'tp', [(i, (i + 2 * by) % tp_size) for i in range(tp_...  11.2 us
    unnamed x30, local copies, waits for them, and re-layouts  9.8 us
    ppermute x8, waiting for transfers between devices, around(): lax.ppermute(value, 'tp', [(i, (i + 2 * by) % tp_size) for i in range(tp_...  6.19 us
  transfers between devices with their start and end apart: 29, of which 12 were waited for; matrix products, arithmetic and copies ran while one was open for 0% of the time, Pallas kernels for 13%

profile of v2, /device:TPU:1, one launch (start us, length us, event | category | flops | bytes accessed | tf_op | source)
XLA Modules:
  0.0 115.4 jit_solution(9238728508935799148)
XLA Ops:
  0.6 3.3 %collective-permute-start.13 = (bf16[384,5120]{1,0:T(8,128)(2,1)}, bf16[384,5120]{1,0:T(8,128)(2,1)}, u32[]{:S(2)}, u32[]{:S(2)}) collective-permute-start(bf16[384,5120]{1,0:T(8,128)(2,1)} %w.1), channel_id=1, source_target_pairs={{0,1},{1,0},{2,3},{3,2},{4,5},{5,4},{6,7},{7,6},{8,9},{9,8},{10,11... | collective-permute-start | bytes 11796488 | tf_op jit(solution)/shard_map/ppermute | solution.py:617
  6.5 2.7 %collective-permute-start.1 = (bf16[64,5120]{1,0:T(8,128)(2,1)S(1)}, bf16[64,5120]{1,0:T(8,128)(2,1)S(1)}, u32[]{:S(2)}, u32[]{:S(2)}) collective-permute-start(bf16[64,5120]{1,0:T(8,128)(2,1)S(1)} %shard_map.131.refs_0_), channel_id=1, source_target_pairs={{0,6},{1,7},{2,0},{3,1},{4,2},{5,3},{6,4},{7,5},{8,14},{9,15},{10,... | collective-permute-start | bytes 1966088 | tf_op jit(solution)/shard_map/ppermute | solution.py:614
  14.1 2.1 %copy-done.2 = bf16[5120,384]{1,0:T(8,128)(2,1)S(1)} copy-done((bf16[5120,384]{1,0:T(8,128)(2,1)S(1)}, bf16[5120,384]{1,0:T(8,128)(2,1)}, u32[]{:S(2)}) %copy-start.2) | copy-done | bytes 3932184
  16.2 1.3 %copy-done.5 = bf16[5120,128]{1,0:T(8,128)(2,1)S(1)} copy-done((bf16[5120,128]{1,0:T(8,128)(2,1)S(1)}, bf16[5120,128]{1,0:T(8,128)(2,1)}, u32[]{:S(2)}) %copy-start.5) | copy-done | bytes 1310744
  17.6 1.3 %copy-done.6 = bf16[5120,128]{1,0:T(8,128)(2,1)S(1)} copy-done((bf16[5120,128]{1,0:T(8,128)(2,1)S(1)}, bf16[5120,128]{1,0:T(8,128)(2,1)}, u32[]{:S(2)}) %copy-start.6) | copy-done | bytes 1310744
  18.9 2.7 %shard_map.133 = (bf16[32,384]{1,0:T(8,128)(2,1)S(1)}, bf16[32,256]{1,0:T(8,128)(2,1)S(1)}, bf16[5120,640]{1,0:T(8,128)(2,1)S(1)}) custom-call(bf16[32,5120]{1,0:T(8,128)(2,1)S(1)} %get-tuple-element.39.x, bf16[5120,384]{1,0:T(8,128)(2,1)S(1)} %copy-done.2, bf16[5120,128]{1,0:T(8,128)(2,1)S(1)} %copy-done.5, bf16[5120,128]{1,0:T(8,128)(2,1)S(1)} %copy-done.6, ...), custom_call_target="tpu_custom_call" | custom-call | flops 209715200 | bytes 6914048 | tf_op jit(solution)/shard_map/pallas_call | solution.py:35
  21.6 5.3 %collective-permute-start.2 = (bf16[32,384]{1,0:T(8,128)(2,1)S(1)}, bf16[32,384]{1,0:T(8,128)(2,1)S(1)}, u32[]{:S(2)}, u32[]{:S(2)}) collective-permute-start(bf16[32,384]{1,0:T(8,128)(2,1)S(1)} %get-tuple-element.42.a.q), channel_id=1, source_target_pairs={{0,32},{8,40},{16,48},{24,56},{32,0},{40,8},{48,16},{56,24},{64,96... | collective-permute-start | bytes 73736 | tf_op jit(solution)/shard_map/ppermute | solution.py:617
  26.9 1.4 %collective-permute-done.2.b = bf16[32,384]{1,0:T(8,128)(2,1)S(1)} collective-permute-done((bf16[32,384]{1,0:T(8,128)(2,1)S(1)}, bf16[32,384]{1,0:T(8,128)(2,1)S(1)}, u32[]{:S(2)}, u32[]{:S(2)}) %collective-permute-start.2) | collective-permute-done | bytes 24608 | tf_op jit(solution)/shard_map/ppermute | solution.py:617
  30.1 2.5 %collective-permute-done.10.far = bf16[64,384]{1,0:T(8,128)(2,1)S(1)} collective-permute-done((bf16[64,384]{1,0:T(8,128)(2,1)S(1)}, bf16[64,384]{1,0:T(8,128)(2,1)S(1)}, u32[]{:S(2)}, u32[]{:S(2)}) %collective-permute-start.10) | collective-permute-done | bytes 49184 | tf_op jit(solution)/shard_map/ppermute | solution.py:617
  32.6 2.7 %collective-permute-start.7 = (bf16[32,5120]{1,0:T(8,128)(2,1)S(1)}, bf16[32,5120]{1,0:T(8,128)(2,1)S(1)}, u32[]{:S(2)}, u32[]{:S(2)}) collective-permute-start(bf16[32,5120]{1,0:T(8,128)(2,1)S(1)} %get-tuple-element.50), channel_id=1, source_target_pairs={{0,6},{1,7},{2,0},{3,1},{4,2},{5,3},{6,4},{7,5},{8,14},{9,15},{10,... | collective-permute-start | bytes 983048 | tf_op jit(solution)/shard_map/ppermute | solution.py:614
  35.3 6.2 %collective-permute-done.6.rest_0_.refs_0_ = bf16[32,5120]{1,0:T(8,128)(2,1)S(1)} collective-permute-done((bf16[32,5120]{1,0:T(8,128)(2,1)S(1)}, bf16[32,5120]{1,0:T(8,128)(2,1)S(1)}, u32[]{:S(2)}, u32[]{:S(2)}) %collective-permute-start.6) | collective-permute-done | bytes 327712 | tf_op jit(solution)/shard_map/ppermute | solution.py:614
  41.5 2.5 %collective-permute-start.8 = (bf16[32,5120]{1,0:T(8,128)(2,1)S(1)}, bf16[32,5120]{1,0:T(8,128)(2,1)S(1)}, u32[]{:S(2)}, u32[]{:S(2)}) collective-permute-start(bf16[32,5120]{1,0:T(8,128)(2,1)S(1)} %collective-permute-done.6.rest_0_.refs_0_), channel_id=1, source_target_pairs={{0,1},{1,0},{2,3},{3,2},{4,5},{5,4},{6,7},{7,6},{8,9},{9,8},{10,11... | collective-permute-start | bytes 983048 | tf_op jit(solution)/shard_map/ppermute | solution.py:617
  45.4 1.8 %collective-permute-start.11 = (bf16[64,384]{1,0:T(8,128)(2,1)S(1)}, bf16[64,384]{1,0:T(8,128)(2,1)S(1)}, u32[]{:S(2)}, u32[]{:S(2)}) collective-permute-start(bf16[64,384]{1,0:T(8,128)(2,1)S(1)} %get-tuple-element.57), channel_id=1, source_target_pairs={{0,16},{8,24},{16,0},{24,8},{32,48},{40,56},{48,32},{56,40},{64,80... | collective-permute-start | bytes 147464 | tf_op jit(solution)/shard_map/ppermute | solution.py:617
  47.2 2.2 %shard_map.137 = (bf16[384,384]{1,0:T(8,128)(2,1)S(1)}, bf16[384,256]{1,0:T(8,128)(2,1)S(1)}) custom-call(bf16[64,5120]{1,0:T(8,128)(2,1)S(1)} %get-tuple-element.43.refs_0_.a, bf16[64,5120]{1,0:T(8,128)(2,1)S(1)} %get-tuple-element.44.refs_1_.b, bf16[64,5120]{1,0:T(8,128)(2,1)S(1)} %collective-permute-done.3.refs_2_, ...), custom_call_target="tpu_custom_call" | custom-call | flops 1677721600 | bytes 9863172 | tf_op jit(solution)/shard_map/pallas_call | solution.py:35
  49.4 1.6 %collective-permute-start.15 = (bf16[384,256]{1,0:T(8,128)(2,1)S(1)}, bf16[384,256]{1,0:T(8,128)(2,1)S(1)}, u32[]{:S(2)}, u32[]{:S(2)}) collective-permute-start(bf16[384,256]{1,0:T(8,128)(2,1)S(1)} %get-tuple-element.54.rest_0_.kv_a), channel_id=1, source_target_pairs={{0,128},{128,0},{1,129},{129,1},{2,130},{130,2},{3,131},{131,3},{4... | collective-permute-start | bytes 589832 | tf_op jit(solution)/shard_map/ppermute | solution.py:617
  52.4 1.5 %shard_map.142 = (bf16[256,384]{1,0:T(8,128)(2,1)S(1)}, bf16[256,384]{1,0:T(8,128)(2,1)S(1)}) custom-call(bf16[384,384]{1,0:T(8,128)(2,1)S(1)} %get-tuple-element.48.q_a, bf16[128,384]{1,0:T(8,128)(2,1)S(1)} %get-tuple-element.53.q_b, bf16[384,256]{1,0:T(8,128)(2,1)S(1)} %get-tuple-element.54.rest_0_.kv_a, bf16[128,256]{1,0:T(8,128)(2,1)S(1)} %get-tuple-element.55.kv_b, ...), custom_call_target="tpu_custom_call" | custom-call | flops 402653184 | bytes 679940 | tf_op jit(solution)/shard_map/pallas_call | solution.py:35
  55.7 2.5 %collective-permute-start.14 = (bf16[32,384]{1,0:T(8,128)(2,1)S(1)}, bf16[32,384]{1,0:T(8,128)(2,1)S(1)}, u32[]{:S(2)}, u32[]{:S(2)}) collective-permute-start(bf16[32,384]{1,0:T(8,128)(2,1)S(1)} %shard_map.141.rest_0_), channel_id=1, source_target_pairs={{0,64},{8,72},{16,80},{24,88},{32,96},{40,104},{48,112},{56,120},{... | collective-permute-start | bytes 73736 | tf_op jit(solution)/shard_map/ppermute | solution.py:617
  58.1 2.4 %collective-permute-done.14.last = bf16[32,384]{1,0:T(8,128)(2,1)S(1)} collective-permute-done((bf16[32,384]{1,0:T(8,128)(2,1)S(1)}, bf16[32,384]{1,0:T(8,128)(2,1)S(1)}, u32[]{:S(2)}, u32[]{:S(2)}) %collective-permute-start.14) | collective-permute-done | bytes 24608 | tf_op jit(solution)/shard_map/ppermute | solution.py:617
  61.0 4.5 %shard_map.144 = (bf16[64,5120]{1,0:T(8,128)(2,1)S(1)}, bf16[64,5120]{1,0:T(8,128)(2,1)S(1)}, bf16[64,5120]{1,0:T(8,128)(2,1)S(1)}, bf16[32,5120]{1,0:T(8,128)(2,1)S(1)}, bf16[32,5120]{1,0:T(8,128)(2,1)S(1)}) custom-call(bf16[256,384]{1,0:T(8,128)(2,1)S(1)} %get-tuple-element.58.after.own, bf16[256,384]{1,0:T(8,128)(2,1)S(1)} %collective-permute-done.12.other, ...), custom_call_target="tpu_custom_call" | custom-call | tf_op jit(solution)/shard_map/pallas_call | solution.py:35
  65.6 2.6 %collective-permute-start.22 = (bf16[32,5120]{1,0:T(8,128)(2,1)S(1)}, bf16[32,5120]{1,0:T(8,128)(2,1)S(1)}, u32[]{:S(2)}, u32[]{:S(2)}) collective-permute-start(bf16[32,5120]{1,0:T(8,128)(2,1)S(1)} %get-tuple-element.69), channel_id=1, source_target_pairs={{0,6},{1,7},{2,0},{3,1},{4,2},{5,3},{6,4},{7,5},{8,14},{9,15},{10,... | collective-permute-start | bytes 983048 | tf_op jit(solution)/shard_map/ppermute | solution.py:614
  68.3 5.5 %collective-permute-start.18 = (bf16[32,512]{1,0:T(8,128)(2,1)S(1)}, bf16[32,512]{1,0:T(8,128)(2,1)S(1)}, u32[]{:S(2)}, u32[]{:S(2)}) collective-permute-start(bf16[32,512]{1,0:T(8,128)(2,1)S(1)} %shard_map.143.after.a), channel_id=1, source_target_pairs={{0,32},{8,40},{16,48},{24,56},{32,0},{40,8},{48,16},{56,24},{64,96... | collective-permute-start | bytes 98312 | tf_op jit(solution)/shard_map/ppermute | solution.py:617
  73.8 1.3 %collective-permute-done.18.b = bf16[32,512]{1,0:T(8,128)(2,1)S(1)} collective-permute-done((bf16[32,512]{1,0:T(8,128)(2,1)S(1)}, bf16[32,512]{1,0:T(8,128)(2,1)S(1)}, u32[]{:S(2)}, u32[]{:S(2)}) %collective-permute-start.18) | collective-permute-done | bytes 32800 | tf_op jit(solution)/shard_map/ppermute | solution.py:617
  76.9 1.3 %collective-permute-done.19.far = bf16[64,512]{1,0:T(8,128)(2,1)S(1)} collective-permute-done((bf16[64,512]{1,0:T(8,128)(2,1)S(1)}, bf16[64,512]{1,0:T(8,128)(2,1)S(1)}, u32[]{:S(2)}, u32[]{:S(2)}) %collective-permute-start.19) | collective-permute-done | bytes 65568 | tf_op jit(solution)/shard_map/ppermute | solution.py:617
  78.4 1.7 %collective-permute-start.20 = (bf16[64,512]{1,0:T(8,128)(2,1)S(1)}, bf16[64,512]{1,0:T(8,128)(2,1)S(1)}, u32[]{:S(2)}, u32[]{:S(2)}) collective-permute-start(bf16[64,512]{1,0:T(8,128)(2,1)S(1)} %get-tuple-element.67), channel_id=1, source_target_pairs={{0,16},{8,24},{16,0},{24,8},{32,48},{40,56},{48,32},{56,40},{64,80... | collective-permute-start | bytes 196616 | tf_op jit(solution)/shard_map/ppermute | solution.py:617
  80.1 2.4 %collective-permute-done.20.came = bf16[64,512]{1,0:T(8,128)(2,1)S(1)} collective-permute-done((bf16[64,512]{1,0:T(8,128)(2,1)S(1)}, bf16[64,512]{1,0:T(8,128)(2,1)S(1)}, u32[]{:S(2)}, u32[]{:S(2)}) %collective-permute-start.20) | collective-permute-done | bytes 65568 | tf_op jit(solution)/shard_map/ppermute | solution.py:617
  83.1 2.7 %collective-permute-start.23 = (bf16[64,5120]{1,0:T(8,128)(2,1)S(1)}, bf16[64,5120]{1,0:T(8,128)(2,1)S(1)}, u32[]{:S(2)}, u32[]{:S(2)}) collective-permute-start(bf16[64,5120]{1,0:T(8,128)(2,1)S(1)} %shard_map.150.rest_1_), channel_id=1, source_target_pairs={{0,6},{1,7},{2,0},{3,1},{4,2},{5,3},{6,4},{7,5},{8,14},{9,15},{10,... | collective-permute-start | bytes 1966088 | tf_op jit(solution)/shard_map/ppermute | solution.py:614
  85.8 1.9 %collective-permute-start.24 = (bf16[32,512]{1,0:T(8,128)(2,1)S(1)}, bf16[32,512]{1,0:T(8,128)(2,1)S(1)}, u32[]{:S(2)}, u32[]{:S(2)}) collective-permute-start(bf16[32,512]{1,0:T(8,128)(2,1)S(1)} %shard_map.148.rest_0_), channel_id=1, source_target_pairs={{0,64},{8,72},{16,80},{24,88},{32,96},{40,104},{48,112},{56,120},{... | collective-permute-start | bytes 98312 | tf_op jit(solution)/shard_map/ppermute | solution.py:617
  87.7 2.3 %collective-permute-done.24.last = bf16[32,512]{1,0:T(8,128)(2,1)S(1)} collective-permute-done((bf16[32,512]{1,0:T(8,128)(2,1)S(1)}, bf16[32,512]{1,0:T(8,128)(2,1)S(1)}, u32[]{:S(2)}, u32[]{:S(2)}) %collective-permute-start.24) | collective-permute-done | bytes 32800 | tf_op jit(solution)/shard_map/ppermute | solution.py:617
  91.2 6.8 %collective-permute-start.25 = (bf16[16,5120]{1,0:T(8,128)(2,1)S(1)}, bf16[16,5120]{1,0:T(8,128)(2,1)S(1)}, u32[]{:S(2)}, u32[]{:S(2)}) collective-permute-start(bf16[16,5120]{1,0:T(8,128)(2,1)S(1)} %get-tuple-element.74), channel_id=1, source_target_pairs={{0,1},{1,0},{2,3},{3,2},{4,5},{5,4},{6,7},{7,6},{8,9},{9,8},{10,11... | collective-permute-start | bytes 491528 | tf_op jit(solution)/shard_map/ppermute | solution.py:617
  99.2 5.4 %collective-permute-done.26.b = bf16[16,5120]{1,0:T(8,128)(2,1)S(1)} collective-permute-done((bf16[16,5120]{1,0:T(8,128)(2,1)S(1)}, bf16[16,5120]{1,0:T(8,128)(2,1)S(1)}, u32[]{:S(2)}, u32[]{:S(2)}) %collective-permute-start.26) | collective-permute-done | bytes 163872 | tf_op jit(solution)/shard_map/ppermute | solution.py:617
  106.6 4.1 %collective-permute-done.27.b = bf16[16,5120]{1,0:T(8,128)(2,1)S(1)} collective-permute-done((bf16[16,5120]{1,0:T(8,128)(2,1)S(1)}, bf16[16,5120]{1,0:T(8,128)(2,1)S(1)}, u32[]{:S(2)}, u32[]{:S(2)}) %collective-permute-start.27) | collective-permute-done | bytes 163872 | tf_op jit(solution)/shard_map/ppermute | solution.py:617
  110.8 2.2 %collective-permute-start.28 = (f32[16,5120]{1,0:T(8,128)S(1)}, f32[16,5120]{1,0:T(8,128)S(1)}, u32[]{:S(2)}, u32[]{:S(2)}) collective-permute-start(f32[16,5120]{1,0:T(8,128)S(1)} %shard_map.156.kept), channel_id=1, source_target_pairs={{0,1},{1,0},{2,3},{3,2},{4,5},{5,4},{6,7},{7,6},{8,9},{9,8},{10,11... | collective-permute-start | bytes 983048 | tf_op jit(solution)/shard_map/ppermute | solution.py:617
  (83 shorter events, 23.6 us)
Async XLA Ops:
  0.6 60.4 %collective-permute-start.13 = (bf16[384,5120]{1,0:T(8,128)(2,1)}, bf16[384,5120]{1,0:T(8,128)(2,1)}, u32[]{:S(2)}, u32[]{:S(2)}) collective-permute-start(bf16[384,5120]{1,0:T(8,128)(2,1)} %w.1), channel_id=1, source_target_pairs={{0,1},{1,0},{2,3},{3,2},{4,5},{5,4},{6,7},{7,6},{8,9},{9,8},{10,11... | collective-permute-start | bytes 11796488 | tf_op jit(solution)/shard_map/ppermute | solution.py:617
  6.4 21.9 %collective-permute-start = (bf16[64,5120]{1,0:T(8,128)(2,1)S(1)}, bf16[64,5120]{1,0:T(8,128)(2,1)S(1)}, u32[]{:S(2)}, u32[]{:S(2)}) collective-permute-start(bf16[64,5120]{1,0:T(8,128)(2,1)S(1)} %shard_map.131.refs_0_), channel_id=1, source_target_pairs={{0,2},{1,3},{2,4},{3,5},{4,6},{5,7},{6,0},{7,1},{8,10},{9,11},{10,... | collective-permute-start | bytes 1966088 | tf_op jit(solution)/shard_map/ppermute | solution.py:614
  6.5 21.9 %collective-permute-start.1 = (bf16[64,5120]{1,0:T(8,128)(2,1)S(1)}, bf16[64,5120]{1,0:T(8,128)(2,1)S(1)}, u32[]{:S(2)}, u32[]{:S(2)}) collective-permute-start(bf16[64,5120]{1,0:T(8,128)(2,1)S(1)} %shard_map.131.refs_0_), channel_id=1, source_target_pairs={{0,6},{1,7},{2,0},{3,1},{4,2},{5,3},{6,4},{7,5},{8,14},{9,15},{10,... | collective-permute-start | bytes 1966088 | tf_op jit(solution)/shard_map/ppermute | solution.py:614
  9.1 23.5 %collective-permute-start.5 = (bf16[64,5120]{1,0:T(8,128)(2,1)S(1)}, bf16[64,5120]{1,0:T(8,128)(2,1)S(1)}, u32[]{:S(2)}, u32[]{:S(2)}) collective-permute-start(bf16[64,5120]{1,0:T(8,128)(2,1)S(1)} %shard_map.131.refs_0_), channel_id=1, source_target_pairs={{0,1},{1,0},{2,3},{3,2},{4,5},{5,4},{6,7},{7,6},{8,9},{9,8},{10,11... | collective-permute-start | bytes 1966088 | tf_op jit(solution)/shard_map/ppermute | solution.py:617
  18.9 25.1 %copy-start.1 = (f32[512,256]{1,0:T(8,128)S(1)}, f32[512,256]{1,0:T(8,128)}, u32[]{:S(2)}) copy-start(f32[512,256]{1,0:T(8,128)} %constant.14.clone.refs_3_.refs_5_) | copy-start | bytes 1572868
  21.6 6.7 %collective-permute-start.2 = (bf16[32,384]{1,0:T(8,128)(2,1)S(1)}, bf16[32,384]{1,0:T(8,128)(2,1)S(1)}, u32[]{:S(2)}, u32[]{:S(2)}) collective-permute-start(bf16[32,384]{1,0:T(8,128)(2,1)S(1)} %get-tuple-element.42.a.q), channel_id=1, source_target_pairs={{0,32},{8,40},{16,48},{24,56},{32,0},{40,8},{48,16},{56,24},{64,96... | collective-permute-start | bytes 73736 | tf_op jit(solution)/shard_map/ppermute | solution.py:617
  28.3 17.1 %collective-permute-start.3 = (bf16[64,5120]{1,0:T(8,128)(2,1)S(1)}, bf16[64,5120]{1,0:T(8,128)(2,1)S(1)}, u32[]{:S(2)}, u32[]{:S(2)}) collective-permute-start(bf16[64,5120]{1,0:T(8,128)(2,1)S(1)} %get-tuple-element.43.refs_0_.a), channel_id=1, source_target_pairs={{0,1},{1,0},{2,3},{3,2},{4,5},{5,4},{6,7},{7,6},{8,9},{9,8},{10,11... | collective-permute-start | bytes 1966088 | tf_op jit(solution)/shard_map/ppermute | solution.py:617
  29.6 17.6 %collective-permute-start.4 = (bf16[64,5120]{1,0:T(8,128)(2,1)S(1)}, bf16[64,5120]{1,0:T(8,128)(2,1)S(1)}, u32[]{:S(2)}, u32[]{:S(2)}) collective-permute-start(bf16[64,5120]{1,0:T(8,128)(2,1)S(1)} %get-tuple-element.44.refs_1_.b), channel_id=1, source_target_pairs={{0,1},{1,0},{2,3},{3,2},{4,5},{5,4},{6,7},{7,6},{8,9},{9,8},{10,11... | collective-permute-start | bytes 1966088 | tf_op jit(solution)/shard_map/ppermute | solution.py:617
  29.7 2.9 %collective-permute-start.10 = (bf16[64,384]{1,0:T(8,128)(2,1)S(1)}, bf16[64,384]{1,0:T(8,128)(2,1)S(1)}, u32[]{:S(2)}, u32[]{:S(2)}) collective-permute-start(bf16[64,384]{1,0:T(8,128)(2,1)S(1)} %shard_map.134.refs_2_.near), channel_id=1, source_target_pairs={{0,8},{8,0},{16,24},{24,16},{32,40},{40,32},{48,56},{56,48},{64,72... | collective-permute-start | bytes 147464 | tf_op jit(solution)/shard_map/ppermute | solution.py:617
  32.6 8.9 %collective-permute-start.6 = (bf16[32,5120]{1,0:T(8,128)(2,1)S(1)}, bf16[32,5120]{1,0:T(8,128)(2,1)S(1)}, u32[]{:S(2)}, u32[]{:S(2)}) collective-permute-start(bf16[32,5120]{1,0:T(8,128)(2,1)S(1)} %get-tuple-element.49), channel_id=1, source_target_pairs={{0,2},{1,3},{2,4},{3,5},{4,6},{5,7},{6,0},{7,1},{8,10},{9,11},{10,... | collective-permute-start | bytes 983048 | tf_op jit(solution)/shard_map/ppermute | solution.py:614
  32.6 11.3 %collective-permute-start.7 = (bf16[32,5120]{1,0:T(8,128)(2,1)S(1)}, bf16[32,5120]{1,0:T(8,128)(2,1)S(1)}, u32[]{:S(2)}, u32[]{:S(2)}) collective-permute-start(bf16[32,5120]{1,0:T(8,128)(2,1)S(1)} %get-tuple-element.50), channel_id=1, source_target_pairs={{0,6},{1,7},{2,0},{3,1},{4,2},{5,3},{6,4},{7,5},{8,14},{9,15},{10,... | collective-permute-start | bytes 983048 | tf_op jit(solution)/shard_map/ppermute | solution.py:614
  41.5 9.6 %collective-permute-start.8 = (bf16[32,5120]{1,0:T(8,128)(2,1)S(1)}, bf16[32,5120]{1,0:T(8,128)(2,1)S(1)}, u32[]{:S(2)}, u32[]{:S(2)}) collective-permute-start(bf16[32,5120]{1,0:T(8,128)(2,1)S(1)} %collective-permute-done.6.rest_0_.refs_0_), channel_id=1, source_target_pairs={{0,1},{1,0},{2,3},{3,2},{4,5},{5,4},{6,7},{7,6},{8,9},{9,8},{10,11... | collective-permute-start | bytes 983048 | tf_op jit(solution)/shard_map/ppermute | solution.py:617
  44.0 7.2 %collective-permute-start.9 = (bf16[32,5120]{1,0:T(8,128)(2,1)S(1)}, bf16[32,5120]{1,0:T(8,128)(2,1)S(1)}, u32[]{:S(2)}, u32[]{:S(2)}) collective-permute-start(bf16[32,5120]{1,0:T(8,128)(2,1)S(1)} %collective-permute-done.7.rest_1_.refs_1_), channel_id=1, source_target_pairs={{0,1},{1,0},{2,3},{3,2},{4,5},{5,4},{6,7},{7,6},{8,9},{9,8},{10,11... | collective-permute-start | bytes 983048 | tf_op jit(solution)/shard_map/ppermute | solution.py:617
  45.4 5.7 %collective-permute-start.11 = (bf16[64,384]{1,0:T(8,128)(2,1)S(1)}, bf16[64,384]{1,0:T(8,128)(2,1)S(1)}, u32[]{:S(2)}, u32[]{:S(2)}) collective-permute-start(bf16[64,384]{1,0:T(8,128)(2,1)S(1)} %get-tuple-element.57), channel_id=1, source_target_pairs={{0,16},{8,24},{16,0},{24,8},{32,48},{40,56},{48,32},{56,40},{64,80... | collective-permute-start | bytes 147464 | tf_op jit(solution)/shard_map/ppermute | solution.py:617
  49.4 11.1 %collective-permute-start.15 = (bf16[384,256]{1,0:T(8,128)(2,1)S(1)}, bf16[384,256]{1,0:T(8,128)(2,1)S(1)}, u32[]{:S(2)}, u32[]{:S(2)}) collective-permute-start(bf16[384,256]{1,0:T(8,128)(2,1)S(1)} %get-tuple-element.54.rest_0_.kv_a), channel_id=1, source_target_pairs={{0,128},{128,0},{1,129},{129,1},{2,130},{130,2},{3,131},{131,3},{4... | collective-permute-start | bytes 589832 | tf_op jit(solution)/shard_map/ppermute | solution.py:617
  53.9 7.1 %collective-permute-start.12 = (bf16[256,384]{1,0:T(8,128)(2,1)S(1)}, bf16[256,384]{1,0:T(8,128)(2,1)S(1)}, u32[]{:S(2)}, u32[]{:S(2)}) collective-permute-start(bf16[256,384]{1,0:T(8,128)(2,1)S(1)} %get-tuple-element.59), channel_id=1, source_target_pairs={{0,1},{1,0},{2,3},{3,2},{4,5},{5,4},{6,7},{7,6},{8,9},{9,8},{10,11... | collective-permute-start | bytes 589832 | tf_op jit(solution)/shard_map/ppermute | solution.py:617
  55.0 5.5 %collective-permute-start.16 = (bf16[128,256]{1,0:T(8,128)(2,1)S(1)}, bf16[128,256]{1,0:T(8,128)(2,1)S(1)}, u32[]{:S(2)}, u32[]{:S(2)}) collective-permute-start(bf16[128,256]{1,0:T(8,128)(2,1)S(1)} %get-tuple-element.55.kv_b), channel_id=1, source_target_pairs={{0,128},{128,0},{1,129},{129,1},{2,130},{130,2},{3,131},{131,3},{4... | collective-permute-start | bytes 196616 | tf_op jit(solution)/shard_map/ppermute | solution.py:617
  55.7 4.9 %collective-permute-start.14 = (bf16[32,384]{1,0:T(8,128)(2,1)S(1)}, bf16[32,384]{1,0:T(8,128)(2,1)S(1)}, u32[]{:S(2)}, u32[]{:S(2)}) collective-permute-start(bf16[32,384]{1,0:T(8,128)(2,1)S(1)} %shard_map.141.rest_0_), channel_id=1, source_target_pairs={{0,64},{8,72},{16,80},{24,88},{32,96},{40,104},{48,112},{56,120},{... | collective-permute-start | bytes 73736 | tf_op jit(solution)/shard_map/ppermute | solution.py:617
  65.5 17.0 %collective-permute-start.17 = (bf16[32,5120]{1,0:T(8,128)(2,1)S(1)}, bf16[32,5120]{1,0:T(8,128)(2,1)S(1)}, u32[]{:S(2)}, u32[]{:S(2)}) collective-permute-start(bf16[32,5120]{1,0:T(8,128)(2,1)S(1)} %get-tuple-element.62), channel_id=1, source_target_pairs={{0,2},{1,3},{2,4},{3,5},{4,6},{5,7},{6,0},{7,1},{8,10},{9,11},{10,... | collective-permute-start | bytes 983048 | tf_op jit(solution)/shard_map/ppermute | solution.py:614
  65.6 17.3 %collective-permute-start.22 = (bf16[32,5120]{1,0:T(8,128)(2,1)S(1)}, bf16[32,5120]{1,0:T(8,128)(2,1)S(1)}, u32[]{:S(2)}, u32[]{:S(2)}) collective-permute-start(bf16[32,5120]{1,0:T(8,128)(2,1)S(1)} %get-tuple-element.69), channel_id=1, source_target_pairs={{0,6},{1,7},{2,0},{3,1},{4,2},{5,3},{6,4},{7,5},{8,14},{9,15},{10,... | collective-permute-start | bytes 983048 | tf_op jit(solution)/shard_map/ppermute | solution.py:614
  68.3 6.8 %collective-permute-start.18 = (bf16[32,512]{1,0:T(8,128)(2,1)S(1)}, bf16[32,512]{1,0:T(8,128)(2,1)S(1)}, u32[]{:S(2)}, u32[]{:S(2)}) collective-permute-start(bf16[32,512]{1,0:T(8,128)(2,1)S(1)} %shard_map.143.after.a), channel_id=1, source_target_pairs={{0,32},{8,40},{16,48},{24,56},{32,0},{40,8},{48,16},{56,24},{64,96... | collective-permute-start | bytes 98312 | tf_op jit(solution)/shard_map/ppermute | solution.py:617
  75.1 3.1 %collective-permute-start.19 = (bf16[64,512]{1,0:T(8,128)(2,1)S(1)}, bf16[64,512]{1,0:T(8,128)(2,1)S(1)}, u32[]{:S(2)}, u32[]{:S(2)}) collective-permute-start(bf16[64,512]{1,0:T(8,128)(2,1)S(1)} %shard_map.145.after.near), channel_id=1, source_target_pairs={{0,8},{8,0},{16,24},{24,16},{32,40},{40,32},{48,56},{56,48},{64,72... | collective-permute-start | bytes 196616 | tf_op jit(solution)/shard_map/ppermute | solution.py:617
  78.4 4.1 %collective-permute-start.20 = (bf16[64,512]{1,0:T(8,128)(2,1)S(1)}, bf16[64,512]{1,0:T(8,128)(2,1)S(1)}, u32[]{:S(2)}, u32[]{:S(2)}) collective-permute-start(bf16[64,512]{1,0:T(8,128)(2,1)S(1)} %get-tuple-element.67), channel_id=1, source_target_pairs={{0,16},{8,24},{16,0},{24,8},{32,48},{40,56},{48,32},{56,40},{64,80... | collective-permute-start | bytes 196616 | tf_op jit(solution)/shard_map/ppermute | solution.py:617
  82.6 22.9 %collective-permute-start.21 = (bf16[64,5120]{1,0:T(8,128)(2,1)S(1)}, bf16[64,5120]{1,0:T(8,128)(2,1)S(1)}, u32[]{:S(2)}, u32[]{:S(2)}) collective-permute-start(bf16[64,5120]{1,0:T(8,128)(2,1)S(1)} %shard_map.149.rest_0_), channel_id=1, source_target_pairs={{0,2},{1,3},{2,4},{3,5},{4,6},{5,7},{6,0},{7,1},{8,10},{9,11},{10,... | collective-permute-start | bytes 1966088 | tf_op jit(solution)/shard_map/ppermute | solution.py:614
  82.9 22.6 %copy-start.4 = (bf16[1,1,64,5120]{3,2,1,0:T(8,128)(2,1)S(1)}, bf16[1,1,64,5120]{3,2,1,0:T(8,128)(2,1)}, u32[]{:S(2)}) copy-start(bf16[1,1,64,5120]{3,2,1,0:T(8,128)(2,1)} %param.12) | copy-start | bytes 1966084
  83.1 22.4 %collective-permute-start.23 = (bf16[64,5120]{1,0:T(8,128)(2,1)S(1)}, bf16[64,5120]{1,0:T(8,128)(2,1)S(1)}, u32[]{:S(2)}, u32[]{:S(2)}) collective-permute-start(bf16[64,5120]{1,0:T(8,128)(2,1)S(1)} %shard_map.150.rest_1_), channel_id=1, source_target_pairs={{0,6},{1,7},{2,0},{3,1},{4,2},{5,3},{6,4},{7,5},{8,14},{9,15},{10,... | collective-permute-start | bytes 1966088 | tf_op jit(solution)/shard_map/ppermute | solution.py:614
  85.8 4.3 %collective-permute-start.24 = (bf16[32,512]{1,0:T(8,128)(2,1)S(1)}, bf16[32,512]{1,0:T(8,128)(2,1)S(1)}, u32[]{:S(2)}, u32[]{:S(2)}) collective-permute-start(bf16[32,512]{1,0:T(8,128)(2,1)S(1)} %shard_map.148.rest_0_), channel_id=1, source_target_pairs={{0,64},{8,72},{16,80},{24,88},{32,96},{40,104},{48,112},{56,120},{... | collective-permute-start | bytes 98312 | tf_op jit(solution)/shard_map/ppermute | solution.py:617
  90.4 23.8 %copy-start.8 = (bf16[1,16,2,5120]{3,2,1,0:T(2,128)(2,1)S(1)}, bf16[1,16,2,5120]{3,2,1,0:T(2,128)(2,1)}, u32[]{:S(2)}) copy-start(bf16[1,16,2,5120]{3,2,1,0:T(2,128)(2,1)} %param.13) | copy-start | bytes 983044
  91.2 7.8 %collective-permute-start.25 = (bf16[16,5120]{1,0:T(8,128)(2,1)S(1)}, bf16[16,5120]{1,0:T(8,128)(2,1)S(1)}, u32[]{:S(2)}, u32[]{:S(2)}) collective-permute-start(bf16[16,5120]{1,0:T(8,128)(2,1)S(1)} %get-tuple-element.74), channel_id=1, source_target_pairs={{0,1},{1,0},{2,3},{3,2},{4,5},{5,4},{6,7},{7,6},{8,9},{9,8},{10,11... | collective-permute-start | bytes 491528 | tf_op jit(solution)/shard_map/ppermute | solution.py:617
  99.1 5.5 %collective-permute-start.26 = (bf16[16,5120]{1,0:T(8,128)(2,1)S(1)}, bf16[16,5120]{1,0:T(8,128)(2,1)S(1)}, u32[]{:S(2)}, u32[]{:S(2)}) collective-permute-start(bf16[16,5120]{1,0:T(8,128)(2,1)S(1)} %shard_map.154.a), channel_id=1, source_target_pairs={{0,2},{1,3},{2,0},{3,1},{4,6},{5,7},{6,4},{7,5},{8,10},{9,11},{10,... | collective-permute-start | bytes 491528 | tf_op jit(solution)/shard_map/ppermute | solution.py:617
  104.6 6.1 %collective-permute-start.27 = (bf16[16,5120]{1,0:T(8,128)(2,1)S(1)}, bf16[16,5120]{1,0:T(8,128)(2,1)S(1)}, u32[]{:S(2)}, u32[]{:S(2)}) collective-permute-start(bf16[16,5120]{1,0:T(8,128)(2,1)S(1)} %shard_map.155.a), channel_id=1, source_target_pairs={{0,4},{1,5},{2,6},{3,7},{4,0},{5,1},{6,2},{7,3},{8,12},{9,13},{10,... | collective-permute-start | bytes 491528 | tf_op jit(solution)/shard_map/ppermute | solution.py:617
  110.8 3.5 %collective-permute-start.28 = (f32[16,5120]{1,0:T(8,128)S(1)}, f32[16,5120]{1,0:T(8,128)S(1)}, u32[]{:S(2)}, u32[]{:S(2)}) collective-permute-start(f32[16,5120]{1,0:T(8,128)S(1)} %shard_map.156.kept), channel_id=1, source_target_pairs={{0,1},{1,0},{2,3},{3,2},{4,5},{5,4},{6,7},{7,6},{8,9},{9,8},{10,11... | collective-permute-start | bytes 983048 | tf_op jit(solution)/shard_map/ppermute | solution.py:617
  (12 other events, 49.7 us)

commit v3 on v2

--- a/solution.py
+++ b/solution.py
@@ -12,6 +12,10 @@
 EPSILON = 1e-06
 ROPE_BASE = 1000000.0
 VMEM_LIMIT = 14 * 1024 * 1024
+WIDE_LIMIT = VMEM_LIMIT
+FULL_LIMIT = VMEM_LIMIT
+STEP = 900_000_000
+TAIL = STEP*2
 FIRST, SECOND, THIRD, FOURTH = 4, 1, 2, 8
 HELD = (0, FIRST, SECOND, FIRST ^ SECOND)
 SERVED = (0, THIRD, FOURTH, THIRD ^ FOURTH)
@@ -30,7 +34,7 @@
 HBM = pl.BlockSpec(memory_space=pltpu.HBM)
 
 
-def simple_call(body, out_shape, flops, *args, specs=None, scratch=()):
+def simple_call(body, out_shape, flops, *args, specs=None, scratch=(), limit=VMEM_LIMIT):
     nbytes = sum(a.size * a.dtype.itemsize for a in args)
     return pl.pallas_call(
         body,
@@ -38,8 +42,8 @@
         out_specs=jax.tree.map(lambda _: VMEM, out_shape),
         out_shape=out_shape,
         scratch_shapes=list(scratch),
-        compiler_params=pltpu.CompilerParams(vmem_limit_bytes=VMEM_LIMIT),
-        cost_estimate=pl.CostEstimate(flops=flops, bytes_accessed=nbytes if flops else 0, transcendentals=0),
+        compiler_params=pltpu.CompilerParams(vmem_limit_bytes=limit),
+        cost_estimate=pl.CostEstimate(flops=flops, bytes_accessed=nbytes if flops > 9 * STEP else 0, transcendentals=0),
     )(*args)
 
 
@@ -114,7 +118,7 @@
     return simple_call(
         functools.partial(fresh_body, samples),
         (jax.ShapeDtypeStruct((rows, width), jnp.bfloat16), flat, flat, choice, choice),
-        1_000_000, grp, *far,
+        6 * STEP, grp, *far,
         specs=[SMEM] + [HBM] * 5,
         scratch=held
         + [
@@ -129,8 +133,8 @@
     shape = jax.ShapeDtypeStruct(x.shape, jnp.bfloat16)
     far = (x, gain.reshape(1, -1))
     return simple_call(
-        norm_body, shape, 1_000_000, tp, grp, *far,
-        specs=[SMEM] * 2 + [HBM] * 2, scratch=like(*far),
+        norm_body, shape, 8 * STEP, tp, grp, *far,
+        specs=[SMEM] * 2 + [HBM] * 2, scratch=like(*far), limit=FULL_LIMIT,
     )
 
 
@@ -206,28 +210,28 @@
     out[...] = part[...] + came[rows:]
 
 
-def exchange_near(value, swap, after):
+def exchange_near(value, swap, after, cost=0):
     shape = jax.ShapeDtypeStruct((2 * value.shape[0], value.shape[1]), value.dtype)
     args = (value, swap(value, "grp", FIRST))
     specs = [VMEM] * 2 + [ANY] * len(after)
-    return simple_call(join_body, shape, 0, *args, *after, specs=specs)
-
-
-def exchange_pick(near, choice, swap, after):
+    return simple_call(join_body, shape, cost, *args, *after, specs=specs)
+
+
+def exchange_pick(near, choice, swap, after, cost=0):
     rows, wide = near.shape[0] // 2, near.shape[1]
     shape = lambda n: jax.ShapeDtypeStruct((n * rows, wide), near.dtype)
     args = (choice, near, swap(near, "grp", SECOND))
     return simple_call(
-        pick_body, (shape(1), shape(2), shape(1)), 0, *args, *after,
+        pick_body, (shape(1), shape(2), shape(1)), cost, *args, *after,
         specs=[VMEM] * 3 + [ANY] * len(after),
     )
 
 
-def exchange_pass(third, fourth, swap, after):
+def exchange_pass(third, fourth, swap, after, cost=0):
     came = swap(third, "grp", THIRD)
     shape = jax.ShapeDtypeStruct(fourth.shape, fourth.dtype)
     specs = [VMEM] * 2 + [ANY] * len(after)
-    return came, simple_call(pass_body, shape, 0, fourth, came, *after, specs=specs)
+    return came, simple_call(pass_body, shape, cost, fourth, came, *after, specs=specs)
 
 
 def arrived(kept, came, last):
@@ -271,19 +275,11 @@
     return [slice(i * depth // count, (i + 1) * depth // count) for i in range(count)]
 
 
-def fresh_qkv_body(x, wq, wk, wv, cos, sin, q_out, kv_out, joined, acc, sems):
-    copies = []
+def fresh_qkv_body(x, wq, wk, wv, cos, sin, q_out, kv_out, joined, acc):
     for i, part in enumerate(chunks(x.shape[1])):
-        at = 0
-        for j, w in enumerate((wq, wk, wv)):
-            target = joined.at[part, at : at + w.shape[1]]
-            at += w.shape[1]
-            copies.append(pltpu.make_async_copy(w.at[part], target, sems.at[i, j]))
-            copies[-1].start()
-    for i, part in enumerate(chunks(x.shape[1])):
-        for j in range(3):
-            copies[3 * i + j].wait()
-        piece = jnp.dot(x[:, part], joined[part], preferred_element_type=jnp.float32)
+        w = jnp.concatenate([wq[part], wk[part], wv[part]], axis=1)
+        joined[part] = w
+        piece = jnp.dot(x[:, part], w, preferred_element_type=jnp.float32)
         acc[...] = piece if i == 0 else acc[...] + piece
     rotate(acc, cos[...], sin[...], q_out, kv_out, 0)
 
@@ -295,12 +291,8 @@
     return simple_call(
         fresh_qkv_body,
         (shape(rows, total - 2 * HEAD_WIDTH), shape(rows, 2 * HEAD_WIDTH), shape(depth, total)),
-        2 * rows * depth * total, x, *weights, *tables,
-        specs=[VMEM] + [HBM] * 3 + [VMEM] * 2,
-        scratch=[
-            pltpu.VMEM((rows, total), jnp.float32),
-            pltpu.SemaphoreType.DMA((len(chunks(depth)), 3)),
-        ],
+        STEP, x, *weights, *tables,
+        scratch=[pltpu.VMEM((rows, total), jnp.float32)],
     )
 
 
@@ -324,14 +316,14 @@
     rotate(acc, both[:, :HEAD_WIDTH], both[:, HEAD_WIDTH:], q_out, kv_out, base)
 
 
-def qkv(blocks, joined, table, where, first, block, early=(), after=()):
+def qkv(blocks, joined, table, where, first, block, cost, early=(), after=()):
     rows, (depth, total) = sum(b.shape[0] for b in blocks), joined.shape
     base = early[0].shape[0] if early else 0
     shape = lambda wide: jax.ShapeDtypeStruct((base + rows, wide), jnp.bfloat16)
     return simple_call(
         functools.partial(qkv_body, len(blocks), first, block, bool(early), len(after)),
         (shape(total - 2 * HEAD_WIDTH), shape(2 * HEAD_WIDTH)),
-        2 * rows * depth * total, *blocks, joined, jnp.asarray(table), where, *early, *after,
+        cost, *blocks, joined, jnp.asarray(table), where, *early, *after,
         specs=[VMEM] * (len(blocks) + 2) + [SMEM] + [VMEM] * len(early) + [ANY] * len(after),
         scratch=[pltpu.VMEM((rows, total), jnp.float32)],
     )
@@ -417,7 +409,7 @@
     rows, wide = asked[0].shape
     shape = jax.ShapeDtypeStruct((rows, wide + HEAD_WIDTH), jnp.bfloat16)
     return simple_call(
-        functools.partial(prefix_body, scale), shape, 100_000_000, *asked, kv_a, kv_b, after,
+        functools.partial(prefix_body, scale), shape, 4 * STEP, *asked, kv_a, kv_b, after,
         specs=[VMEM] * 5 + [ANY],
     )
 
@@ -502,29 +494,50 @@
     return [slice(i * tile, (i + 1) * tile) for i in range(wide // tile)]
 
 
-def out_body(own, other, w_own, w_other, after, *outs):
+def stage_body(own, other, *rest):
+    both, sems = rest[-2:]
+    depth = own.shape[0]
+    copies = [
+        pltpu.make_async_copy(own, both.at[:depth], sems.at[0]),
+        pltpu.make_async_copy(other, both.at[depth:], sems.at[1]),
+    ]
+    for copy in copies:
+        copy.start()
+    for copy in copies:
+        copy.wait()
+
+
+def stage(own, other, after):
+    shape = jax.ShapeDtypeStruct((2 * own.shape[0], own.shape[1]), own.dtype)
+    return simple_call(
+        stage_body, shape, 0, own, other, *after,
+        specs=[HBM] * 2 + [ANY] * len(after), scratch=[pltpu.SemaphoreType.DMA((2,))],
+    )
+
+
+def out_body(own, other, w, *rest):
+    outs = rest[1:]
     heads = jnp.concatenate([own[...], other[...]], axis=1)
-    for part in strips(w_own.shape[1]):
-        w = jnp.concatenate([w_own[:, part], w_other[:, part]], axis=0)
-        rows = jnp.dot(heads, w, preferred_element_type=jnp.float32)
+    for part in strips(w.shape[1]):
+        rows = jnp.dot(heads, w[:, part], preferred_element_type=jnp.float32)
         base = 0
         for out in outs:
             out[:, part] = rows[base : base + out.shape[0]].astype(out.dtype)
             base += out.shape[0]
 
 
-def out_projection(own, other, w_own, w_other, blocks, dtype, after):
-    shapes = tuple(jax.ShapeDtypeStruct((b, w_own.shape[1]), dtype) for b in blocks)
-    return simple_call(
-        out_body, shapes, 0, own, other, w_own, w_other, after, specs=[VMEM] * 4 + [ANY]
+def out_projection(own, other, w, blocks, dtype, after):
+    shapes = tuple(jax.ShapeDtypeStruct((b, w.shape[1]), dtype) for b in blocks)
+    return simple_call(
+        out_body, shapes, 0, own, other, w, after, specs=[VMEM] * 3 + [ANY]
     )
 
 
 def partial_body(tp, heads, w, kept, given):
     core = tp[0] % 2
-    rows = kept.shape[0]
+    rows, depth = kept.shape[0], heads.shape[1]
     for columns in strips(w.shape[1]):
-        part = jnp.dot(heads[...], w[:, columns], preferred_element_type=jnp.float32)
+        part = jnp.dot(heads[...], w[:depth, columns], preferred_element_type=jnp.float32)
         low, high = part[:rows], part[rows:]
         kept[:, columns] = jnp.where(core == 0, low, high).astype(kept.dtype)
         given[:, columns] = jnp.where(core == 0, high, low).astype(given.dtype)
@@ -533,7 +546,7 @@
 def partial_projection(tp, heads, w):
     shape = jax.ShapeDtypeStruct((heads.shape[0] // 2, w.shape[1]), jnp.bfloat16)
     return simple_call(
-        partial_body, (shape, shape), 0, tp, heads, w, specs=[SMEM, VMEM, VMEM]
+        partial_body, (shape, shape), TAIL, tp, heads, w, specs=[SMEM, VMEM, VMEM]
     )
 
 
@@ -545,7 +558,19 @@
 def add(a, b, dtype, after=()):
     shape = jax.ShapeDtypeStruct(a.shape, dtype)
     specs = [VMEM] * 2 + [ANY] * len(after)
-    return simple_call(add_body, shape, 0, a, b, *after, specs=specs)
+    return simple_call(add_body, shape, TAIL, a, b, *after, specs=specs)
+
+
+def add_four_body(own, far, down, up, *rest):
+    out = rest[-1]
+    wide = own[...].astype(jnp.float32) + far[...].astype(jnp.float32)
+    out[...] = wide + (down[...].astype(jnp.float32) + up[...].astype(jnp.float32))
+
+
+def add_four(own, far, down, up, after):
+    shape = jax.ShapeDtypeStruct(own.shape, jnp.float32)
+    specs = [VMEM] * 4 + [ANY] * len(after)
+    return simple_call(add_four_body, shape, TAIL, own, far, down, up, *after, specs=specs)
 
 
 def add_half_body(first, whole, part, *rest):
@@ -587,7 +612,7 @@
 def finish(tp, kept, taken, tokens):
     shape = jax.ShapeDtypeStruct(tokens.shape, jnp.float32)
     return simple_call(
-        finish_body, shape, 0, tp, kept, taken, tokens,
+        finish_body, shape, TAIL, tp, kept, taken, tokens,
         specs=[SMEM] + [VMEM] * 3,
     )
 
@@ -635,37 +660,40 @@
     where = tp
     tables = fixed_tables(0, length)
     asked = exchange_near(fresh_q, swap, ())
-    from_down, from_up = hold((from_down, from_up), (asked,))
+    early = qkv([normed, mate_own], weights, tables, where, 0, block, STEP)
+    kept, third, fourth = exchange_pick(asked, forth, swap, ())
+    from_down, from_up = hold((from_down, from_up), (third, early[1]))
     down_top, up_low = cut(from_down, from_up)
     ahead = around(down_top, 1)
     behind = around(up_low, -1)
     near = [from_down, from_up, swap(from_down, "tp", 1), swap(from_up, "tp", 1)]
-    early = qkv([normed, mate_own], weights, tables, where, 0, block)
-    kept, third, fourth = exchange_pick(asked, forth, swap, (ahead, behind))
-    q_a, kv_a = qkv(near, weights, tables, where, 2, block, early)
+    q_a, kv_a = qkv(near, weights, tables, where, 2, block, 0, early)
     handed_a = swap(kv_a, "role", 1)
+    w_both = stage(w_out, w_mate, (kv_a,))
+    came, fourth = exchange_pass(third, fourth, swap, ())
+    ahead, behind = hold((ahead, behind), (w_both,))
+    last = swap(fourth, "grp", FOURTH)
     far = [ahead, behind, swap(ahead, "tp", 1), swap(behind, "tp", 1)]
-    q_b, kv_b = qkv(far, weights, tables, where, 6, block, after=(kept,))
+    q_b, kv_b = qkv(far, weights, tables, where, 6, block, 0)
     handed_b = swap(kv_b, "role", 1)
-    came, fourth = exchange_pass(third, fourth, swap, (kv_a,))
-
-    heads_own, heads_other = prefill_attention(q_a, q_b, kv_a, kv_b, where, scale, (fourth,))
+
+    heads_own, heads_other = prefill_attention(q_a, q_b, kv_a, kv_b, where, scale, ())
     heads_mate = swap(heads_other, "tp", 1)
 
-    asked = (kept, came, swap(fourth, "grp", FOURTH))
+    asked = (kept, came, last)
     answered = prefix_attention(asked, handed_a, handed_b, scale, heads_own)
 
     sizes = (block, block, block, half, half)
     to_own, to_down, to_up, far_top, far_low = out_projection(
-        heads_own, heads_mate, w_out, w_mate, sizes, jnp.bfloat16, answered
+        heads_own, heads_mate, w_both, sizes, jnp.bfloat16, answered
     )
     via_up = around(far_top, 1)
     via_down = around(far_low, -1)
 
-    back = exchange_near(answered, swap, ())
+    back = exchange_near(answered, swap, (), STEP)
     local, stats = local_attention(fresh_q, fresh_kv, answer_cache[0], suffix_len, scale, back)
-    kept, third, fourth = exchange_pick(back, home, swap, (local,))
-    came, fourth = exchange_pass(third, fourth, swap, ())
+    kept, third, fourth = exchange_pick(back, home, swap, (local,), STEP)
+    came, fourth = exchange_pass(third, fourth, swap, (), STEP)
     up = add_half(0, to_up, via_up, (fourth,))
     down = add_half(1, to_down, via_down, (fourth,))
     back = (kept, came, swap(fourth, "grp", FOURTH))
@@ -678,10 +706,9 @@
     )
 
     decoded = merge(back, local, stats, (up, down))
-    kept, given = partial_projection(tp, decoded, w_out)
+    kept, given = partial_projection(tp, decoded, w_both)
     level = add(kept, swap(given, "tp", 1), jnp.bfloat16)
-    level = add(level, swap(level, "tp", 2), jnp.bfloat16)
-    summed = add(level, swap(level, "tp", 4), jnp.float32, (token,))
+    summed = add_four(level, around(level, 2), around(level, 1), around(level, -1), (token,))
     decode_out = finish(tp, summed, swap(summed, "tp", 1), new_states[0])
     return prefill_out[None, None], decode_out[None]
 

time: 116 us -> 99.4 us (0.86)
  waiting for transfers between devices: 31.7 us -> 21.3 us
  local copies, waits for them, and re-layouts: 9.8 us -> 3.5 us
  starting transfers between devices: 52.2 us -> 53.4 us
    ppermute x21 -> x19, waiting for transfers between devices: 25.5 us -> 11.5 us  [swap(): lax.ppermute(value, axis, [(i, i ^ mask) for i in range(lax.axis_size(axi...]
    unnamed x30 -> x28, local copies, waits for them, and re-layouts: 9.8 us -> 3.5 us
    ppermute x8 -> x11, waiting for transfers between devices: 6.19 us -> 9.81 us  [around(): lax.ppermute(value, 'tp', [(i, (i + 2 * by) % tp_size) for i in range(tp_...]
    ppermute x8 -> x11, starting transfers between devices: 11.2 us -> 14 us  [around(): lax.ppermute(value, 'tp', [(i, (i + 2 * by) % tp_size) for i in range(tp_...]
    ppermute x21 -> x19, starting transfers between devices: 41 us -> 39.4 us  [swap(): lax.ppermute(value, axis, [(i, i ^ mask) for i in range(lax.axis_size(axi...]
  transfers between devices with their start and end apart: 29 -> 30, of which waited for: 12 -> 11; matrix products, arithmetic and copies ran while one was open for 0% -> 0% of each run, Pallas kernels for 13% -> 19%
where the time goes in v3:
time: 99.4 us; the launch traced here: 99.2 us
  starting transfers between devices  53.4 us (54%)
  waiting for transfers between devices  21.3 us (21%)
  Pallas kernels  20 us (20%)
  local copies, waits for them, and re-layouts  3.5 us (4%)
    ppermute x19, starting transfers between devices, swap(): lax.ppermute(value, axis, [(i, i ^ mask) for i in range(lax.axis_size(axi...  39.4 us
    pallas_call x26, Pallas kernels, simple_call(): pl.pallas_call(body, in_specs=specs or [VMEM] * len(args), out_specs=jax....  20 us
    ppermute x11, starting transfers between devices, around(): lax.ppermute(value, 'tp', [(i, (i + 2 * by) % tp_size) for i in range(tp_...  14 us
    ppermute x19, waiting for transfers between devices, swap(): lax.ppermute(value, axis, [(i, i ^ mask) for i in range(lax.axis_size(axi...  11.5 us
    ppermute x11, waiting for transfers between devices, around(): lax.ppermute(value, 'tp', [(i, (i + 2 * by) % tp_size) for i in range(tp_...  9.81 us
    unnamed x28, local copies, waits for them, and re-layouts  3.5 us
  transfers between devices with their start and end apart: 30, of which 11 were waited for; matrix products, arithmetic and copies ran while one was open for 0% of the time, Pallas kernels for 19%

profile of v3, /device:TPU:1, one launch (start us, length us, event | category | flops | bytes accessed | tf_op | source)
XLA Modules:
  0.0 99.2 jit_solution(317816557406544086)
XLA Ops:
  0.6 3.3 %collective-permute-start.9 = (bf16[384,5120]{1,0:T(8,128)(2,1)}, bf16[384,5120]{1,0:T(8,128)(2,1)}, u32[]{:S(2)}, u32[]{:S(2)}) collective-permute-start(bf16[384,5120]{1,0:T(8,128)(2,1)} %own.1), channel_id=1, source_target_pairs={{0,1},{1,0},{2,3},{3,2},{4,5},{5,4},{6,7},{7,6},{8,9},{9,8},{10,11... | collective-permute-start | bytes 11796488 | tf_op jit(solution)/shard_map/ppermute | solution.py:642
  6.5 2.7 %collective-permute-start.1 = (bf16[64,5120]{1,0:T(8,128)(2,1)S(1)}, bf16[64,5120]{1,0:T(8,128)(2,1)S(1)}, u32[]{:S(2)}, u32[]{:S(2)}) collective-permute-start(bf16[64,5120]{1,0:T(8,128)(2,1)S(1)} %shard_map.131.refs_0_), channel_id=1, source_target_pairs={{0,6},{1,7},{2,0},{3,1},{4,2},{5,3},{6,4},{7,5},{8,14},{9,15},{10,... | collective-permute-start | bytes 1966088 | tf_op jit(solution)/shard_map/ppermute | solution.py:639
  9.8 1.2 %shard_map.132 = (bf16[32,5120]{1,0:T(8,128)(2,1)S(1)}, f32[32,128]{1,0:T(8,128)S(1)}, f32[32,128]{1,0:T(8,128)S(1)}, bf16[128,128]{1,0:T(8,128)(2,1)S(1)}, bf16[128,128]{1,0:T(8,128)(2,1)S(1)}) custom-call(s32[1]{0:T(128)} %bitcast.2.grp.where, bf16[16,2,5120]{2,1,0:T(2,128)(2,1)S(1)} %bitcast.11, f32[1,5120]{1,0:T(1,128)S(1)} %bitcast.14, ...), custom_call_target="tpu_custom_call" | custom-call | flops 5400000000 | tf_op jit(solution)/shard_map/pallas_call | solution.py:39
  12.7 1.8 %shard_map.133 = (bf16[32,384]{1,0:T(8,128)(2,1)S(1)}, bf16[32,256]{1,0:T(8,128)(2,1)S(1)}, bf16[5120,640]{1,0:T(8,128)(2,1)S(1)}) custom-call(bf16[32,5120]{1,0:T(8,128)(2,1)S(1)} %get-tuple-element.42.x, bf16[5120,384]{1,0:T(8,128)(2,1)S(1)} %copy-done.1, bf16[5120,128]{1,0:T(8,128)(2,1)S(1)} %copy-done.3, bf16[5120,128]{1,0:T(8,128)(2,1)S(1)} %copy-done.4, ...), custom_call_target="tpu_custom_call" | custom-call | flops 900000000 | tf_op jit(solution)/shard_map/pallas_call | solution.py:39
  14.5 5.3 %collective-permute-start.2 = (bf16[32,384]{1,0:T(8,128)(2,1)S(1)}, bf16[32,384]{1,0:T(8,128)(2,1)S(1)}, u32[]{:S(2)}, u32[]{:S(2)}) collective-permute-start(bf16[32,384]{1,0:T(8,128)(2,1)S(1)} %get-tuple-element.45.a.q), channel_id=1, source_target_pairs={{0,32},{8,40},{16,48},{24,56},{32,0},{40,8},{48,16},{56,24},{64,96... | collective-permute-start | bytes 73736 | tf_op jit(solution)/shard_map/ppermute | solution.py:642
  19.7 1.4 %collective-permute-done.2.b = bf16[32,384]{1,0:T(8,128)(2,1)S(1)} collective-permute-done((bf16[32,384]{1,0:T(8,128)(2,1)S(1)}, bf16[32,384]{1,0:T(8,128)(2,1)S(1)}, u32[]{:S(2)}, u32[]{:S(2)}) %collective-permute-start.2) | collective-permute-done | bytes 24608 | tf_op jit(solution)/shard_map/ppermute | solution.py:642
  22.0 2.4 %collective-permute-done.3.far = bf16[64,384]{1,0:T(8,128)(2,1)S(1)} collective-permute-done((bf16[64,384]{1,0:T(8,128)(2,1)S(1)}, bf16[64,384]{1,0:T(8,128)(2,1)S(1)}, u32[]{:S(2)}, u32[]{:S(2)}) %collective-permute-start.3) | collective-permute-done | bytes 49184 | tf_op jit(solution)/shard_map/ppermute | solution.py:642
  24.6 1.3 %shard_map.136 = (bf16[128,384]{1,0:T(8,128)(2,1)S(1)}, bf16[128,256]{1,0:T(8,128)(2,1)S(1)}) custom-call(bf16[64,5120]{1,0:T(8,128)(2,1)S(1)} %shard_map.131.refs_0_, bf16[64,5120]{1,0:T(8,128)(2,1)S(1)} %collective-permute-done.4.refs_1_, bf16[5120,640]{1,0:T(8,128)(2,1)S(1)} %get-tuple-element.47.refs_2_.refs_4_, f32[512,256]{1,0:T(8,128)S(1)} %copy-done, ...), custom_call_target="tpu_custom_call" | custom-call | flops 900000000 | tf_op jit(solution)/shard_map/pallas_call | solution.py:39
  25.9 2.1 %collective-permute-start.5 = (bf16[64,5120]{1,0:T(8,128)(2,1)S(1)}, bf16[64,5120]{1,0:T(8,128)(2,1)S(1)}, u32[]{:S(2)}, u32[]{:S(2)}) collective-permute-start(bf16[64,5120]{1,0:T(8,128)(2,1)S(1)} %get-tuple-element.49.refs_0_.a), channel_id=1, source_target_pairs={{0,1},{1,0},{2,3},{3,2},{4,5},{5,4},{6,7},{7,6},{8,9},{9,8},{10,11... | collective-permute-start | bytes 1966088 | tf_op jit(solution)/shard_map/ppermute | solution.py:642
  28.2 2.7 %collective-permute-start.8 = (bf16[32,5120]{1,0:T(8,128)(2,1)S(1)}, bf16[32,5120]{1,0:T(8,128)(2,1)S(1)}, u32[]{:S(2)}, u32[]{:S(2)}) collective-permute-start(bf16[32,5120]{1,0:T(8,128)(2,1)S(1)} %get-tuple-element.54), channel_id=1, source_target_pairs={{0,6},{1,7},{2,0},{3,1},{4,2},{5,3},{6,4},{7,5},{8,14},{9,15},{10,... | collective-permute-start | bytes 983048 | tf_op jit(solution)/shard_map/ppermute | solution.py:639
  30.9 2.3 %shard_map.138 = (bf16[384,384]{1,0:T(8,128)(2,1)S(1)}, bf16[384,256]{1,0:T(8,128)(2,1)S(1)}) custom-call(bf16[64,5120]{1,0:T(8,128)(2,1)S(1)} %get-tuple-element.49.refs_0_.a, bf16[64,5120]{1,0:T(8,128)(2,1)S(1)} %get-tuple-element.50.refs_1_.b, bf16[64,5120]{1,0:T(8,128)(2,1)S(1)} %collective-permute-done.5.refs_2_, ...), custom_call_target="tpu_custom_call" | custom-call | tf_op jit(solution)/shard_map/pallas_call | solution.py:39
  33.2 2.4 %shard_map.140.refs_2_.w = bf16[768,5120]{1,0:T(8,128)(2,1)S(1)} custom-call(bf16[384,5120]{1,0:T(8,128)(2,1)S(1)} %copy-done.2, bf16[384,5120]{1,0:T(8,128)(2,1)} %collective-permute-done.9.other, bf16[384,256]{1,0:T(8,128)(2,1)S(1)} %get-tuple-element.55.rest_0_.kv_a), custom_call_target="tpu_custom_call" | custom-call | tf_op jit(solution)/shard_map/pallas_call | solution.py:39
  35.6 2.7 %collective-permute-done.7.refs_0_ = bf16[32,5120]{1,0:T(8,128)(2,1)S(1)} collective-permute-done((bf16[32,5120]{1,0:T(8,128)(2,1)S(1)}, bf16[32,5120]{1,0:T(8,128)(2,1)S(1)}, u32[]{:S(2)}, u32[]{:S(2)}) %collective-permute-start.7) | collective-permute-done | bytes 327712 | tf_op jit(solution)/shard_map/ppermute | solution.py:639
  38.3 1.2 %collective-permute-start.10 = (bf16[32,5120]{1,0:T(8,128)(2,1)S(1)}, bf16[32,5120]{1,0:T(8,128)(2,1)S(1)}, u32[]{:S(2)}, u32[]{:S(2)}) collective-permute-start(bf16[32,5120]{1,0:T(8,128)(2,1)S(1)} %get-tuple-element.56.refs_0_), channel_id=1, source_target_pairs={{0,1},{1,0},{2,3},{3,2},{4,5},{5,4},{6,7},{7,6},{8,9},{9,8},{10,11... | collective-permute-start | bytes 983048 | tf_op jit(solution)/shard_map/ppermute | solution.py:642
  40.6 2.1 %collective-permute-start.13 = (bf16[64,384]{1,0:T(8,128)(2,1)S(1)}, bf16[64,384]{1,0:T(8,128)(2,1)S(1)}, u32[]{:S(2)}, u32[]{:S(2)}) collective-permute-start(bf16[64,384]{1,0:T(8,128)(2,1)S(1)} %get-tuple-element.46.refs_2_), channel_id=1, source_target_pairs={{0,16},{8,24},{16,0},{24,8},{32,48},{40,56},{48,32},{56,40},{64,80... | collective-permute-start | bytes 147464 | tf_op jit(solution)/shard_map/ppermute | solution.py:642
  42.7 1.3 %shard_map.142 = (bf16[128,384]{1,0:T(8,128)(2,1)S(1)}, bf16[128,256]{1,0:T(8,128)(2,1)S(1)}) custom-call(bf16[32,5120]{1,0:T(8,128)(2,1)S(1)} %get-tuple-element.56.refs_0_, bf16[32,5120]{1,0:T(8,128)(2,1)S(1)} %get-tuple-element.57.refs_1_, bf16[32,5120]{1,0:T(8,128)(2,1)S(1)} %collective-permute-done.10.refs_2_, ...), custom_call_target="tpu_custom_call" | custom-call | tf_op jit(solution)/shard_map/pallas_call | solution.py:39
  44.4 2.7 %collective-permute-start.14 = (bf16[32,384]{1,0:T(8,128)(2,1)S(1)}, bf16[32,384]{1,0:T(8,128)(2,1)S(1)}, u32[]{:S(2)}, u32[]{:S(2)}) collective-permute-start(bf16[32,384]{1,0:T(8,128)(2,1)S(1)} %shard_map.144), channel_id=1, source_target_pairs={{0,64},{8,72},{16,80},{24,88},{32,96},{40,104},{48,112},{56,120},{... | collective-permute-start | bytes 73736 | tf_op jit(solution)/shard_map/ppermute | solution.py:642
  47.2 1.5 %shard_map.143 = (bf16[256,384]{1,0:T(8,128)(2,1)S(1)}, bf16[256,384]{1,0:T(8,128)(2,1)S(1)}) custom-call(bf16[384,384]{1,0:T(8,128)(2,1)S(1)} %get-tuple-element.52.q_a, bf16[128,384]{1,0:T(8,128)(2,1)S(1)} %get-tuple-element.58.q_b, bf16[384,256]{1,0:T(8,128)(2,1)S(1)} %get-tuple-element.55.rest_0_.kv_a, bf16[128,256]{1,0:T(8,128)(2,1)S(1)} %get-tuple-element.59.kv_b, ...), custom_call_target="tpu_custom_call" | custom-call | flops 402653184 | tf_op jit(solution)/shard_map/pallas_call | solution.py:39
  48.6 2.4 %collective-permute-start.12 = (bf16[256,384]{1,0:T(8,128)(2,1)S(1)}, bf16[256,384]{1,0:T(8,128)(2,1)S(1)}, u32[]{:S(2)}, u32[]{:S(2)}) collective-permute-start(bf16[256,384]{1,0:T(8,128)(2,1)S(1)} %get-tuple-element.61), channel_id=1, source_target_pairs={{0,1},{1,0},{2,3},{3,2},{4,5},{5,4},{6,7},{7,6},{8,9},{9,8},{10,11... | collective-permute-start | bytes 589832 | tf_op jit(solution)/shard_map/ppermute | solution.py:642
  51.5 5.1 %collective-permute-start.18 = (bf16[32,512]{1,0:T(8,128)(2,1)S(1)}, bf16[32,512]{1,0:T(8,128)(2,1)S(1)}, u32[]{:S(2)}, u32[]{:S(2)}) collective-permute-start(bf16[32,512]{1,0:T(8,128)(2,1)S(1)} %shard_map.145.rest_0_.a), channel_id=1, source_target_pairs={{0,32},{8,40},{16,48},{24,56},{32,0},{40,8},{48,16},{56,24},{64,96... | collective-permute-start | bytes 98312 | tf_op jit(solution)/shard_map/ppermute | solution.py:642
  56.6 1.7 %collective-permute-done.18.b = bf16[32,512]{1,0:T(8,128)(2,1)S(1)} collective-permute-done((bf16[32,512]{1,0:T(8,128)(2,1)S(1)}, bf16[32,512]{1,0:T(8,128)(2,1)S(1)}, u32[]{:S(2)}, u32[]{:S(2)}) %collective-permute-start.18) | collective-permute-done | bytes 32800 | tf_op jit(solution)/shard_map/ppermute | solution.py:642
  58.8 2.3 %shard_map.146 = (bf16[64,5120]{1,0:T(8,128)(2,1)S(1)}, bf16[64,5120]{1,0:T(8,128)(2,1)S(1)}, bf16[64,5120]{1,0:T(8,128)(2,1)S(1)}, bf16[32,5120]{1,0:T(8,128)(2,1)S(1)}, bf16[32,5120]{1,0:T(8,128)(2,1)S(1)}) custom-call(bf16[256,384]{1,0:T(8,128)(2,1)S(1)} %get-tuple-element.60.after.own, bf16[256,384]{1,0:T(8,128)(2,1)S(1)} %collective-permute-done.12.other, ...), custom_call_target="tpu_custom_call" | custom-call | tf_op jit(solution)/shard_map/pallas_call | solution.py:39
  61.3 2.7 %collective-permute-start.22 = (bf16[32,5120]{1,0:T(8,128)(2,1)S(1)}, bf16[32,5120]{1,0:T(8,128)(2,1)S(1)}, u32[]{:S(2)}, u32[]{:S(2)}) collective-permute-start(bf16[32,5120]{1,0:T(8,128)(2,1)S(1)} %get-tuple-element.73), channel_id=1, source_target_pairs={{0,6},{1,7},{2,0},{3,1},{4,2},{5,3},{6,4},{7,5},{8,14},{9,15},{10,... | collective-permute-start | bytes 983048 | tf_op jit(solution)/shard_map/ppermute | solution.py:639
  65.0 2.9 %collective-permute-start.20 = (bf16[64,512]{1,0:T(8,128)(2,1)S(1)}, bf16[64,512]{1,0:T(8,128)(2,1)S(1)}, u32[]{:S(2)}, u32[]{:S(2)}) collective-permute-start(bf16[64,512]{1,0:T(8,128)(2,1)S(1)} %get-tuple-element.71), channel_id=1, source_target_pairs={{0,16},{8,24},{16,0},{24,8},{32,48},{40,56},{48,32},{56,40},{64,80... | collective-permute-start | bytes 196616 | tf_op jit(solution)/shard_map/ppermute | solution.py:642
  67.9 2.7 %collective-permute-done.20.came = bf16[64,512]{1,0:T(8,128)(2,1)S(1)} collective-permute-done((bf16[64,512]{1,0:T(8,128)(2,1)S(1)}, bf16[64,512]{1,0:T(8,128)(2,1)S(1)}, u32[]{:S(2)}, u32[]{:S(2)}) %collective-permute-start.20) | collective-permute-done | bytes 65568 | tf_op jit(solution)/shard_map/ppermute | solution.py:642
  71.4 2.7 %collective-permute-start.23 = (bf16[64,5120]{1,0:T(8,128)(2,1)S(1)}, bf16[64,5120]{1,0:T(8,128)(2,1)S(1)}, u32[]{:S(2)}, u32[]{:S(2)}) collective-permute-start(bf16[64,5120]{1,0:T(8,128)(2,1)S(1)} %shard_map.152.rest_1_), channel_id=1, source_target_pairs={{0,6},{1,7},{2,0},{3,1},{4,2},{5,3},{6,4},{7,5},{8,14},{9,15},{10,... | collective-permute-start | bytes 1966088 | tf_op jit(solution)/shard_map/ppermute | solution.py:639
  76.0 5.7 %collective-permute-start.25 = (bf16[16,5120]{1,0:T(8,128)(2,1)S(1)}, bf16[16,5120]{1,0:T(8,128)(2,1)S(1)}, u32[]{:S(2)}, u32[]{:S(2)}) collective-permute-start(bf16[16,5120]{1,0:T(8,128)(2,1)S(1)} %get-tuple-element.78), channel_id=1, source_target_pairs={{0,1},{1,0},{2,3},{3,2},{4,5},{5,4},{6,7},{7,6},{8,9},{9,8},{10,11... | collective-permute-start | bytes 491528 | tf_op jit(solution)/shard_map/ppermute | solution.py:642
  84.0 1.6 %collective-permute-start.28 = (bf16[16,5120]{1,0:T(8,128)(2,1)S(1)}, bf16[16,5120]{1,0:T(8,128)(2,1)S(1)}, u32[]{:S(2)}, u32[]{:S(2)}) collective-permute-start(bf16[16,5120]{1,0:T(8,128)(2,1)S(1)} %shard_map.156.own), channel_id=1, source_target_pairs={{0,6},{1,7},{2,0},{3,1},{4,2},{5,3},{6,4},{7,5},{8,14},{9,15},{10,... | collective-permute-start | bytes 491528 | tf_op jit(solution)/shard_map/ppermute | solution.py:639
  86.8 3.8 %collective-permute-done.26.far = bf16[16,5120]{1,0:T(8,128)(2,1)S(1)} collective-permute-done((bf16[16,5120]{1,0:T(8,128)(2,1)S(1)}, bf16[16,5120]{1,0:T(8,128)(2,1)S(1)}, u32[]{:S(2)}, u32[]{:S(2)}) %collective-permute-start.26) | collective-permute-done | bytes 163872 | tf_op jit(solution)/shard_map/ppermute | solution.py:639
  90.6 3.2 %collective-permute-done.27.down = bf16[16,5120]{1,0:T(8,128)(2,1)S(1)} collective-permute-done((bf16[16,5120]{1,0:T(8,128)(2,1)S(1)}, bf16[16,5120]{1,0:T(8,128)(2,1)S(1)}, u32[]{:S(2)}, u32[]{:S(2)}) %collective-permute-start.27) | collective-permute-done | bytes 163872 | tf_op jit(solution)/shard_map/ppermute | solution.py:639
  94.0 2.8 %collective-permute-start.29 = (f32[16,5120]{1,0:T(8,128)S(1)}, f32[16,5120]{1,0:T(8,128)S(1)}, u32[]{:S(2)}, u32[]{:S(2)}) collective-permute-start(f32[16,5120]{1,0:T(8,128)S(1)} %shard_map.157.kept), channel_id=1, source_target_pairs={{0,1},{1,0},{2,3},{3,2},{4,5},{5,4},{6,7},{7,6},{8,9},{9,8},{10,11... | collective-permute-start | bytes 983048 | tf_op jit(solution)/shard_map/ppermute | solution.py:642
  96.8 1.3 %collective-permute-done.29.taken = f32[16,5120]{1,0:T(8,128)S(1)} collective-permute-done((f32[16,5120]{1,0:T(8,128)S(1)}, f32[16,5120]{1,0:T(8,128)S(1)}, u32[]{:S(2)}, u32[]{:S(2)}) %collective-permute-start.29) | collective-permute-done | bytes 327712 | tf_op jit(solution)/shard_map/ppermute | solution.py:642
  (84 shorter events, 17.0 us)
Async XLA Ops:
  0.6 32.6 %collective-permute-start.9 = (bf16[384,5120]{1,0:T(8,128)(2,1)}, bf16[384,5120]{1,0:T(8,128)(2,1)}, u32[]{:S(2)}, u32[]{:S(2)}) collective-permute-start(bf16[384,5120]{1,0:T(8,128)(2,1)} %own.1), channel_id=1, source_target_pairs={{0,1},{1,0},{2,3},{3,2},{4,5},{5,4},{6,7},{7,6},{8,9},{9,8},{10,11... | collective-permute-start | bytes 11796488 | tf_op jit(solution)/shard_map/ppermute | solution.py:642
  6.4 19.5 %collective-permute-start = (bf16[64,5120]{1,0:T(8,128)(2,1)S(1)}, bf16[64,5120]{1,0:T(8,128)(2,1)S(1)}, u32[]{:S(2)}, u32[]{:S(2)}) collective-permute-start(bf16[64,5120]{1,0:T(8,128)(2,1)S(1)} %shard_map.131.refs_0_), channel_id=1, source_target_pairs={{0,2},{1,3},{2,4},{3,5},{4,6},{5,7},{6,0},{7,1},{8,10},{9,11},{10,... | collective-permute-start | bytes 1966088 | tf_op jit(solution)/shard_map/ppermute | solution.py:639
  6.5 19.4 %collective-permute-start.1 = (bf16[64,5120]{1,0:T(8,128)(2,1)S(1)}, bf16[64,5120]{1,0:T(8,128)(2,1)S(1)}, u32[]{:S(2)}, u32[]{:S(2)}) collective-permute-start(bf16[64,5120]{1,0:T(8,128)(2,1)S(1)} %shard_map.131.refs_0_), channel_id=1, source_target_pairs={{0,6},{1,7},{2,0},{3,1},{4,2},{5,3},{6,4},{7,5},{8,14},{9,15},{10,... | collective-permute-start | bytes 1966088 | tf_op jit(solution)/shard_map/ppermute | solution.py:639
  9.2 15.4 %collective-permute-start.4 = (bf16[64,5120]{1,0:T(8,128)(2,1)S(1)}, bf16[64,5120]{1,0:T(8,128)(2,1)S(1)}, u32[]{:S(2)}, u32[]{:S(2)}) collective-permute-start(bf16[64,5120]{1,0:T(8,128)(2,1)S(1)} %shard_map.131.refs_0_), channel_id=1, source_target_pairs={{0,1},{1,0},{2,3},{3,2},{4,5},{5,4},{6,7},{7,6},{8,9},{9,8},{10,11... | collective-permute-start | bytes 1966088 | tf_op jit(solution)/shard_map/ppermute | solution.py:642
  11.0 13.6 %copy-start = (f32[512,256]{1,0:T(8,128)S(1)}, f32[512,256]{1,0:T(8,128)}, u32[]{:S(2)}) copy-start(f32[512,256]{1,0:T(8,128)} %constant.14.clone.refs_3_.refs_5_) | copy-start | bytes 1572868
  14.5 6.7 %collective-permute-start.2 = (bf16[32,384]{1,0:T(8,128)(2,1)S(1)}, bf16[32,384]{1,0:T(8,128)(2,1)S(1)}, u32[]{:S(2)}, u32[]{:S(2)}) collective-permute-start(bf16[32,384]{1,0:T(8,128)(2,1)S(1)} %get-tuple-element.45.a.q), channel_id=1, source_target_pairs={{0,32},{8,40},{16,48},{24,56},{32,0},{40,8},{48,16},{56,24},{64,96... | collective-permute-start | bytes 73736 | tf_op jit(solution)/shard_map/ppermute | solution.py:642
  21.2 3.2 %collective-permute-start.3 = (bf16[64,384]{1,0:T(8,128)(2,1)S(1)}, bf16[64,384]{1,0:T(8,128)(2,1)S(1)}, u32[]{:S(2)}, u32[]{:S(2)}) collective-permute-start(bf16[64,384]{1,0:T(8,128)(2,1)S(1)} %shard_map.134.near), channel_id=1, source_target_pairs={{0,8},{8,0},{16,24},{24,16},{32,40},{40,32},{48,56},{56,48},{64,72... | collective-permute-start | bytes 147464 | tf_op jit(solution)/shard_map/ppermute | solution.py:642
  25.9 5.0 %collective-permute-start.5 = (bf16[64,5120]{1,0:T(8,128)(2,1)S(1)}, bf16[64,5120]{1,0:T(8,128)(2,1)S(1)}, u32[]{:S(2)}, u32[]{:S(2)}) collective-permute-start(bf16[64,5120]{1,0:T(8,128)(2,1)S(1)} %get-tuple-element.49.refs_0_.a), channel_id=1, source_target_pairs={{0,1},{1,0},{2,3},{3,2},{4,5},{5,4},{6,7},{7,6},{8,9},{9,8},{10,11... | collective-permute-start | bytes 1966088 | tf_op jit(solution)/shard_map/ppermute | solution.py:642
  28.0 2.9 %collective-permute-start.6 = (bf16[64,5120]{1,0:T(8,128)(2,1)S(1)}, bf16[64,5120]{1,0:T(8,128)(2,1)S(1)}, u32[]{:S(2)}, u32[]{:S(2)}) collective-permute-start(bf16[64,5120]{1,0:T(8,128)(2,1)S(1)} %get-tuple-element.50.refs_1_.b), channel_id=1, source_target_pairs={{0,1},{1,0},{2,3},{3,2},{4,5},{5,4},{6,7},{7,6},{8,9},{9,8},{10,11... | collective-permute-start | bytes 1966088 | tf_op jit(solution)/shard_map/ppermute | solution.py:642
  28.2 10.2 %collective-permute-start.7 = (bf16[32,5120]{1,0:T(8,128)(2,1)S(1)}, bf16[32,5120]{1,0:T(8,128)(2,1)S(1)}, u32[]{:S(2)}, u32[]{:S(2)}) collective-permute-start(bf16[32,5120]{1,0:T(8,128)(2,1)S(1)} %get-tuple-element.53), channel_id=1, source_target_pairs={{0,2},{1,3},{2,4},{3,5},{4,6},{5,7},{6,0},{7,1},{8,10},{9,11},{10,... | collective-permute-start | bytes 983048 | tf_op jit(solution)/shard_map/ppermute | solution.py:639
  28.2 10.1 %collective-permute-start.8 = (bf16[32,5120]{1,0:T(8,128)(2,1)S(1)}, bf16[32,5120]{1,0:T(8,128)(2,1)S(1)}, u32[]{:S(2)}, u32[]{:S(2)}) collective-permute-start(bf16[32,5120]{1,0:T(8,128)(2,1)S(1)} %get-tuple-element.54), channel_id=1, source_target_pairs={{0,6},{1,7},{2,0},{3,1},{4,2},{5,3},{6,4},{7,5},{8,14},{9,15},{10,... | collective-permute-start | bytes 983048 | tf_op jit(solution)/shard_map/ppermute | solution.py:639
  38.3 4.4 %collective-permute-start.10 = (bf16[32,5120]{1,0:T(8,128)(2,1)S(1)}, bf16[32,5120]{1,0:T(8,128)(2,1)S(1)}, u32[]{:S(2)}, u32[]{:S(2)}) collective-permute-start(bf16[32,5120]{1,0:T(8,128)(2,1)S(1)} %get-tuple-element.56.refs_0_), channel_id=1, source_target_pairs={{0,1},{1,0},{2,3},{3,2},{4,5},{5,4},{6,7},{7,6},{8,9},{9,8},{10,11... | collective-permute-start | bytes 983048 | tf_op jit(solution)/shard_map/ppermute | solution.py:642
  39.6 3.2 %collective-permute-start.11 = (bf16[32,5120]{1,0:T(8,128)(2,1)S(1)}, bf16[32,5120]{1,0:T(8,128)(2,1)S(1)}, u32[]{:S(2)}, u32[]{:S(2)}) collective-permute-start(bf16[32,5120]{1,0:T(8,128)(2,1)S(1)} %get-tuple-element.57.refs_1_), channel_id=1, source_target_pairs={{0,1},{1,0},{2,3},{3,2},{4,5},{5,4},{6,7},{7,6},{8,9},{9,8},{10,11... | collective-permute-start | bytes 983048 | tf_op jit(solution)/shard_map/ppermute | solution.py:642
  39.7 11.4 %collective-permute-start.15 = (bf16[384,256]{1,0:T(8,128)(2,1)S(1)}, bf16[384,256]{1,0:T(8,128)(2,1)S(1)}, u32[]{:S(2)}, u32[]{:S(2)}) collective-permute-start(bf16[384,256]{1,0:T(8,128)(2,1)S(1)} %get-tuple-element.55.rest_0_.kv_a), channel_id=1, source_target_pairs={{0,128},{128,0},{1,129},{129,1},{2,130},{130,2},{3,131},{131,3},{4... | collective-permute-start | bytes 589832 | tf_op jit(solution)/shard_map/ppermute | solution.py:642
  40.6 3.8 %collective-permute-start.13 = (bf16[64,384]{1,0:T(8,128)(2,1)S(1)}, bf16[64,384]{1,0:T(8,128)(2,1)S(1)}, u32[]{:S(2)}, u32[]{:S(2)}) collective-permute-start(bf16[64,384]{1,0:T(8,128)(2,1)S(1)} %get-tuple-element.46.refs_2_), channel_id=1, source_target_pairs={{0,16},{8,24},{16,0},{24,8},{32,48},{40,56},{48,32},{56,40},{64,80... | collective-permute-start | bytes 147464 | tf_op jit(solution)/shard_map/ppermute | solution.py:642
  44.0 7.1 %collective-permute-start.16 = (bf16[128,256]{1,0:T(8,128)(2,1)S(1)}, bf16[128,256]{1,0:T(8,128)(2,1)S(1)}, u32[]{:S(2)}, u32[]{:S(2)}) collective-permute-start(bf16[128,256]{1,0:T(8,128)(2,1)S(1)} %get-tuple-element.59.kv_b), channel_id=1, source_target_pairs={{0,128},{128,0},{1,129},{129,1},{2,130},{130,2},{3,131},{131,3},{4... | collective-permute-start | bytes 196616 | tf_op jit(solution)/shard_map/ppermute | solution.py:642
  44.4 6.7 %collective-permute-start.14 = (bf16[32,384]{1,0:T(8,128)(2,1)S(1)}, bf16[32,384]{1,0:T(8,128)(2,1)S(1)}, u32[]{:S(2)}, u32[]{:S(2)}) collective-permute-start(bf16[32,384]{1,0:T(8,128)(2,1)S(1)} %shard_map.144), channel_id=1, source_target_pairs={{0,64},{8,72},{16,80},{24,88},{32,96},{40,104},{48,112},{56,120},{... | collective-permute-start | bytes 73736 | tf_op jit(solution)/shard_map/ppermute | solution.py:642
  48.6 10.2 %collective-permute-start.12 = (bf16[256,384]{1,0:T(8,128)(2,1)S(1)}, bf16[256,384]{1,0:T(8,128)(2,1)S(1)}, u32[]{:S(2)}, u32[]{:S(2)}) collective-permute-start(bf16[256,384]{1,0:T(8,128)(2,1)S(1)} %get-tuple-element.61), channel_id=1, source_target_pairs={{0,1},{1,0},{2,3},{3,2},{4,5},{5,4},{6,7},{7,6},{8,9},{9,8},{10,11... | collective-permute-start | bytes 589832 | tf_op jit(solution)/shard_map/ppermute | solution.py:642
  51.5 6.8 %collective-permute-start.18 = (bf16[32,512]{1,0:T(8,128)(2,1)S(1)}, bf16[32,512]{1,0:T(8,128)(2,1)S(1)}, u32[]{:S(2)}, u32[]{:S(2)}) collective-permute-start(bf16[32,512]{1,0:T(8,128)(2,1)S(1)} %shard_map.145.rest_0_.a), channel_id=1, source_target_pairs={{0,32},{8,40},{16,48},{24,56},{32,0},{40,8},{48,16},{56,24},{64,96... | collective-permute-start | bytes 98312 | tf_op jit(solution)/shard_map/ppermute | solution.py:642
  58.3 6.6 %collective-permute-start.19 = (bf16[64,512]{1,0:T(8,128)(2,1)S(1)}, bf16[64,512]{1,0:T(8,128)(2,1)S(1)}, u32[]{:S(2)}, u32[]{:S(2)}) collective-permute-start(bf16[64,512]{1,0:T(8,128)(2,1)S(1)} %shard_map.147.after.near), channel_id=1, source_target_pairs={{0,8},{8,0},{16,24},{24,16},{32,40},{40,32},{48,56},{56,48},{64,72... | collective-permute-start | bytes 196616 | tf_op jit(solution)/shard_map/ppermute | solution.py:642
  61.1 10.0 %collective-permute-start.17 = (bf16[32,5120]{1,0:T(8,128)(2,1)S(1)}, bf16[32,5120]{1,0:T(8,128)(2,1)S(1)}, u32[]{:S(2)}, u32[]{:S(2)}) collective-permute-start(bf16[32,5120]{1,0:T(8,128)(2,1)S(1)} %get-tuple-element.66), channel_id=1, source_target_pairs={{0,2},{1,3},{2,4},{3,5},{4,6},{5,7},{6,0},{7,1},{8,10},{9,11},{10,... | collective-permute-start | bytes 983048 | tf_op jit(solution)/shard_map/ppermute | solution.py:639
  61.3 10.0 %collective-permute-start.22 = (bf16[32,5120]{1,0:T(8,128)(2,1)S(1)}, bf16[32,5120]{1,0:T(8,128)(2,1)S(1)}, u32[]{:S(2)}, u32[]{:S(2)}) collective-permute-start(bf16[32,5120]{1,0:T(8,128)(2,1)S(1)} %get-tuple-element.73), channel_id=1, source_target_pairs={{0,6},{1,7},{2,0},{3,1},{4,2},{5,3},{6,4},{7,5},{8,14},{9,15},{10,... | collective-permute-start | bytes 983048 | tf_op jit(solution)/shard_map/ppermute | solution.py:639
  65.0 5.5 %collective-permute-start.20 = (bf16[64,512]{1,0:T(8,128)(2,1)S(1)}, bf16[64,512]{1,0:T(8,128)(2,1)S(1)}, u32[]{:S(2)}, u32[]{:S(2)}) collective-permute-start(bf16[64,512]{1,0:T(8,128)(2,1)S(1)} %get-tuple-element.71), channel_id=1, source_target_pairs={{0,16},{8,24},{16,0},{24,8},{32,48},{40,56},{48,32},{56,40},{64,80... | collective-permute-start | bytes 196616 | tf_op jit(solution)/shard_map/ppermute | solution.py:642
  70.6 4.3 %collective-permute-start.24 = (bf16[32,512]{1,0:T(8,128)(2,1)S(1)}, bf16[32,512]{1,0:T(8,128)(2,1)S(1)}, u32[]{:S(2)}, u32[]{:S(2)}) collective-permute-start(bf16[32,512]{1,0:T(8,128)(2,1)S(1)} %shard_map.150.rest_0_), channel_id=1, source_target_pairs={{0,64},{8,72},{16,80},{24,88},{32,96},{40,104},{48,112},{56,120},{... | collective-permute-start | bytes 98312 | tf_op jit(solution)/shard_map/ppermute | solution.py:642
  71.2 14.4 %collective-permute-start.21 = (bf16[64,5120]{1,0:T(8,128)(2,1)S(1)}, bf16[64,5120]{1,0:T(8,128)(2,1)S(1)}, u32[]{:S(2)}, u32[]{:S(2)}) collective-permute-start(bf16[64,5120]{1,0:T(8,128)(2,1)S(1)} %shard_map.151.rest_0_), channel_id=1, source_target_pairs={{0,2},{1,3},{2,4},{3,5},{4,6},{5,7},{6,0},{7,1},{8,10},{9,11},{10,... | collective-permute-start | bytes 1966088 | tf_op jit(solution)/shard_map/ppermute | solution.py:639
  71.4 14.2 %collective-permute-start.23 = (bf16[64,5120]{1,0:T(8,128)(2,1)S(1)}, bf16[64,5120]{1,0:T(8,128)(2,1)S(1)}, u32[]{:S(2)}, u32[]{:S(2)}) collective-permute-start(bf16[64,5120]{1,0:T(8,128)(2,1)S(1)} %shard_map.152.rest_1_), channel_id=1, source_target_pairs={{0,6},{1,7},{2,0},{3,1},{4,2},{5,3},{6,4},{7,5},{8,14},{9,15},{10,... | collective-permute-start | bytes 1966088 | tf_op jit(solution)/shard_map/ppermute | solution.py:639
  76.0 9.6 %copy-start.7 = (bf16[1,1,64,5120]{3,2,1,0:T(8,128)(2,1)S(1)}, bf16[1,1,64,5120]{3,2,1,0:T(8,128)(2,1)}, u32[]{:S(2)}) copy-start(bf16[1,1,64,5120]{3,2,1,0:T(8,128)(2,1)} %param.12) | copy-start | bytes 1966084
  76.0 6.7 %collective-permute-start.25 = (bf16[16,5120]{1,0:T(8,128)(2,1)S(1)}, bf16[16,5120]{1,0:T(8,128)(2,1)S(1)}, u32[]{:S(2)}, u32[]{:S(2)}) collective-permute-start(bf16[16,5120]{1,0:T(8,128)(2,1)S(1)} %get-tuple-element.78), channel_id=1, source_target_pairs={{0,1},{1,0},{2,3},{3,2},{4,5},{5,4},{6,7},{7,6},{8,9},{9,8},{10,11... | collective-permute-start | bytes 491528 | tf_op jit(solution)/shard_map/ppermute | solution.py:642
  82.8 7.9 %collective-permute-start.26 = (bf16[16,5120]{1,0:T(8,128)(2,1)S(1)}, bf16[16,5120]{1,0:T(8,128)(2,1)S(1)}, u32[]{:S(2)}, u32[]{:S(2)}) collective-permute-start(bf16[16,5120]{1,0:T(8,128)(2,1)S(1)} %shard_map.156.own), channel_id=1, source_target_pairs={{0,4},{1,5},{2,6},{3,7},{4,0},{5,1},{6,2},{7,3},{8,12},{9,13},{10,... | collective-permute-start | bytes 491528 | tf_op jit(solution)/shard_map/ppermute | solution.py:639
  82.9 11.0 %collective-permute-start.27 = (bf16[16,5120]{1,0:T(8,128)(2,1)S(1)}, bf16[16,5120]{1,0:T(8,128)(2,1)S(1)}, u32[]{:S(2)}, u32[]{:S(2)}) collective-permute-start(bf16[16,5120]{1,0:T(8,128)(2,1)S(1)} %shard_map.156.own), channel_id=1, source_target_pairs={{0,2},{1,3},{2,4},{3,5},{4,6},{5,7},{6,0},{7,1},{8,10},{9,11},{10,... | collective-permute-start | bytes 491528 | tf_op jit(solution)/shard_map/ppermute | solution.py:639
  84.0 9.9 %collective-permute-start.28 = (bf16[16,5120]{1,0:T(8,128)(2,1)S(1)}, bf16[16,5120]{1,0:T(8,128)(2,1)S(1)}, u32[]{:S(2)}, u32[]{:S(2)}) collective-permute-start(bf16[16,5120]{1,0:T(8,128)(2,1)S(1)} %shard_map.156.own), channel_id=1, source_target_pairs={{0,6},{1,7},{2,0},{3,1},{4,2},{5,3},{6,4},{7,5},{8,14},{9,15},{10,... | collective-permute-start | bytes 491528 | tf_op jit(solution)/shard_map/ppermute | solution.py:639
  94.0 4.1 %collective-permute-start.29 = (f32[16,5120]{1,0:T(8,128)S(1)}, f32[16,5120]{1,0:T(8,128)S(1)}, u32[]{:S(2)}, u32[]{:S(2)}) collective-permute-start(f32[16,5120]{1,0:T(8,128)S(1)} %shard_map.157.kept), channel_id=1, source_target_pairs={{0,1},{1,0},{2,3},{3,2},{4,5},{5,4},{6,7},{7,6},{8,9},{9,8},{10,11... | collective-permute-start | bytes 983048 | tf_op jit(solution)/shard_map/ppermute | solution.py:642
  (12 other events, 37.1 us)

commit v4 on v3

--- a/solution.py
+++ b/solution.py
@@ -670,8 +670,9 @@
     q_a, kv_a = qkv(near, weights, tables, where, 2, block, 0, early)
     handed_a = swap(kv_a, "role", 1)
     w_both = stage(w_out, w_mate, (kv_a,))
+    local, stats = local_attention(fresh_q, fresh_kv, answer_cache[0], suffix_len, scale, w_both)
     came, fourth = exchange_pass(third, fourth, swap, ())
-    ahead, behind = hold((ahead, behind), (w_both,))
+    ahead, behind = hold((ahead, behind), (local,))
     last = swap(fourth, "grp", FOURTH)
     far = [ahead, behind, swap(ahead, "tp", 1), swap(behind, "tp", 1)]
     q_b, kv_b = qkv(far, weights, tables, where, 6, block, 0)
@@ -691,11 +692,10 @@
     via_down = around(far_low, -1)
 
     back = exchange_near(answered, swap, (), STEP)
-    local, stats = local_attention(fresh_q, fresh_kv, answer_cache[0], suffix_len, scale, back)
-    kept, third, fourth = exchange_pick(back, home, swap, (local,), STEP)
-    came, fourth = exchange_pass(third, fourth, swap, (), STEP)
-    up = add_half(0, to_up, via_up, (fourth,))
-    down = add_half(1, to_down, via_down, (fourth,))
+    kept, third, fourth = exchange_pick(back, home, swap, (), STEP)
+    up = add_half(0, to_up, via_up, (third,))
+    down = add_half(1, to_down, via_down, (third,))
+    came, fourth = exchange_pass(third, fourth, swap, (up, down), STEP)
     back = (kept, came, swap(fourth, "grp", FOURTH))
     sum_up = around(up, 1)
     sum_down = around(down, -1)

time: 99.4 us -> 99.1 us (level)
  starting transfers between devices: 53.4 us -> 51.8 us
  waiting for transfers between devices: 21.3 us -> 22.6 us
    ppermute x19, starting transfers between devices: 39.4 us -> 37.7 us  [swap(): lax.ppermute(value, axis, [(i, i ^ mask) for i in range(lax.axis_size(axi...]
    ppermute x19, waiting for transfers between devices: 11.5 us -> 12.6 us  [swap(): lax.ppermute(value, axis, [(i, i ^ mask) for i in range(lax.axis_size(axi...]
  transfers between devices with their start and end apart: 30 -> 30, of which waited for: 11 -> 12; matrix products, arithmetic and copies ran while one was open for 0% -> 0% of each run, Pallas kernels for 19% -> 19%
where the time goes in v4:
time: 99.1 us; the launch traced here: 98.9 us
  starting transfers between devices  51.8 us (52%)
  waiting for transfers between devices  22.6 us (23%)
  Pallas kernels  20.1 us (20%)
  local copies, waits for them, and re-layouts  3.5 us (4%)
    ppermute x19, starting transfers between devices, swap(): lax.ppermute(value, axis, [(i, i ^ mask) for i in range(lax.axis_size(axi...  37.7 us
    pallas_call x26, Pallas kernels, simple_call(): pl.pallas_call(body, in_specs=specs or [VMEM] * len(args), out_specs=jax....  20.1 us
    ppermute x11, starting transfers between devices, around(): lax.ppermute(value, 'tp', [(i, (i + 2 * by) % tp_size) for i in range(tp_...  14.1 us
    ppermute x19, waiting for transfers between devices, swap(): lax.ppermute(value, axis, [(i, i ^ mask) for i in range(lax.axis_size(axi...  12.6 us
    ppermute x11, waiting for transfers between devices, around(): lax.ppermute(value, 'tp', [(i, (i + 2 * by) % tp_size) for i in range(tp_...  9.94 us
    unnamed x28, local copies, waits for them, and re-layouts  3.5 us
  transfers between devices with their start and end apart: 30, of which 12 were waited for; matrix products, arithmetic and copies ran while one was open for 0% of the time, Pallas kernels for 19%

profile of v4, /device:TPU:1, one launch (start us, length us, event | category | flops | bytes accessed | tf_op | source)
XLA Modules:
  0.0 98.9 jit_solution(1934143825961398211)
XLA Ops:
  0.6 3.3 %collective-permute-start.9 = (bf16[384,5120]{1,0:T(8,128)(2,1)}, bf16[384,5120]{1,0:T(8,128)(2,1)}, u32[]{:S(2)}, u32[]{:S(2)}) collective-permute-start(bf16[384,5120]{1,0:T(8,128)(2,1)} %own.1), channel_id=1, source_target_pairs={{0,1},{1,0},{2,3},{3,2},{4,5},{5,4},{6,7},{7,6},{8,9},{9,8},{10,11... | collective-permute-start | bytes 11796488 | tf_op jit(solution)/shard_map/ppermute | solution.py:642
  6.5 2.7 %collective-permute-start.1 = (bf16[64,5120]{1,0:T(8,128)(2,1)S(1)}, bf16[64,5120]{1,0:T(8,128)(2,1)S(1)}, u32[]{:S(2)}, u32[]{:S(2)}) collective-permute-start(bf16[64,5120]{1,0:T(8,128)(2,1)S(1)} %shard_map.131.refs_0_), channel_id=1, source_target_pairs={{0,6},{1,7},{2,0},{3,1},{4,2},{5,3},{6,4},{7,5},{8,14},{9,15},{10,... | collective-permute-start | bytes 1966088 | tf_op jit(solution)/shard_map/ppermute | solution.py:639
  12.7 1.8 %shard_map.133 = (bf16[32,384]{1,0:T(8,128)(2,1)S(1)}, bf16[32,256]{1,0:T(8,128)(2,1)S(1)}, bf16[5120,640]{1,0:T(8,128)(2,1)S(1)}) custom-call(bf16[32,5120]{1,0:T(8,128)(2,1)S(1)} %get-tuple-element.42.x, bf16[5120,384]{1,0:T(8,128)(2,1)S(1)} %copy-done.1, bf16[5120,128]{1,0:T(8,128)(2,1)S(1)} %copy-done.3, bf16[5120,128]{1,0:T(8,128)(2,1)S(1)} %copy-done.4, ...), custom_call_target="tpu_custom_call" | custom-call | flops 900000000 | tf_op jit(solution)/shard_map/pallas_call | solution.py:39
  14.5 5.3 %collective-permute-start.2 = (bf16[32,384]{1,0:T(8,128)(2,1)S(1)}, bf16[32,384]{1,0:T(8,128)(2,1)S(1)}, u32[]{:S(2)}, u32[]{:S(2)}) collective-permute-start(bf16[32,384]{1,0:T(8,128)(2,1)S(1)} %get-tuple-element.45.a.q), channel_id=1, source_target_pairs={{0,32},{8,40},{16,48},{24,56},{32,0},{40,8},{48,16},{56,24},{64,96... | collective-permute-start | bytes 73736 | tf_op jit(solution)/shard_map/ppermute | solution.py:642
  19.7 1.4 %collective-permute-done.2.b = bf16[32,384]{1,0:T(8,128)(2,1)S(1)} collective-permute-done((bf16[32,384]{1,0:T(8,128)(2,1)S(1)}, bf16[32,384]{1,0:T(8,128)(2,1)S(1)}, u32[]{:S(2)}, u32[]{:S(2)}) %collective-permute-start.2) | collective-permute-done | bytes 24608 | tf_op jit(solution)/shard_map/ppermute | solution.py:642
  22.0 2.4 %collective-permute-done.3.far = bf16[64,384]{1,0:T(8,128)(2,1)S(1)} collective-permute-done((bf16[64,384]{1,0:T(8,128)(2,1)S(1)}, bf16[64,384]{1,0:T(8,128)(2,1)S(1)}, u32[]{:S(2)}, u32[]{:S(2)}) %collective-permute-start.3) | collective-permute-done | bytes 49184 | tf_op jit(solution)/shard_map/ppermute | solution.py:642
  24.6 1.3 %shard_map.136 = (bf16[128,384]{1,0:T(8,128)(2,1)S(1)}, bf16[128,256]{1,0:T(8,128)(2,1)S(1)}) custom-call(bf16[64,5120]{1,0:T(8,128)(2,1)S(1)} %shard_map.131.refs_0_, bf16[64,5120]{1,0:T(8,128)(2,1)S(1)} %collective-permute-done.4.refs_1_, bf16[5120,640]{1,0:T(8,128)(2,1)S(1)} %get-tuple-element.47.refs_2_.refs_4_, f32[512,256]{1,0:T(8,128)S(1)} %copy-done, ...), custom_call_target="tpu_custom_call" | custom-call | flops 900000000 | tf_op jit(solution)/shard_map/pallas_call | solution.py:39
  25.9 2.1 %collective-permute-start.5 = (bf16[64,5120]{1,0:T(8,128)(2,1)S(1)}, bf16[64,5120]{1,0:T(8,128)(2,1)S(1)}, u32[]{:S(2)}, u32[]{:S(2)}) collective-permute-start(bf16[64,5120]{1,0:T(8,128)(2,1)S(1)} %get-tuple-element.49.refs_0_.a), channel_id=1, source_target_pairs={{0,1},{1,0},{2,3},{3,2},{4,5},{5,4},{6,7},{7,6},{8,9},{9,8},{10,11... | collective-permute-start | bytes 1966088 | tf_op jit(solution)/shard_map/ppermute | solution.py:642
  28.2 2.7 %collective-permute-start.8 = (bf16[32,5120]{1,0:T(8,128)(2,1)S(1)}, bf16[32,5120]{1,0:T(8,128)(2,1)S(1)}, u32[]{:S(2)}, u32[]{:S(2)}) collective-permute-start(bf16[32,5120]{1,0:T(8,128)(2,1)S(1)} %get-tuple-element.54), channel_id=1, source_target_pairs={{0,6},{1,7},{2,0},{3,1},{4,2},{5,3},{6,4},{7,5},{8,14},{9,15},{10,... | collective-permute-start | bytes 983048 | tf_op jit(solution)/shard_map/ppermute | solution.py:639
  30.9 2.3 %shard_map.138 = (bf16[384,384]{1,0:T(8,128)(2,1)S(1)}, bf16[384,256]{1,0:T(8,128)(2,1)S(1)}) custom-call(bf16[64,5120]{1,0:T(8,128)(2,1)S(1)} %get-tuple-element.49.refs_0_.a, bf16[64,5120]{1,0:T(8,128)(2,1)S(1)} %get-tuple-element.50.refs_1_.b, bf16[64,5120]{1,0:T(8,128)(2,1)S(1)} %collective-permute-done.5.refs_2_, ...), custom_call_target="tpu_custom_call" | custom-call | tf_op jit(solution)/shard_map/pallas_call | solution.py:39
  33.2 2.4 %shard_map.140.after.w = bf16[768,5120]{1,0:T(8,128)(2,1)S(1)} custom-call(bf16[384,5120]{1,0:T(8,128)(2,1)S(1)} %copy-done.2, bf16[384,5120]{1,0:T(8,128)(2,1)} %collective-permute-done.9.other, bf16[384,256]{1,0:T(8,128)(2,1)S(1)} %get-tuple-element.56.rest_0_.kv_a), custom_call_target="tpu_custom_call" | custom-call | tf_op jit(solution)/shard_map/pallas_call | solution.py:39
  36.6 1.7 %collective-permute-done.7.refs_0_ = bf16[32,5120]{1,0:T(8,128)(2,1)S(1)} collective-permute-done((bf16[32,5120]{1,0:T(8,128)(2,1)S(1)}, bf16[32,5120]{1,0:T(8,128)(2,1)S(1)}, u32[]{:S(2)}, u32[]{:S(2)}) %collective-permute-start.7) | collective-permute-done | bytes 327712 | tf_op jit(solution)/shard_map/ppermute | solution.py:639
  38.3 1.2 %collective-permute-start.10 = (bf16[32,5120]{1,0:T(8,128)(2,1)S(1)}, bf16[32,5120]{1,0:T(8,128)(2,1)S(1)}, u32[]{:S(2)}, u32[]{:S(2)}) collective-permute-start(bf16[32,5120]{1,0:T(8,128)(2,1)S(1)} %get-tuple-element.58.refs_0_), channel_id=1, source_target_pairs={{0,1},{1,0},{2,3},{3,2},{4,5},{5,4},{6,7},{7,6},{8,9},{9,8},{10,11... | collective-permute-start | bytes 983048 | tf_op jit(solution)/shard_map/ppermute | solution.py:642
  40.6 2.1 %collective-permute-start.13 = (bf16[64,384]{1,0:T(8,128)(2,1)S(1)}, bf16[64,384]{1,0:T(8,128)(2,1)S(1)}, u32[]{:S(2)}, u32[]{:S(2)}) collective-permute-start(bf16[64,384]{1,0:T(8,128)(2,1)S(1)} %get-tuple-element.46.refs_2_), channel_id=1, source_target_pairs={{0,16},{8,24},{16,0},{24,8},{32,48},{40,56},{48,32},{56,40},{64,80... | collective-permute-start | bytes 147464 | tf_op jit(solution)/shard_map/ppermute | solution.py:642
  42.7 1.3 %shard_map.143 = (bf16[128,384]{1,0:T(8,128)(2,1)S(1)}, bf16[128,256]{1,0:T(8,128)(2,1)S(1)}) custom-call(bf16[32,5120]{1,0:T(8,128)(2,1)S(1)} %get-tuple-element.58.refs_0_, bf16[32,5120]{1,0:T(8,128)(2,1)S(1)} %get-tuple-element.59.refs_1_, bf16[32,5120]{1,0:T(8,128)(2,1)S(1)} %collective-permute-done.10.refs_2_, ...), custom_call_target="tpu_custom_call" | custom-call | tf_op jit(solution)/shard_map/pallas_call | solution.py:39
  44.4 2.7 %collective-permute-start.14 = (bf16[32,384]{1,0:T(8,128)(2,1)S(1)}, bf16[32,384]{1,0:T(8,128)(2,1)S(1)}, u32[]{:S(2)}, u32[]{:S(2)}) collective-permute-start(bf16[32,384]{1,0:T(8,128)(2,1)S(1)} %shard_map.145), channel_id=1, source_target_pairs={{0,64},{8,72},{16,80},{24,88},{32,96},{40,104},{48,112},{56,120},{... | collective-permute-start | bytes 73736 | tf_op jit(solution)/shard_map/ppermute | solution.py:642
  47.2 1.5 %shard_map.144 = (bf16[256,384]{1,0:T(8,128)(2,1)S(1)}, bf16[256,384]{1,0:T(8,128)(2,1)S(1)}) custom-call(bf16[384,384]{1,0:T(8,128)(2,1)S(1)} %get-tuple-element.52.q_a, bf16[128,384]{1,0:T(8,128)(2,1)S(1)} %get-tuple-element.60.q_b, bf16[384,256]{1,0:T(8,128)(2,1)S(1)} %get-tuple-element.56.rest_0_.kv_a, bf16[128,256]{1,0:T(8,128)(2,1)S(1)} %get-tuple-element.61.kv_b, ...), custom_call_target="tpu_custom_call" | custom-call | flops 402653184 | tf_op jit(solution)/shard_map/pallas_call | solution.py:39
  48.6 2.5 %collective-permute-start.12 = (bf16[256,384]{1,0:T(8,128)(2,1)S(1)}, bf16[256,384]{1,0:T(8,128)(2,1)S(1)}, u32[]{:S(2)}, u32[]{:S(2)}) collective-permute-start(bf16[256,384]{1,0:T(8,128)(2,1)S(1)} %get-tuple-element.63), channel_id=1, source_target_pairs={{0,1},{1,0},{2,3},{3,2},{4,5},{5,4},{6,7},{7,6},{8,9},{9,8},{10,11... | collective-permute-start | bytes 589832 | tf_op jit(solution)/shard_map/ppermute | solution.py:642
  51.5 5.1 %collective-permute-start.18 = (bf16[32,512]{1,0:T(8,128)(2,1)S(1)}, bf16[32,512]{1,0:T(8,128)(2,1)S(1)}, u32[]{:S(2)}, u32[]{:S(2)}) collective-permute-start(bf16[32,512]{1,0:T(8,128)(2,1)S(1)} %shard_map.146.rest_0_.a), channel_id=1, source_target_pairs={{0,32},{8,40},{16,48},{24,56},{32,0},{40,8},{48,16},{56,24},{64,96... | collective-permute-start | bytes 98312 | tf_op jit(solution)/shard_map/ppermute | solution.py:642
  56.6 2.3 %shard_map.147 = (bf16[64,5120]{1,0:T(8,128)(2,1)S(1)}, bf16[64,5120]{1,0:T(8,128)(2,1)S(1)}, bf16[64,5120]{1,0:T(8,128)(2,1)S(1)}, bf16[32,5120]{1,0:T(8,128)(2,1)S(1)}, bf16[32,5120]{1,0:T(8,128)(2,1)S(1)}) custom-call(bf16[256,384]{1,0:T(8,128)(2,1)S(1)} %get-tuple-element.62.after.own, bf16[256,384]{1,0:T(8,128)(2,1)S(1)} %collective-permute-done.12.other, ...), custom_call_target="tpu_custom_call" | custom-call | tf_op jit(solution)/shard_map/pallas_call | solution.py:39
  59.1 2.9 %collective-permute-start.21 = (bf16[32,5120]{1,0:T(8,128)(2,1)S(1)}, bf16[32,5120]{1,0:T(8,128)(2,1)S(1)}, u32[]{:S(2)}, u32[]{:S(2)}) collective-permute-start(bf16[32,5120]{1,0:T(8,128)(2,1)S(1)} %get-tuple-element.72), channel_id=1, source_target_pairs={{0,6},{1,7},{2,0},{3,1},{4,2},{5,3},{6,4},{7,5},{8,14},{9,15},{10,... | collective-permute-start | bytes 983048 | tf_op jit(solution)/shard_map/ppermute | solution.py:639
  62.8 2.6 %collective-permute-done.19.far = bf16[64,512]{1,0:T(8,128)(2,1)S(1)} collective-permute-done((bf16[64,512]{1,0:T(8,128)(2,1)S(1)}, bf16[64,512]{1,0:T(8,128)(2,1)S(1)}, u32[]{:S(2)}, u32[]{:S(2)}) %collective-permute-start.19) | collective-permute-done | bytes 65568 | tf_op jit(solution)/shard_map/ppermute | solution.py:642
  65.6 1.4 %collective-permute-start.23 = (bf16[64,512]{1,0:T(8,128)(2,1)S(1)}, bf16[64,512]{1,0:T(8,128)(2,1)S(1)}, u32[]{:S(2)}, u32[]{:S(2)}) collective-permute-start(bf16[64,512]{1,0:T(8,128)(2,1)S(1)} %get-tuple-element.70.rest_0_), channel_id=1, source_target_pairs={{0,16},{8,24},{16,0},{24,8},{32,48},{40,56},{48,32},{56,40},{64,80... | collective-permute-start | bytes 196616 | tf_op jit(solution)/shard_map/ppermute | solution.py:642
  68.2 2.2 %collective-permute-done.23.came = bf16[64,512]{1,0:T(8,128)(2,1)S(1)} collective-permute-done((bf16[64,512]{1,0:T(8,128)(2,1)S(1)}, bf16[64,512]{1,0:T(8,128)(2,1)S(1)}, u32[]{:S(2)}, u32[]{:S(2)}) %collective-permute-start.23) | collective-permute-done | bytes 65568 | tf_op jit(solution)/shard_map/ppermute | solution.py:642
  70.6 2.7 %collective-permute-start.22 = (bf16[64,5120]{1,0:T(8,128)(2,1)S(1)}, bf16[64,5120]{1,0:T(8,128)(2,1)S(1)}, u32[]{:S(2)}, u32[]{:S(2)}) collective-permute-start(bf16[64,5120]{1,0:T(8,128)(2,1)S(1)} %shard_map.151.rest_1_), channel_id=1, source_target_pairs={{0,6},{1,7},{2,0},{3,1},{4,2},{5,3},{6,4},{7,5},{8,14},{9,15},{10,... | collective-permute-start | bytes 1966088 | tf_op jit(solution)/shard_map/ppermute | solution.py:639
  73.3 1.4 %collective-permute-done.24.last = bf16[32,512]{1,0:T(8,128)(2,1)S(1)} collective-permute-done((bf16[32,512]{1,0:T(8,128)(2,1)S(1)}, bf16[32,512]{1,0:T(8,128)(2,1)S(1)}, u32[]{:S(2)}, u32[]{:S(2)}) %collective-permute-start.24) | collective-permute-done | bytes 32800 | tf_op jit(solution)/shard_map/ppermute | solution.py:642
  75.9 6.1 %collective-permute-start.25 = (bf16[16,5120]{1,0:T(8,128)(2,1)S(1)}, bf16[16,5120]{1,0:T(8,128)(2,1)S(1)}, u32[]{:S(2)}, u32[]{:S(2)}) collective-permute-start(bf16[16,5120]{1,0:T(8,128)(2,1)S(1)} %get-tuple-element.78), channel_id=1, source_target_pairs={{0,1},{1,0},{2,3},{3,2},{4,5},{5,4},{6,7},{7,6},{8,9},{9,8},{10,11... | collective-permute-start | bytes 491528 | tf_op jit(solution)/shard_map/ppermute | solution.py:642
  84.0 2.0 %collective-permute-start.28 = (bf16[16,5120]{1,0:T(8,128)(2,1)S(1)}, bf16[16,5120]{1,0:T(8,128)(2,1)S(1)}, u32[]{:S(2)}, u32[]{:S(2)}) collective-permute-start(bf16[16,5120]{1,0:T(8,128)(2,1)S(1)} %shard_map.156.own), channel_id=1, source_target_pairs={{0,6},{1,7},{2,0},{3,1},{4,2},{5,3},{6,4},{7,5},{8,14},{9,15},{10,... | collective-permute-start | bytes 491528 | tf_op jit(solution)/shard_map/ppermute | solution.py:639
  87.1 3.8 %collective-permute-done.26.far = bf16[16,5120]{1,0:T(8,128)(2,1)S(1)} collective-permute-done((bf16[16,5120]{1,0:T(8,128)(2,1)S(1)}, bf16[16,5120]{1,0:T(8,128)(2,1)S(1)}, u32[]{:S(2)}, u32[]{:S(2)}) %collective-permute-start.26) | collective-permute-done | bytes 163872 | tf_op jit(solution)/shard_map/ppermute | solution.py:639
  90.9 3.3 %collective-permute-done.27.down = bf16[16,5120]{1,0:T(8,128)(2,1)S(1)} collective-permute-done((bf16[16,5120]{1,0:T(8,128)(2,1)S(1)}, bf16[16,5120]{1,0:T(8,128)(2,1)S(1)}, u32[]{:S(2)}, u32[]{:S(2)}) %collective-permute-start.27) | collective-permute-done | bytes 163872 | tf_op jit(solution)/shard_map/ppermute | solution.py:639
  94.3 2.1 %collective-permute-start.29 = (f32[16,5120]{1,0:T(8,128)S(1)}, f32[16,5120]{1,0:T(8,128)S(1)}, u32[]{:S(2)}, u32[]{:S(2)}) collective-permute-start(f32[16,5120]{1,0:T(8,128)S(1)} %shard_map.157.kept), channel_id=1, source_target_pairs={{0,1},{1,0},{2,3},{3,2},{4,5},{5,4},{6,7},{7,6},{8,9},{9,8},{10,11... | collective-permute-start | bytes 983048 | tf_op jit(solution)/shard_map/ppermute | solution.py:642
  96.5 1.3 %collective-permute-done.29.taken = f32[16,5120]{1,0:T(8,128)S(1)} collective-permute-done((f32[16,5120]{1,0:T(8,128)S(1)}, f32[16,5120]{1,0:T(8,128)S(1)}, u32[]{:S(2)}, u32[]{:S(2)}) %collective-permute-start.29) | collective-permute-done | bytes 327712 | tf_op jit(solution)/shard_map/ppermute | solution.py:642
  (84 shorter events, 18.2 us)
Async XLA Ops:
  0.6 32.6 %collective-permute-start.9 = (bf16[384,5120]{1,0:T(8,128)(2,1)}, bf16[384,5120]{1,0:T(8,128)(2,1)}, u32[]{:S(2)}, u32[]{:S(2)}) collective-permute-start(bf16[384,5120]{1,0:T(8,128)(2,1)} %own.1), channel_id=1, source_target_pairs={{0,1},{1,0},{2,3},{3,2},{4,5},{5,4},{6,7},{7,6},{8,9},{9,8},{10,11... | collective-permute-start | bytes 11796488 | tf_op jit(solution)/shard_map/ppermute | solution.py:642
  6.4 19.5 %collective-permute-start = (bf16[64,5120]{1,0:T(8,128)(2,1)S(1)}, bf16[64,5120]{1,0:T(8,128)(2,1)S(1)}, u32[]{:S(2)}, u32[]{:S(2)}) collective-permute-start(bf16[64,5120]{1,0:T(8,128)(2,1)S(1)} %shard_map.131.refs_0_), channel_id=1, source_target_pairs={{0,2},{1,3},{2,4},{3,5},{4,6},{5,7},{6,0},{7,1},{8,10},{9,11},{10,... | collective-permute-start | bytes 1966088 | tf_op jit(solution)/shard_map/ppermute | solution.py:639
  6.5 19.4 %collective-permute-start.1 = (bf16[64,5120]{1,0:T(8,128)(2,1)S(1)}, bf16[64,5120]{1,0:T(8,128)(2,1)S(1)}, u32[]{:S(2)}, u32[]{:S(2)}) collective-permute-start(bf16[64,5120]{1,0:T(8,128)(2,1)S(1)} %shard_map.131.refs_0_), channel_id=1, source_target_pairs={{0,6},{1,7},{2,0},{3,1},{4,2},{5,3},{6,4},{7,5},{8,14},{9,15},{10,... | collective-permute-start | bytes 1966088 | tf_op jit(solution)/shard_map/ppermute | solution.py:639
  9.2 15.4 %collective-permute-start.4 = (bf16[64,5120]{1,0:T(8,128)(2,1)S(1)}, bf16[64,5120]{1,0:T(8,128)(2,1)S(1)}, u32[]{:S(2)}, u32[]{:S(2)}) collective-permute-start(bf16[64,5120]{1,0:T(8,128)(2,1)S(1)} %shard_map.131.refs_0_), channel_id=1, source_target_pairs={{0,1},{1,0},{2,3},{3,2},{4,5},{5,4},{6,7},{7,6},{8,9},{9,8},{10,11... | collective-permute-start | bytes 1966088 | tf_op jit(solution)/shard_map/ppermute | solution.py:642
  11.0 13.6 %copy-start = (f32[512,256]{1,0:T(8,128)S(1)}, f32[512,256]{1,0:T(8,128)}, u32[]{:S(2)}) copy-start(f32[512,256]{1,0:T(8,128)} %constant.14.clone.refs_3_.refs_5_) | copy-start | bytes 1572868
  14.5 6.7 %collective-permute-start.2 = (bf16[32,384]{1,0:T(8,128)(2,1)S(1)}, bf16[32,384]{1,0:T(8,128)(2,1)S(1)}, u32[]{:S(2)}, u32[]{:S(2)}) collective-permute-start(bf16[32,384]{1,0:T(8,128)(2,1)S(1)} %get-tuple-element.45.a.q), channel_id=1, source_target_pairs={{0,32},{8,40},{16,48},{24,56},{32,0},{40,8},{48,16},{56,24},{64,96... | collective-permute-start | bytes 73736 | tf_op jit(solution)/shard_map/ppermute | solution.py:642
  21.2 3.2 %collective-permute-start.3 = (bf16[64,384]{1,0:T(8,128)(2,1)S(1)}, bf16[64,384]{1,0:T(8,128)(2,1)S(1)}, u32[]{:S(2)}, u32[]{:S(2)}) collective-permute-start(bf16[64,384]{1,0:T(8,128)(2,1)S(1)} %shard_map.134.near), channel_id=1, source_target_pairs={{0,8},{8,0},{16,24},{24,16},{32,40},{40,32},{48,56},{56,48},{64,72... | collective-permute-start | bytes 147464 | tf_op jit(solution)/shard_map/ppermute | solution.py:642
  25.9 5.0 %collective-permute-start.5 = (bf16[64,5120]{1,0:T(8,128)(2,1)S(1)}, bf16[64,5120]{1,0:T(8,128)(2,1)S(1)}, u32[]{:S(2)}, u32[]{:S(2)}) collective-permute-start(bf16[64,5120]{1,0:T(8,128)(2,1)S(1)} %get-tuple-element.49.refs_0_.a), channel_id=1, source_target_pairs={{0,1},{1,0},{2,3},{3,2},{4,5},{5,4},{6,7},{7,6},{8,9},{9,8},{10,11... | collective-permute-start | bytes 1966088 | tf_op jit(solution)/shard_map/ppermute | solution.py:642
  28.0 2.9 %collective-permute-start.6 = (bf16[64,5120]{1,0:T(8,128)(2,1)S(1)}, bf16[64,5120]{1,0:T(8,128)(2,1)S(1)}, u32[]{:S(2)}, u32[]{:S(2)}) collective-permute-start(bf16[64,5120]{1,0:T(8,128)(2,1)S(1)} %get-tuple-element.50.refs_1_.b), channel_id=1, source_target_pairs={{0,1},{1,0},{2,3},{3,2},{4,5},{5,4},{6,7},{7,6},{8,9},{9,8},{10,11... | collective-permute-start | bytes 1966088 | tf_op jit(solution)/shard_map/ppermute | solution.py:642
  28.2 10.2 %collective-permute-start.7 = (bf16[32,5120]{1,0:T(8,128)(2,1)S(1)}, bf16[32,5120]{1,0:T(8,128)(2,1)S(1)}, u32[]{:S(2)}, u32[]{:S(2)}) collective-permute-start(bf16[32,5120]{1,0:T(8,128)(2,1)S(1)} %get-tuple-element.53), channel_id=1, source_target_pairs={{0,2},{1,3},{2,4},{3,5},{4,6},{5,7},{6,0},{7,1},{8,10},{9,11},{10,... | collective-permute-start | bytes 983048 | tf_op jit(solution)/shard_map/ppermute | solution.py:639
  28.2 10.1 %collective-permute-start.8 = (bf16[32,5120]{1,0:T(8,128)(2,1)S(1)}, bf16[32,5120]{1,0:T(8,128)(2,1)S(1)}, u32[]{:S(2)}, u32[]{:S(2)}) collective-permute-start(bf16[32,5120]{1,0:T(8,128)(2,1)S(1)} %get-tuple-element.54), channel_id=1, source_target_pairs={{0,6},{1,7},{2,0},{3,1},{4,2},{5,3},{6,4},{7,5},{8,14},{9,15},{10,... | collective-permute-start | bytes 983048 | tf_op jit(solution)/shard_map/ppermute | solution.py:639
  38.3 4.4 %collective-permute-start.10 = (bf16[32,5120]{1,0:T(8,128)(2,1)S(1)}, bf16[32,5120]{1,0:T(8,128)(2,1)S(1)}, u32[]{:S(2)}, u32[]{:S(2)}) collective-permute-start(bf16[32,5120]{1,0:T(8,128)(2,1)S(1)} %get-tuple-element.58.refs_0_), channel_id=1, source_target_pairs={{0,1},{1,0},{2,3},{3,2},{4,5},{5,4},{6,7},{7,6},{8,9},{9,8},{10,11... | collective-permute-start | bytes 983048 | tf_op jit(solution)/shard_map/ppermute | solution.py:642
  39.6 3.1 %collective-permute-start.11 = (bf16[32,5120]{1,0:T(8,128)(2,1)S(1)}, bf16[32,5120]{1,0:T(8,128)(2,1)S(1)}, u32[]{:S(2)}, u32[]{:S(2)}) collective-permute-start(bf16[32,5120]{1,0:T(8,128)(2,1)S(1)} %get-tuple-element.59.refs_1_), channel_id=1, source_target_pairs={{0,1},{1,0},{2,3},{3,2},{4,5},{5,4},{6,7},{7,6},{8,9},{9,8},{10,11... | collective-permute-start | bytes 983048 | tf_op jit(solution)/shard_map/ppermute | solution.py:642
  39.7 11.4 %collective-permute-start.15 = (bf16[384,256]{1,0:T(8,128)(2,1)S(1)}, bf16[384,256]{1,0:T(8,128)(2,1)S(1)}, u32[]{:S(2)}, u32[]{:S(2)}) collective-permute-start(bf16[384,256]{1,0:T(8,128)(2,1)S(1)} %get-tuple-element.56.rest_0_.kv_a), channel_id=1, source_target_pairs={{0,128},{128,0},{1,129},{129,1},{2,130},{130,2},{3,131},{131,3},{4... | collective-permute-start | bytes 589832 | tf_op jit(solution)/shard_map/ppermute | solution.py:642
  40.6 3.8 %collective-permute-start.13 = (bf16[64,384]{1,0:T(8,128)(2,1)S(1)}, bf16[64,384]{1,0:T(8,128)(2,1)S(1)}, u32[]{:S(2)}, u32[]{:S(2)}) collective-permute-start(bf16[64,384]{1,0:T(8,128)(2,1)S(1)} %get-tuple-element.46.refs_2_), channel_id=1, source_target_pairs={{0,16},{8,24},{16,0},{24,8},{32,48},{40,56},{48,32},{56,40},{64,80... | collective-permute-start | bytes 147464 | tf_op jit(solution)/shard_map/ppermute | solution.py:642
  44.0 7.1 %collective-permute-start.16 = (bf16[128,256]{1,0:T(8,128)(2,1)S(1)}, bf16[128,256]{1,0:T(8,128)(2,1)S(1)}, u32[]{:S(2)}, u32[]{:S(2)}) collective-permute-start(bf16[128,256]{1,0:T(8,128)(2,1)S(1)} %get-tuple-element.61.kv_b), channel_id=1, source_target_pairs={{0,128},{128,0},{1,129},{129,1},{2,130},{130,2},{3,131},{131,3},{4... | collective-permute-start | bytes 196616 | tf_op jit(solution)/shard_map/ppermute | solution.py:642
  44.4 6.7 %collective-permute-start.14 = (bf16[32,384]{1,0:T(8,128)(2,1)S(1)}, bf16[32,384]{1,0:T(8,128)(2,1)S(1)}, u32[]{:S(2)}, u32[]{:S(2)}) collective-permute-start(bf16[32,384]{1,0:T(8,128)(2,1)S(1)} %shard_map.145), channel_id=1, source_target_pairs={{0,64},{8,72},{16,80},{24,88},{32,96},{40,104},{48,112},{56,120},{... | collective-permute-start | bytes 73736 | tf_op jit(solution)/shard_map/ppermute | solution.py:642
  48.6 8.0 %collective-permute-start.12 = (bf16[256,384]{1,0:T(8,128)(2,1)S(1)}, bf16[256,384]{1,0:T(8,128)(2,1)S(1)}, u32[]{:S(2)}, u32[]{:S(2)}) collective-permute-start(bf16[256,384]{1,0:T(8,128)(2,1)S(1)} %get-tuple-element.63), channel_id=1, source_target_pairs={{0,1},{1,0},{2,3},{3,2},{4,5},{5,4},{6,7},{7,6},{8,9},{9,8},{10,11... | collective-permute-start | bytes 589832 | tf_op jit(solution)/shard_map/ppermute | solution.py:642
  51.5 10.4 %collective-permute-start.18 = (bf16[32,512]{1,0:T(8,128)(2,1)S(1)}, bf16[32,512]{1,0:T(8,128)(2,1)S(1)}, u32[]{:S(2)}, u32[]{:S(2)}) collective-permute-start(bf16[32,512]{1,0:T(8,128)(2,1)S(1)} %shard_map.146.rest_0_.a), channel_id=1, source_target_pairs={{0,32},{8,40},{16,48},{24,56},{32,0},{40,8},{48,16},{56,24},{64,96... | collective-permute-start | bytes 98312 | tf_op jit(solution)/shard_map/ppermute | solution.py:642
  58.9 9.2 %collective-permute-start.17 = (bf16[32,5120]{1,0:T(8,128)(2,1)S(1)}, bf16[32,5120]{1,0:T(8,128)(2,1)S(1)}, u32[]{:S(2)}, u32[]{:S(2)}) collective-permute-start(bf16[32,5120]{1,0:T(8,128)(2,1)S(1)} %get-tuple-element.68), channel_id=1, source_target_pairs={{0,2},{1,3},{2,4},{3,5},{4,6},{5,7},{6,0},{7,1},{8,10},{9,11},{10,... | collective-permute-start | bytes 983048 | tf_op jit(solution)/shard_map/ppermute | solution.py:639
  59.1 9.1 %collective-permute-start.21 = (bf16[32,5120]{1,0:T(8,128)(2,1)S(1)}, bf16[32,5120]{1,0:T(8,128)(2,1)S(1)}, u32[]{:S(2)}, u32[]{:S(2)}) collective-permute-start(bf16[32,5120]{1,0:T(8,128)(2,1)S(1)} %get-tuple-element.72), channel_id=1, source_target_pairs={{0,6},{1,7},{2,0},{3,1},{4,2},{5,3},{6,4},{7,5},{8,14},{9,15},{10,... | collective-permute-start | bytes 983048 | tf_op jit(solution)/shard_map/ppermute | solution.py:639
  61.9 3.5 %collective-permute-start.19 = (bf16[64,512]{1,0:T(8,128)(2,1)S(1)}, bf16[64,512]{1,0:T(8,128)(2,1)S(1)}, u32[]{:S(2)}, u32[]{:S(2)}) collective-permute-start(bf16[64,512]{1,0:T(8,128)(2,1)S(1)} %shard_map.148.near), channel_id=1, source_target_pairs={{0,8},{8,0},{16,24},{24,16},{32,40},{40,32},{48,56},{56,48},{64,72... | collective-permute-start | bytes 196616 | tf_op jit(solution)/shard_map/ppermute | solution.py:642
  65.6 4.8 %collective-permute-start.23 = (bf16[64,512]{1,0:T(8,128)(2,1)S(1)}, bf16[64,512]{1,0:T(8,128)(2,1)S(1)}, u32[]{:S(2)}, u32[]{:S(2)}) collective-permute-start(bf16[64,512]{1,0:T(8,128)(2,1)S(1)} %get-tuple-element.70.rest_0_), channel_id=1, source_target_pairs={{0,16},{8,24},{16,0},{24,8},{32,48},{40,56},{48,32},{56,40},{64,80... | collective-permute-start | bytes 196616 | tf_op jit(solution)/shard_map/ppermute | solution.py:642
  70.4 4.3 %collective-permute-start.24 = (bf16[32,512]{1,0:T(8,128)(2,1)S(1)}, bf16[32,512]{1,0:T(8,128)(2,1)S(1)}, u32[]{:S(2)}, u32[]{:S(2)}) collective-permute-start(bf16[32,512]{1,0:T(8,128)(2,1)S(1)} %shard_map.153), channel_id=1, source_target_pairs={{0,64},{8,72},{16,80},{24,88},{32,96},{40,104},{48,112},{56,120},{... | collective-permute-start | bytes 98312 | tf_op jit(solution)/shard_map/ppermute | solution.py:642
  70.6 15.3 %collective-permute-start.20 = (bf16[64,5120]{1,0:T(8,128)(2,1)S(1)}, bf16[64,5120]{1,0:T(8,128)(2,1)S(1)}, u32[]{:S(2)}, u32[]{:S(2)}) collective-permute-start(bf16[64,5120]{1,0:T(8,128)(2,1)S(1)} %shard_map.150.rest_0_), channel_id=1, source_target_pairs={{0,2},{1,3},{2,4},{3,5},{4,6},{5,7},{6,0},{7,1},{8,10},{9,11},{10,... | collective-permute-start | bytes 1966088 | tf_op jit(solution)/shard_map/ppermute | solution.py:639
  70.6 15.3 %collective-permute-start.22 = (bf16[64,5120]{1,0:T(8,128)(2,1)S(1)}, bf16[64,5120]{1,0:T(8,128)(2,1)S(1)}, u32[]{:S(2)}, u32[]{:S(2)}) collective-permute-start(bf16[64,5120]{1,0:T(8,128)(2,1)S(1)} %shard_map.151.rest_1_), channel_id=1, source_target_pairs={{0,6},{1,7},{2,0},{3,1},{4,2},{5,3},{6,4},{7,5},{8,14},{9,15},{10,... | collective-permute-start | bytes 1966088 | tf_op jit(solution)/shard_map/ppermute | solution.py:639
  75.9 10.1 %copy-start.7 = (bf16[1,1,64,5120]{3,2,1,0:T(8,128)(2,1)S(1)}, bf16[1,1,64,5120]{3,2,1,0:T(8,128)(2,1)}, u32[]{:S(2)}) copy-start(bf16[1,1,64,5120]{3,2,1,0:T(8,128)(2,1)} %param.12) | copy-start | bytes 1966084
  75.9 7.1 %collective-permute-start.25 = (bf16[16,5120]{1,0:T(8,128)(2,1)S(1)}, bf16[16,5120]{1,0:T(8,128)(2,1)S(1)}, u32[]{:S(2)}, u32[]{:S(2)}) collective-permute-start(bf16[16,5120]{1,0:T(8,128)(2,1)S(1)} %get-tuple-element.78), channel_id=1, source_target_pairs={{0,1},{1,0},{2,3},{3,2},{4,5},{5,4},{6,7},{7,6},{8,9},{9,8},{10,11... | collective-permute-start | bytes 491528 | tf_op jit(solution)/shard_map/ppermute | solution.py:642
  83.1 7.9 %collective-permute-start.26 = (bf16[16,5120]{1,0:T(8,128)(2,1)S(1)}, bf16[16,5120]{1,0:T(8,128)(2,1)S(1)}, u32[]{:S(2)}, u32[]{:S(2)}) collective-permute-start(bf16[16,5120]{1,0:T(8,128)(2,1)S(1)} %shard_map.156.own), channel_id=1, source_target_pairs={{0,4},{1,5},{2,6},{3,7},{4,0},{5,1},{6,2},{7,3},{8,12},{9,13},{10,... | collective-permute-start | bytes 491528 | tf_op jit(solution)/shard_map/ppermute | solution.py:639
  83.2 11.1 %collective-permute-start.27 = (bf16[16,5120]{1,0:T(8,128)(2,1)S(1)}, bf16[16,5120]{1,0:T(8,128)(2,1)S(1)}, u32[]{:S(2)}, u32[]{:S(2)}) collective-permute-start(bf16[16,5120]{1,0:T(8,128)(2,1)S(1)} %shard_map.156.own), channel_id=1, source_target_pairs={{0,2},{1,3},{2,4},{3,5},{4,6},{5,7},{6,0},{7,1},{8,10},{9,11},{10,... | collective-permute-start | bytes 491528 | tf_op jit(solution)/shard_map/ppermute | solution.py:639
  84.0 10.3 %collective-permute-start.28 = (bf16[16,5120]{1,0:T(8,128)(2,1)S(1)}, bf16[16,5120]{1,0:T(8,128)(2,1)S(1)}, u32[]{:S(2)}, u32[]{:S(2)}) collective-permute-start(bf16[16,5120]{1,0:T(8,128)(2,1)S(1)} %shard_map.156.own), channel_id=1, source_target_pairs={{0,6},{1,7},{2,0},{3,1},{4,2},{5,3},{6,4},{7,5},{8,14},{9,15},{10,... | collective-permute-start | bytes 491528 | tf_op jit(solution)/shard_map/ppermute | solution.py:639
  94.3 3.4 %collective-permute-start.29 = (f32[16,5120]{1,0:T(8,128)S(1)}, f32[16,5120]{1,0:T(8,128)S(1)}, u32[]{:S(2)}, u32[]{:S(2)}) collective-permute-start(f32[16,5120]{1,0:T(8,128)S(1)} %shard_map.157.kept), channel_id=1, source_target_pairs={{0,1},{1,0},{2,3},{3,2},{4,5},{5,4},{6,7},{7,6},{8,9},{9,8},{10,11... | collective-permute-start | bytes 983048 | tf_op jit(solution)/shard_map/ppermute | solution.py:642
  (12 other events, 33.9 us)
